TPU v7x, 256 devices: a whole 4x4x8 slice. The times are simulated.
256 devices in a mesh: row: 32 (over x, y, core), col: 8 (over z).
Axes of the slice: x: 4, y: 4, z: 8, core: 2. Of those that a mesh axis runs over, the one named last changes fastest.
Arguments:
- inputs: bfloat16 [512, 12288], P('col', 'row'), may hold values from -6 to 6
- weight: bfloat16 [12288, 49152], P('row', 'col'), may hold values from -0.0546875 to 0.0546875
- grad_out: bfloat16 [512, 49152], P('row', 'col'), may hold values from -1.5 to 1.5
Outputs:
- projected: bfloat16 [512, 49152], P('row', 'col')
- grad_inputs: bfloat16 [512, 12288], P('col', 'row')
- grad_weight: bfloat16 [12288, 49152], P('row', 'col')
All inputs are finite; a program needn't handle non-finite values.
Results may differ from a plain program's by a relative error of at most 0.001.
Values may be sent and summed in bfloat16 or wider, within the bound.
No kernel may reach another device: no remote copies, remote signals or barrier semaphores. Data moves between devices by JAX's collectives and lax.ppermute only.
A program may use at most 128 MiB of HBM per device.

v0:
```python
import jax
import jax.numpy as jnp
from jax import lax
from jax.sharding import PartitionSpec as P


def body(inputs, weight, grad_out):
    gathered = lax.all_gather(inputs, "col", axis=0, tiled=True)
    projected = lax.psum_scatter(
        jnp.dot(gathered, weight, preferred_element_type=jnp.float32),
        "row",
        scatter_dimension=0,
        tiled=True,
    ).astype(jnp.bfloat16)
    cotangent = lax.all_gather(grad_out, "row", axis=0, tiled=True)
    input_terms = lax.dot_general(
        cotangent, weight, (((1,), (1,)), ((), ())), preferred_element_type=jnp.float32
    )
    weight_terms = lax.dot_general(
        gathered, cotangent, (((0,), (0,)), ((), ())), preferred_element_type=jnp.float32
    )
    grad_inputs = lax.psum_scatter(input_terms, "col", scatter_dimension=0, tiled=True).astype(
        jnp.bfloat16
    )
    return (projected, grad_inputs, weight_terms.astype(jnp.bfloat16))


def solution(mesh):
    placed = (P("col", "row"), P("row", "col"), P("row", "col"))
    return jax.shard_map(
        body,
        mesh=mesh,
        in_specs=placed,
        out_specs=(P("row", "col"), P("col", "row"), P("row", "col")),
        check_vma=False,
    )
```

profile of v0, /device:TPU:1, one launch (start us, length us, event | category | flops | bytes accessed | tf_op | source)
XLA Modules:
  0.0 237.0 jit_solution(1545565876936955098)
XLA Ops:
  7.2 0.0 all-gather.2.cloned.1.call-start
  7.2 0.7 all-gather.2.cloned.1.call-update
  7.9 0.0 copy-start
  7.9 0.0 reduce-scatter.5.cloned.1.call-start
  8.0 61.0 %all-gather.2.cloned.1.call-done = bf16[512,6144]{1,0:T(8,128)(2,1)} async-done(((bf16[16,6144]{1,0:T(8,128)(2,1)}), bf16[512,6144]{1,0:T(8,128)(2,1)}) %all-gather.2.cloned.1.call-update) | async-done | bytes 6291472 | tf_op jit(solution)/shard_map/all_gather | solution.py:15
  68.9 8.5 %fusion.1 = f32[512,384]{1,0:T(8,128)} fusion(bf16[512,6144]{1,0:T(8,128)(2,1)} %all-gather.2.cloned.1.call-done, bf16[384,6144]{1,0:T(8,128)(2,1)} %param.4), kind=kOutput, calls=%fused_computation.2 | convolution fusion | flops 2415919104 | bytes 11796480 | tf_op jit(solution)/shard_map/dot_general | solution.py:16
  77.4 0.0 reduce-scatter.5.cloned.1.call-update
  77.4 0.0 reduce-scatter.3.cloned.1.call-start
  77.5 0.0 copy-done
  77.5 21.5 %all_gather.6 = bf16[512,384]{1,0:T(8,128)(2,1)S(1)} all-gather(bf16[64,384]{1,0:T(8,128)(2,1)S(1)} %copy-done), channel_id=1, replica_groups=mesh['row'=32,'col'=8] {'col'}, dimensions={0}, use_global_device_ids=true | all-gather | bytes 442368 | tf_op jit(solution)/shard_map/all_gather | solution.py:8
  99.0 8.7 %fusion = f32[512,6144]{1,0:T(8,128)} fusion(bf16[512,384]{1,0:T(8,128)(2,1)S(1)} %all_gather.6, bf16[384,6144]{1,0:T(8,128)(2,1)} %param.4), kind=kOutput, calls=%fused_computation.1 | convolution fusion | flops 2415919104 | bytes 17694720 | tf_op jit(solution)/shard_map/dot_general | solution.py:10
  107.7 0.0 reduce-scatter.3.cloned.1.call-update
  107.8 7.6 %convolution_convert_fusion = bf16[384,6144]{1,0:T(8,128)(2,1)} fusion(bf16[512,384]{1,0:T(8,128)(2,1)S(1)} %all_gather.6, bf16[512,6144]{1,0:T(8,128)(2,1)} %all-gather.2.cloned.1.call-done), kind=kOutput, calls=%fused_computation | convolution fusion | flops 2418278400 | bytes 11403264 | tf_op jit(solution)/shard_map/dot_general | solution.py:19
  115.4 0.0 reduce-scatter.5.cloned.1.call-done
  115.4 1.5 convert_element_type.10
  116.9 111.9 %reduce-scatter.3.cloned.1.call-done = f32[16,6144]{1,0:T(8,128)} async-done(((f32[512,6144]{1,0:T(8,128)}), f32[16,6144]{1,0:T(8,128)}) %reduce-scatter.3.cloned.1.call-update) | async-done | bytes 393232 | tf_op jit(solution)/shard_map/reduce_scatter | solution.py:9
  228.8 1.7 convert_element_type.9
Async XLA Ops:
  7.2 61.8 %all-gather.2.cloned.1.call-start = ((), (), s32[]{:S(2)}) async-start(), calls=%async_computation.3 | async-start | bytes 6488064 | tf_op jit(solution)/shard_map/all_gather | solution.py:15
  7.9 69.6 %copy-start = (bf16[64,384]{1,0:T(8,128)(2,1)S(1)}, bf16[64,384]{1,0:T(8,128)(2,1)}, u32[]{:S(2)}) copy-start(bf16[64,384]{1,0:T(8,128)(2,1)} %param.3) | copy-start | bytes 147460
  7.9 107.5 %reduce-scatter.5.cloned.1.call-start = ((), (), s32[]{:S(2)}) async-start(), calls=%async_computation.4 | async-start | bytes 884736 | tf_op jit(solution)/shard_map/reduce_scatter | solution.py:22
  77.4 151.4 %reduce-scatter.3.cloned.1.call-start = ((), (), s32[]{:S(2)}) async-start(), calls=%async_computation.2 | async-start | bytes 12976128 | tf_op jit(solution)/shard_map/reduce_scatter | solution.py:9
Sparse Core Ops, SparseCore 0:
  10.5 58.3 all-gather.1
  77.6 32.3 reduce-scatter.4
  114.6 114.1 reduce-scatter.2
where the time goes:
time: 237 us
  waiting for transfers between devices  174 us (73%)
  matrix products  24.9 us (11%)
  blocking collectives  21.5 us (9%)
  between operations  13.8 us (6%)
  other arithmetic  3.21 us (1%)
    reduce_scatter x1, waiting for transfers between devices, body(): lax.psum_scatter(jnp.dot(gathered, weight, preferred_element_type=jnp.flo...  112 us
    all_gather x1, waiting for transfers between devices, body(): cotangent = lax.all_gather(grad_out, 'row', axis=0, tiled=True)  61 us
    all_gather x1, blocking collectives, body(): gathered = lax.all_gather(inputs, 'col', axis=0, tiled=True)  21.5 us
    dot_general x1, matrix products, body(): jnp.dot(gathered, weight, preferred_element_type=jnp.float32)  8.73 us
    dot_general x1, matrix products, body(): lax.dot_general(cotangent, weight, (((1,), (1,)), ((), ())), preferred_el...  8.48 us
    dot_general x1, matrix products, body(): lax.dot_general(gathered, cotangent, (((0,), (0,)), ((), ())), preferred_...  7.64 us
  transfers between devices with their start and end apart: 3, of which 2 were waited for; matrix products, arithmetic and copies ran while one was open for 8% of the time, Pallas kernels for 0%

commit v1 on v0

v1 whole, which is shorter than its diff:
```python
import functools

import jax
import jax.numpy as jnp
from jax import lax
from jax.experimental import pallas as pl
from jax.experimental.pallas import tpu as pltpu
from jax.sharding import Mesh, PartitionSpec as P

BF = jnp.bfloat16
F32 = jnp.float32
SPAN = 86.5
LANES = 128
STEPS = (1, 3, 2)


def get(value, axis, distance):
    return lax.ppermute(value, axis, [((i + distance) % 4, i) for i in range(4)])


def swap(value):
    return lax.ppermute(value, "core", [(0, 1), (1, 0)])


def encode(block):
    size = jnp.abs(block)
    top = jnp.maximum(jnp.max(size, axis=0, keepdims=True), 1e-30)
    top = (top * (1.0 + 2.0**-7)).astype(BF).astype(F32)
    level = jnp.exp(size * (2 * SPAN / top) - SPAN)
    return jnp.where(block < 0, -level, level).astype(BF), top


def decode(code, top):
    code = code.astype(F32)
    size = (jnp.log(jnp.abs(code)) + SPAN) * (top / (2 * SPAN))
    return jnp.where(code < 0, -size, size)


def block_of(pos, dx, dy, core):
    return (((pos[0] + dx) % 4) * 4 + (pos[1] + dy) % 4) * 2 + core


def rows_of(index):
    return pl.ds(pl.multiple_of(index * 16, 16), 16)


def project_kernel(half, pos, own_in, par_in, w_own, w_par, keep, out1, out2, out3, lo, lp, tops):
    j = pl.program_id(0)

    @pl.when(j == 0)
    def _():
        tops[...] = jnp.zeros_like(tops)
        for first in range(4):
            for second in range(4):
                dx, dy = (first, second) if half == 0 else (second, first)
                for core in range(2):
                    to = ((first * 4 + second) * 2 + core) * 16
                    rows = rows_of(block_of(pos, dx, dy, core))
                    lo[to : to + 16, :] = own_in[rows, :]
                    lp[to : to + 16, :] = par_in[rows, :]

    total = jnp.dot(lo[...], w_own[...], preferred_element_type=F32)
    total += jnp.dot(lp[...], w_par[...], preferred_element_type=F32)
    tiles = total.shape[1] // LANES
    for k in range(tiles):
        lanes = slice(k * LANES, (k + 1) * LANES)
        tile = j * tiles + k
        rows = pl.ds(pl.multiple_of(tile * 128, 128), 128)
        keep[rows, :] = total[:128, lanes]
        for p, out in enumerate((out1, out2, out3)):
            d = STEPS[p]
            code, top = encode(total[d * 128 : (d + 1) * 128, lanes])
            out[rows, :] = code
            tops[p, pl.ds(tile, 1), :] = top

    @pl.when(j == pl.num_programs(0) - 1)
    def _():
        for p, out in enumerate((out1, out2, out3)):
            out[1536:1552, :] = tops[p].astype(BF)


def project(half, pos, own_in, par_in, weight, weight_par):
    width = 512
    piece = jax.ShapeDtypeStruct((1552, LANES), BF)
    whole = lambda j, pos: (0, 0)
    return pl.pallas_call(
        functools.partial(project_kernel, half),
        grid_spec=pltpu.PrefetchScalarGridSpec(
            num_scalar_prefetch=1,
            grid=(3,),
            in_specs=[
                pl.BlockSpec((512, 384), whole),
                pl.BlockSpec((512, 384), whole),
                pl.BlockSpec((384, width), lambda j, pos: (0, pos[2] * 6 + half * 3 + j)),
                pl.BlockSpec((384, width), lambda j, pos: (0, half * 3 + j)),
            ],
            out_specs=[pl.BlockSpec((1536, LANES), whole)] + [pl.BlockSpec((1552, LANES), whole)] * 3,
            scratch_shapes=[
                pltpu.VMEM((512, 384), BF),
                pltpu.VMEM((512, 384), BF),
                pltpu.VMEM((3, 16, LANES), F32),
            ],
        ),
        out_shape=[jax.ShapeDtypeStruct((1536, LANES), F32), piece, piece, piece],
        compiler_params=pltpu.CompilerParams(vmem_limit_bytes=24 * 2**20),
        cost_estimate=pl.CostEstimate(flops=2 * 512 * 768 * 1536, bytes_accessed=5 * 2**20, transcendentals=2**19),
        name="project",
    )(pos, own_in, par_in, weight, weight_par)


def relay_kernel(own, in1, in2, in3, keep, out1, out2, out3, tops):
    tops[...] = jnp.zeros_like(tops)
    heads = [ref[1536:1552, :].astype(F32) for ref in (in1, in2, in3)]
    for j in range(12):
        rows = slice(j * 128, (j + 1) * 128)
        total = own[rows, :]
        for ref, head in zip((in1, in2, in3), heads):
            total += decode(ref[rows, :], head[j : j + 1, :])
        to = slice(j * 32, (j + 1) * 32)
        keep[to, :] = total[:32, :]
        for p, out in enumerate((out1, out2, out3)):
            d = STEPS[p]
            code, top = encode(total[d * 32 : (d + 1) * 32, :])
            out[to, :] = code
            tops[p, j : j + 1, :] = top
    for p, out in enumerate((out1, out2, out3)):
        out[384:400, :] = tops[p].astype(BF)


def relay(own, pieces):
    piece = jax.ShapeDtypeStruct((400, LANES), BF)
    return pl.pallas_call(
        relay_kernel,
        out_shape=[jax.ShapeDtypeStruct((384, LANES), F32), piece, piece, piece],
        scratch_shapes=[pltpu.VMEM((3, 16, LANES), F32)],
        compiler_params=pltpu.CompilerParams(vmem_limit_bytes=16 * 2**20),
        cost_estimate=pl.CostEstimate(flops=2**22, bytes_accessed=3 * 2**20, transcendentals=2**20),
        name="relay",
    )(own, *pieces)


def finish_kernel(pos, *refs):
    keep, send = refs[-2:]
    core = pos[2]
    for half in range(2):
        own, *ins = refs[half * 4 : half * 4 + 4]
        heads = [ref[384:400, :].astype(F32) for ref in ins]
        for j in range(12):
            rows = slice(j * 32, (j + 1) * 32)
            total = own[rows, :]
            for ref, head in zip(ins, heads):
                total += decode(ref[rows, :], head[j : j + 1, :])
            lanes = slice(half * 1536 + j * LANES, half * 1536 + (j + 1) * LANES)
            low, high = total[:16, :].astype(BF), total[16:, :].astype(BF)
            keep[:, lanes] = jnp.where(core == 0, low, high)
            send[:, lanes] = jnp.where(core == 0, high, low)


def finish(pos, *arrays):
    return pl.pallas_call(
        finish_kernel,
        in_specs=[pl.BlockSpec(memory_space=pltpu.SMEM)] + [pl.BlockSpec(memory_space=pltpu.VMEM)] * 8,
        out_shape=[jax.ShapeDtypeStruct((16, 3072), BF)] * 2,
        compiler_params=pltpu.CompilerParams(vmem_limit_bytes=16 * 2**20),
        cost_estimate=pl.CostEstimate(flops=2**20, bytes_accessed=2**20, transcendentals=2**18),
        name="finish",
    )(pos, *arrays)


CONTRACT_LAST = (((1,), (1,)), ((), ()))


def grad_inputs_kernel(pos, a_own, a_par, b_own, b_par, w_a, w_b, out, acc_a, acc_b):
    j = pl.program_id(0)
    terms = [
        lax.dot_general(cot[...], w[...], CONTRACT_LAST, preferred_element_type=F32)
        for cot, w in ((a_own, w_a), (a_par, w_a), (b_own, w_b), (b_par, w_b))
    ]

    @pl.when(j == 0)
    def _():
        acc_a[:256, :], acc_a[256:, :], acc_b[:256, :], acc_b[256:, :] = terms

    @pl.when(j > 0)
    def _():
        acc_a[:256, :] = acc_a[:256, :] + terms[0]
        acc_a[256:, :] = acc_a[256:, :] + terms[1]
        acc_b[:256, :] = acc_b[:256, :] + terms[2]
        acc_b[256:, :] = acc_b[256:, :] + terms[3]

    @pl.when(j == pl.num_programs(0) - 1)
    def _():
        for rel in range(2):
            core = pos[2] if rel == 0 else 1 - pos[2]
            for dx in range(4):
                for dy in range(4):
                    a = ((rel * 4 + dy) * 4 + dx) * 16
                    b = ((rel * 4 + dx) * 4 + dy) * 16
                    out[rows_of(block_of(pos, dx, dy, core)), :] = acc_a[a : a + 16, :] + acc_b[b : b + 16, :]


def grad_inputs_terms(pos, a_own, a_par, b_own, b_par, weight):
    width = 512
    part = lambda j, pos: (0, j)
    return pl.pallas_call(
        grad_inputs_kernel,
        grid_spec=pltpu.PrefetchScalarGridSpec(
            num_scalar_prefetch=1,
            grid=(6,),
            in_specs=[pl.BlockSpec((256, width), part)] * 4
            + [pl.BlockSpec((384, width), part), pl.BlockSpec((384, width), lambda j, pos: (0, j + 6))],
            out_specs=pl.BlockSpec((512, 384), lambda j, pos: (0, 0)),
            scratch_shapes=[pltpu.VMEM((512, 384), F32), pltpu.VMEM((512, 384), F32)],
        ),
        out_shape=jax.ShapeDtypeStruct((512, 384), F32),
        compiler_params=pltpu.CompilerParams(vmem_limit_bytes=24 * 2**20),
        cost_estimate=pl.CostEstimate(flops=2 * 512 * 384 * 6144, bytes_accessed=12 * 2**20, transcendentals=0),
        name="grad_inputs",
    )(pos, a_own, a_par, b_own, b_par, weight, weight)


def grad_weight_kernel(pos, acts, a_own, a_par, b_own, b_par, out, lhs, turned):
    j = pl.program_id(0)
    half_steps = pl.num_programs(0) // 2

    def turn(half):
        for rel in range(2):
            core = pos[2] if rel == 0 else 1 - pos[2]
            for first in range(4):
                for second in range(4):
                    dx, dy = (second, first) if half == 0 else (first, second)
                    to = ((rel * 4 + first) * 4 + second) * 16
                    lhs[to : to + 16, :] = acts[rows_of(block_of(pos, dx, dy, core)), :]
        turned[...] = lhs[...].T

    def multiply(own, par):
        total = jnp.dot(turned[:, :256], own[...], preferred_element_type=F32)
        total += jnp.dot(turned[:, 256:], par[...], preferred_element_type=F32)
        out[...] = total.astype(BF)

    @pl.when(j == 0)
    def _():
        turn(0)

    @pl.when(j == half_steps)
    def _():
        turn(1)

    @pl.when(j < half_steps)
    def _():
        multiply(a_own, a_par)

    @pl.when(j >= half_steps)
    def _():
        multiply(b_own, b_par)


def grad_weight_of(pos, acts, a_own, a_par, b_own, b_par):
    width = 512
    early = pl.BlockSpec((256, width), lambda j, pos: (0, jnp.minimum(j, 5)))
    late = pl.BlockSpec((256, width), lambda j, pos: (0, jnp.maximum(j - 6, 0)))
    return pl.pallas_call(
        grad_weight_kernel,
        grid_spec=pltpu.PrefetchScalarGridSpec(
            num_scalar_prefetch=1,
            grid=(12,),
            in_specs=[pl.BlockSpec((512, 384), lambda j, pos: (0, 0)), early, early, late, late],
            out_specs=pl.BlockSpec((384, width), lambda j, pos: (0, j)),
            scratch_shapes=[pltpu.VMEM((512, 384), BF), pltpu.VMEM((384, 512), BF)],
        ),
        out_shape=jax.ShapeDtypeStruct((384, 6144), BF),
        compiler_params=pltpu.CompilerParams(vmem_limit_bytes=24 * 2**20),
        cost_estimate=pl.CostEstimate(flops=2 * 512 * 384 * 6144, bytes_accessed=12 * 2**20, transcendentals=0),
        name="grad_weight",
    )(pos, acts, a_own, a_par, b_own, b_par)


def body(inputs, weight, grad_out):
    core = lax.axis_index("core")
    pos = jnp.stack([lax.axis_index("x"), lax.axis_index("y"), core]).astype(jnp.int32)

    start_a, start_b = grad_out[:, :3072], grad_out[:, 3072:]
    a, b = {0: start_a}, {0: start_b}
    for d in STEPS:
        a[d] = get(start_a, "x", d)
        b[d] = get(start_b, "y", d)

    gathered = lax.all_to_all(jnp.broadcast_to(inputs[None], (8, 64, 384)), "z", 0, 0).reshape(512, 384)
    weight_par = swap(lax.dynamic_slice(weight, (0, (1 - core) * 3072), (384, 3072)))
    gathered_par = swap(gathered)

    row_a = jnp.concatenate([a[d] for d in range(4)])
    row_b = jnp.concatenate([b[d] for d in range(4)])
    a, b = {0: row_a}, {0: row_b}
    for d in STEPS:
        a[d] = get(row_a, "y", d)
        b[d] = get(row_b, "x", d)

    own_a, *send_a = project(0, pos, gathered, gathered_par, weight, weight_par)
    own_b, *send_b = project(1, pos, gathered, gathered_par, weight, weight_par)

    a_own = jnp.concatenate([a[d] for d in range(4)])
    b_own = jnp.concatenate([b[d] for d in range(4)])
    a_par, b_par = swap(a_own), swap(b_own)

    got_a = [get(v, "x", 4 - d) for v, d in zip(send_a, STEPS)]
    got_b = [get(v, "y", 4 - d) for v, d in zip(send_b, STEPS)]

    terms = grad_inputs_terms(pos, a_own, a_par, b_own, b_par, weight)
    grad_inputs = lax.all_to_all(terms.reshape(8, 64, 384), "z", 0, 0).sum(axis=0).astype(BF)
    grad_weight = grad_weight_of(pos, gathered, a_own, a_par, b_own, b_par)

    own_a, *send_a = relay(own_a, got_a)
    own_b, *send_b = relay(own_b, got_b)
    got_a = [get(v, "y", 4 - d) for v, d in zip(send_a, STEPS)]
    got_b = [get(v, "x", 4 - d) for v, d in zip(send_b, STEPS)]
    mine, theirs = finish(pos, own_a, *got_a, own_b, *got_b)
    other = swap(theirs)
    projected = jnp.where(
        core == 0, jnp.concatenate([mine, other], axis=1), jnp.concatenate([other, mine], axis=1)
    )
    return projected, grad_inputs, grad_weight


def solution(mesh):
    fine = Mesh(mesh.devices.reshape(4, 4, 2, 8), ("x", "y", "core", "z"))
    rows = ("x", "y", "core")
    placed = (P("z", rows), P(rows, "z"), P(rows, "z"))
    return jax.shard_map(
        body,
        mesh=fine,
        in_specs=placed,
        out_specs=(P(rows, "z"), P("z", rows), P(rows, "z")),
        check_vma=False,
    )
```

time: 237 us -> 154 us (0.65)
  waiting for transfers between devices: 174 us -> 18.4 us
  starting transfers between devices: 0.12 us -> 76.3 us
  Pallas kernels: 0 us -> 35.5 us
  matrix products: 24.9 us -> 0 us
  blocking collectives: 21.5 us -> 0 us
  local copies, waits for them, and re-layouts: 0.01 us -> 20 us
  between operations: 13.8 us -> 0.75 us
    reduce_scatter x2 -> x0, waiting for transfers between devices: 112 us -> none  [the longest x1 112 us: body(): lax.psum_scatter(jnp.dot(gathered, weight, preferred_element_type=jnp.flo...]
    ppermute x0 -> x29, starting transfers between devices: none -> 61 us  [the longest x24 46.8 us: get(): lax.ppermute(value, axis, [((i + distance) % 4, i) for i in range(4)])]
    all_gather x1 -> x0, waiting for transfers between devices: 61 us -> none  [body(): cotangent = lax.all_gather(grad_out, 'row', axis=0, tiled=True)]
    pallas_call x0 -> x7, Pallas kernels: none -> 35.5 us  [the longest x1 11.6 us: grad_weight_of(): pl.pallas_call(grad_weight_kernel, grid_spec=pltpu.PrefetchScalarGridSpec...]
    dot_general x3 -> x0, matrix products: 24.9 us -> none  [the longest x1 8.73 us: body(): jnp.dot(gathered, weight, preferred_element_type=jnp.float32)]
    all_gather x1 -> x0, blocking collectives: 21.5 us -> none  [body(): gathered = lax.all_gather(inputs, 'col', axis=0, tiled=True)]
    ppermute x0 -> x29, waiting for transfers between devices: none -> 18.4 us  [the longest x24 15 us: get(): lax.ppermute(value, axis, [((i + distance) % 4, i) for i in range(4)])]
    all_to_all x0 -> x2, starting transfers between devices: none -> 15.3 us  [the longest x1 8.19 us: body(): lax.all_to_all(jnp.broadcast_to(inputs[None], (8, 64, 384)), 'z', 0, 0)]
  transfers between devices with their start and end apart: 3 -> 31, of which waited for: 2 -> 8; matrix products, arithmetic and copies ran while one was open for 8% -> 9% of each run, Pallas kernels for 0% -> 23%
where the time goes in v1:
time: 154 us
  starting transfers between devices  76.3 us (50%)
  Pallas kernels  35.5 us (23%)
  local copies, waits for them, and re-layouts  20 us (13%)
  waiting for transfers between devices  18.4 us (12%)
  other arithmetic  2.66 us (2%)
    ppermute x24, starting transfers between devices, get(): lax.ppermute(value, axis, [((i + distance) % 4, i) for i in range(4)])  46.8 us
    ppermute x24, waiting for transfers between devices, get(): lax.ppermute(value, axis, [((i + distance) % 4, i) for i in range(4)])  15 us
    ppermute x5, starting transfers between devices, swap(): return lax.ppermute(value, 'core', [(0, 1), (1, 0)])  14.3 us
    unnamed x24, local copies, waits for them, and re-layouts  11.9 us
    pallas_call x1, Pallas kernels, grad_weight_of(): pl.pallas_call(grad_weight_kernel, grid_spec=pltpu.PrefetchScalarGridSpec...  11.6 us
    pallas_call x2, Pallas kernels, project(): pl.pallas_call(functools.partial(project_kernel, half), grid_spec=pltpu.P...  9.4 us
    pallas_call x1, Pallas kernels, grad_inputs_terms(): pl.pallas_call(grad_inputs_kernel, grid_spec=pltpu.PrefetchScalarGridSpec...  8.88 us
    all_to_all x1, starting transfers between devices, body(): lax.all_to_all(jnp.broadcast_to(inputs[None], (8, 64, 384)), 'z', 0, 0)  8.19 us
  transfers between devices with their start and end apart: 31, of which 8 were waited for; matrix products, arithmetic and copies ran while one was open for 9% of the time, Pallas kernels for 23%

profile of v1, /device:TPU:1, one launch (start us, length us, event | category | flops | bytes accessed | tf_op | source)
XLA Modules:
  0.0 153.6 jit_solution(7342492377307156540)
XLA Ops:
  0.6 1.7 %fusion = (bf16[16,3072]{1,0:T(8,128)(2,1)S(1)}, bf16[256,3072]{1,0:T(8,128)(2,1)}, bf16[256,3072]{1,0:T(8,128)(2,1)}, bf16[16,3072]{1,0:T(8,128)(2,1)S(1)}) fusion(bf16[16,6144]{1,0:T(8,128)(2,1)} %param.5), kind=kLoop, calls=%fused_computation.19 | loop fusion | bytes 589824 | tf_op jit(solution)/shard_map/slice | solution.py:282
  2.3 3.3 %collective-permute-start.15 = (bf16[16,3072]{1,0:T(8,128)(2,1)S(1)}, bf16[16,3072]{1,0:T(8,128)(2,1)S(1)}, u32[]{:S(2)}, u32[]{:S(2)}) collective-permute-start(bf16[16,3072]{1,0:T(8,128)(2,1)S(1)} %get-tuple-element.42), channel_id=1, source_target_pairs={{64,0},{128,64},{192,128},{0,192},{65,1},{129,65},{193,129},{1,193... | collective-permute-start | bytes 294920 | tf_op jit(solution)/shard_map/ppermute | solution.py:18
  6.7 2.7 %collective-permute-start.22 = (bf16[16,3072]{1,0:T(8,128)(2,1)S(1)}, bf16[16,3072]{1,0:T(8,128)(2,1)S(1)}, u32[]{:S(2)}, u32[]{:S(2)}) collective-permute-start(bf16[16,3072]{1,0:T(8,128)(2,1)S(1)} %get-tuple-element.39), channel_id=1, source_target_pairs={{16,0},{32,16},{48,32},{0,48},{17,1},{33,17},{49,33},{1,49},{18,2}... | collective-permute-start | bytes 294920 | tf_op jit(solution)/shard_map/ppermute | solution.py:18
  9.8 1.6 %broadcast_in_dim.2 = bf16[8,64,384]{2,1,0:T(8,128)(2,1)} broadcast(bf16[64,384]{1,0:T(8,128)(2,1)} %param.3), dimensions={1,2} | broadcast | bytes 442368 | tf_op jit(solution)/shard_map/broadcast_in_dim | solution.py:288
  11.4 8.2 %all-to-all-start = ((bf16[8,64,384]{2,1,0:T(8,128)(2,1)}), bf16[8,64,384]{2,1,0:T(8,128)(2,1)S(1)}, u32[]{:S(2)}, u32[]{:S(2)}) async-start(bf16[8,64,384]{2,1,0:T(8,128)(2,1)} %broadcast_in_dim.2), calls=%async_computation | async-start | bytes 786432 | tf_op jit(solution)/shard_map/all_to_all | solution.py:288
  19.6 3.2 %constant_dynamic-slice_fusion = bf16[384,3072]{1,0:T(8,128)(2,1)} fusion(bf16[384,6144]{1,0:T(8,128)(2,1)} %w_b.1, s32[]{:T(128)S(6)} %select_n.12), kind=kLoop, calls=%fused_computation.18 | loop fusion | bytes 4718596 | tf_op jit(solution)/shard_map/dynamic_slice | solution.py:289
  23.5 2.6 %collective-permute-start.1 = (bf16[384,3072]{1,0:T(8,128)(2,1)}, bf16[384,3072]{1,0:T(8,128)(2,1)S(1)}, u32[]{:S(2)}, u32[]{:S(2)}) collective-permute-start(bf16[384,3072]{1,0:T(8,128)(2,1)} %constant_dynamic-slice_fusion), channel_id=1, source_target_pairs={{0,8},{8,0},{1,9},{9,1},{2,10},{10,2},{3,11},{11,3},{4,12},{12,4},... | collective-permute-start | bytes 7077896 | tf_op jit(solution)/shard_map/ppermute | solution.py:22
  26.2 2.1 %collective-permute-start.18 = (bf16[64,3072]{1,0:T(8,128)(2,1)S(1)}, bf16[64,3072]{1,0:T(8,128)(2,1)S(1)}, u32[]{:S(2)}, u32[]{:S(2)}) collective-permute-start(bf16[64,3072]{1,0:T(8,128)(2,1)S(1)} %pad_maximum_fusion), channel_id=1, source_target_pairs={{16,0},{32,16},{48,32},{0,48},{17,1},{33,17},{49,33},{1,49},{18,2}... | collective-permute-start | bytes 1179656 | tf_op jit(solution)/shard_map/ppermute | solution.py:18
  29.7 2.1 %collective-permute-start.25 = (bf16[64,3072]{1,0:T(8,128)(2,1)S(1)}, bf16[64,3072]{1,0:T(8,128)(2,1)S(1)}, u32[]{:S(2)}, u32[]{:S(2)}) collective-permute-start(bf16[64,3072]{1,0:T(8,128)(2,1)S(1)} %pad_maximum_fusion.1), channel_id=1, source_target_pairs={{64,0},{128,64},{192,128},{0,192},{65,1},{129,65},{193,129},{1,193... | collective-permute-start | bytes 1179656 | tf_op jit(solution)/shard_map/ppermute | solution.py:18
  37.2 1.6 %collective-permute-start.26 = (bf16[64,3072]{1,0:T(8,128)(2,1)S(1)}, bf16[64,3072]{1,0:T(8,128)(2,1)S(1)}, u32[]{:S(2)}, u32[]{:S(2)}) collective-permute-start(bf16[64,3072]{1,0:T(8,128)(2,1)S(1)} %pad_maximum_fusion.1), channel_id=1, source_target_pairs={{128,0},{192,64},{0,128},{64,192},{129,1},{193,65},{1,129},{65,193... | collective-permute-start | bytes 1179656 | tf_op jit(solution)/shard_map/ppermute | solution.py:18
  42.5 6.7 %collective-permute-done.20 = bf16[64,3072]{1,0:T(8,128)(2,1)S(1)} collective-permute-done((bf16[64,3072]{1,0:T(8,128)(2,1)S(1)}, bf16[64,3072]{1,0:T(8,128)(2,1)S(1)}, u32[]{:S(2)}, u32[]{:S(2)}) %collective-permute-start.20) | collective-permute-done | bytes 393248 | tf_op jit(solution)/shard_map/ppermute | solution.py:18
  50.0 1.6 %collective-permute-start.21 = (bf16[256,3072]{1,0:T(8,128)(2,1)}, bf16[256,3072]{1,0:T(8,128)(2,1)}, u32[]{:S(2)}, u32[]{:S(2)}) collective-permute-start(bf16[256,3072]{1,0:T(8,128)(2,1)} %constant_dynamic-update-slice_fusion.a_own), channel_id=1, source_target_pairs={{0,8},{8,0},{1,9},{9,1},{2,10},{10,2},{3,11},{11,3},{4,12},{12,4},... | collective-permute-start | bytes 4718600 | tf_op jit(solution)/shard_map/ppermute | solution.py:22
  53.9 6.4 %collective-permute-start.28 = (bf16[256,3072]{1,0:T(8,128)(2,1)}, bf16[256,3072]{1,0:T(8,128)(2,1)}, u32[]{:S(2)}, u32[]{:S(2)}) collective-permute-start(bf16[256,3072]{1,0:T(8,128)(2,1)} %constant_dynamic-update-slice_fusion.7.b_own), channel_id=1, source_target_pairs={{0,8},{8,0},{1,9},{9,1},{2,10},{10,2},{3,11},{11,3},{4,12},{12,4},... | collective-permute-start | bytes 4718600 | tf_op jit(solution)/shard_map/ppermute | solution.py:22
  60.4 3.4 %collective-permute-done.par_in = bf16[512,384]{1,0:T(8,128)(2,1)S(1)} collective-permute-done((bf16[512,384]{1,0:T(8,128)(2,1)S(1)}, bf16[512,384]{1,0:T(8,128)(2,1)S(1)}, u32[]{:S(2)}, u32[]{:S(2)}) %collective-permute-start) | collective-permute-done | bytes 393248 | tf_op jit(solution)/shard_map/ppermute | solution.py:22
  63.8 2.3 %copy-done = bf16[384,6144]{1,0:T(8,128)(2,1)S(1)} copy-done((bf16[384,6144]{1,0:T(8,128)(2,1)S(1)}, bf16[384,6144]{1,0:T(8,128)(2,1)}, u32[]{:S(2)}) %copy-start) | copy-done | bytes 4718616
  66.1 4.7 %project.2 = (f32[1536,128]{1,0:T(8,128)S(1)}, bf16[1552,128]{1,0:T(8,128)(2,1)S(1)}, bf16[1552,128]{1,0:T(8,128)(2,1)}, bf16[1552,128]{1,0:T(8,128)(2,1)}) custom-call(s32[3]{0:T(128)S(1)} %pad_add_fusion.pos, bf16[512,384]{1,0:T(8,128)(2,1)S(1)} %bitcast.6, bf16[512,384]{1,0:T(8,128)(2,1)S(1)} %collective-permute-done.par_in, ...), custom_call_target="tpu_custom_call" | custom-call | flops 1207959552 | bytes 5242880 | tf_op jit(solution)/shard_map/project/pallas_call | solution.py:86
  71.8 2.6 %collective-permute-start.3 = (bf16[1552,128]{1,0:T(8,128)(2,1)}, bf16[1552,128]{1,0:T(8,128)(2,1)}, u32[]{:S(2)}, u32[]{:S(2)}) collective-permute-start(bf16[1552,128]{1,0:T(8,128)(2,1)} %get-tuple-element.23), channel_id=1, source_target_pairs={{64,0},{128,64},{192,128},{0,192},{65,1},{129,65},{193,129},{1,193... | collective-permute-start | bytes 1191944 | tf_op jit(solution)/shard_map/ppermute | solution.py:18
  74.7 4.7 %project.3 = (f32[1536,128]{1,0:T(8,128)S(1)}, bf16[1552,128]{1,0:T(8,128)(2,1)}, bf16[1552,128]{1,0:T(8,128)(2,1)}, bf16[1552,128]{1,0:T(8,128)(2,1)S(1)}) custom-call(s32[3]{0:T(128)S(1)} %pad_add_fusion.pos, bf16[512,384]{1,0:T(8,128)(2,1)S(1)} %bitcast.7, bf16[512,384]{1,0:T(8,128)(2,1)S(1)} %collective-permute-done.par_in, ...), custom_call_target="tpu_custom_call" | custom-call | flops 1207959552 | bytes 5242880 | tf_op jit(solution)/shard_map/project/pallas_call | solution.py:86
  80.4 3.7 %collective-permute-start.8 = (bf16[1552,128]{1,0:T(8,128)(2,1)}, bf16[1552,128]{1,0:T(8,128)(2,1)}, u32[]{:S(2)}, u32[]{:S(2)}) collective-permute-start(bf16[1552,128]{1,0:T(8,128)(2,1)} %get-tuple-element.30), channel_id=1, source_target_pairs={{48,0},{0,16},{16,32},{32,48},{49,1},{1,17},{17,33},{33,49},{50,2}... | collective-permute-start | bytes 1191944 | tf_op jit(solution)/shard_map/ppermute | solution.py:18
  84.1 7.0 %collective-permute-start.9 = (bf16[1552,128]{1,0:T(8,128)(2,1)}, bf16[1552,128]{1,0:T(8,128)(2,1)}, u32[]{:S(2)}, u32[]{:S(2)}) collective-permute-start(bf16[1552,128]{1,0:T(8,128)(2,1)} %get-tuple-element.31), channel_id=1, source_target_pairs={{16,0},{32,16},{48,32},{0,48},{17,1},{33,17},{49,33},{1,49},{18,2}... | collective-permute-start | bytes 1191944 | tf_op jit(solution)/shard_map/ppermute | solution.py:18
  94.3 8.9 %grad_inputs.1 = f32[512,384]{1,0:T(8,128)} custom-call(s32[3]{0:T(128)S(1)} %pad_add_fusion.pos, bf16[256,3072]{1,0:T(8,128)(2,1)} %constant_dynamic-update-slice_fusion.a_own, bf16[256,3072]{1,0:T(8,128)(2,1)} %collective-permute-done.21.a_par, bf16[256,3072]{1,0:T(8,128)(2,1)} %constant_dynamic-update-slice_fusion.7.b_own, ...), custom_call_target="tpu_custom_call" | custom-call | flops 2415919104 | bytes 12582912 | tf_op jit(solution)/shard_map/grad_inputs/pallas_call | solution.py:205
  103.2 7.1 %all-to-all-start.1 = ((f32[8,64,384]{2,1,0:T(8,128)}), f32[8,64,384]{2,1,0:T(8,128)}, u32[]{:S(2)}, u32[]{:S(2)}) async-start(f32[8,64,384]{2,1,0:T(8,128)} %bitcast.4), calls=%async_computation.1 | async-start | bytes 1572864 | tf_op jit(solution)/shard_map/all_to_all | solution.py:310
  110.3 2.3 %relay.2 = (f32[384,128]{1,0:T(8,128)S(1)}, bf16[400,128]{1,0:T(8,128)(2,1)S(1)}, bf16[400,128]{1,0:T(8,128)(2,1)S(1)}, bf16[400,128]{1,0:T(8,128)(2,1)S(1)}) custom-call(f32[1536,128]{1,0:T(8,128)S(1)} %copy-done.4, bf16[1552,128]{1,0:T(8,128)(2,1)S(1)} %copy-done.6, bf16[1552,128]{1,0:T(8,128)(2,1)} %collective-permute-done.3.in2, ...), custom_call_target="tpu_custom_call" | custom-call | flops 4194304 | bytes 3145728 | tf_op jit(solution)/shard_map/relay/pallas_call | solution.py:132
  112.6 9.9 %collective-permute-start.5 = (bf16[400,128]{1,0:T(8,128)(2,1)S(1)}, bf16[400,128]{1,0:T(8,128)(2,1)S(1)}, u32[]{:S(2)}, u32[]{:S(2)}) collective-permute-start(bf16[400,128]{1,0:T(8,128)(2,1)S(1)} %get-tuple-element.26), channel_id=1, source_target_pairs={{48,0},{0,16},{16,32},{32,48},{49,1},{1,17},{17,33},{33,49},{50,2}... | collective-permute-start | bytes 307208 | tf_op jit(solution)/shard_map/ppermute | solution.py:18
  122.5 1.9 %collective-permute-start.7 = (bf16[400,128]{1,0:T(8,128)(2,1)S(1)}, bf16[400,128]{1,0:T(8,128)(2,1)S(1)}, u32[]{:S(2)}, u32[]{:S(2)}) collective-permute-start(bf16[400,128]{1,0:T(8,128)(2,1)S(1)} %get-tuple-element.28), channel_id=1, source_target_pairs={{32,0},{48,16},{0,32},{16,48},{33,1},{49,17},{1,33},{17,49},{34,2}... | collective-permute-start | bytes 307208 | tf_op jit(solution)/shard_map/ppermute | solution.py:18
  124.4 2.4 %relay.3 = (f32[384,128]{1,0:T(8,128)S(1)}, bf16[400,128]{1,0:T(8,128)(2,1)S(1)}, bf16[400,128]{1,0:T(8,128)(2,1)S(1)}, bf16[400,128]{1,0:T(8,128)(2,1)S(1)}) custom-call(f32[1536,128]{1,0:T(8,128)S(1)} %copy-done.2, bf16[1552,128]{1,0:T(8,128)(2,1)} %collective-permute-done.8.in1, bf16[1552,128]{1,0:T(8,128)(2,1)} %collective-permute-done.9.in2, ...), custom_call_target="tpu_custom_call" | custom-call | flops 4194304 | bytes 3145728 | tf_op jit(solution)/shard_map/relay/pallas_call | solution.py:132
  127.1 2.7 %collective-permute-start.12 = (bf16[400,128]{1,0:T(8,128)(2,1)S(1)}, bf16[400,128]{1,0:T(8,128)(2,1)S(1)}, u32[]{:S(2)}, u32[]{:S(2)}) collective-permute-start(bf16[400,128]{1,0:T(8,128)(2,1)S(1)} %get-tuple-element.35), channel_id=1, source_target_pairs={{64,0},{128,64},{192,128},{0,192},{65,1},{129,65},{193,129},{1,193... | collective-permute-start | bytes 307208 | tf_op jit(solution)/shard_map/ppermute | solution.py:18
  129.8 2.4 %collective-permute-done.11.refs_5_ = bf16[400,128]{1,0:T(8,128)(2,1)S(1)} collective-permute-done((bf16[400,128]{1,0:T(8,128)(2,1)S(1)}, bf16[400,128]{1,0:T(8,128)(2,1)S(1)}, u32[]{:S(2)}, u32[]{:S(2)}) %collective-permute-start.11) | collective-permute-done | bytes 102432 | tf_op jit(solution)/shard_map/ppermute | solution.py:18
  132.4 2.4 %collective-permute-done.13.refs_7_ = bf16[400,128]{1,0:T(8,128)(2,1)S(1)} collective-permute-done((bf16[400,128]{1,0:T(8,128)(2,1)S(1)}, bf16[400,128]{1,0:T(8,128)(2,1)S(1)}, u32[]{:S(2)}, u32[]{:S(2)}) %collective-permute-start.13) | collective-permute-done | bytes 102432 | tf_op jit(solution)/shard_map/ppermute | solution.py:18
  135.8 3.7 %collective-permute-start.14 = (bf16[16,3072]{1,0:T(8,128)(2,1)S(1)}, bf16[16,3072]{1,0:T(8,128)(2,1)S(1)}, u32[]{:S(2)}, u32[]{:S(2)}) collective-permute-start(bf16[16,3072]{1,0:T(8,128)(2,1)S(1)} %get-tuple-element.38), channel_id=1, source_target_pairs={{0,8},{8,0},{1,9},{9,1},{2,10},{10,2},{3,11},{11,3},{4,12},{12,4},... | collective-permute-start | bytes 294920 | tf_op jit(solution)/shard_map/ppermute | solution.py:22
  139.5 11.6 %grad_weight.1 = bf16[384,6144]{1,0:T(8,128)(2,1)} custom-call(s32[3]{0:T(128)S(1)} %pad_add_fusion.pos, bf16[512,384]{1,0:T(8,128)(2,1)S(1)} %bitcast.8, bf16[256,3072]{1,0:T(8,128)(2,1)} %constant_dynamic-update-slice_fusion.a_own, bf16[256,3072]{1,0:T(8,128)(2,1)} %collective-permute-done.21.a_par, ...), custom_call_target="tpu_custom_call" | custom-call | flops 2415919104 | bytes 12582912 | tf_op jit(solution)/shard_map/grad_weight/pallas_call | solution.py:262
  151.8 1.8 %reduce_sum.9 = bf16[64,384]{1,0:T(8,128)(2,1)} reduce(f32[8,64,384]{2,1,0:T(8,128)} %all-to-all-done.1, f32[]{:T(128)} %constant.24.clone.1), dimensions={0}, to_apply=%region_0.0 | reduce | flops 172032 | bytes 835588 | tf_op jit(solution)/shard_map/reduce_sum | solution.py:310
  (71 shorter events, 23.8 us)
Async XLA Ops:
  2.3 20.5 %collective-permute-start.15 = (bf16[16,3072]{1,0:T(8,128)(2,1)S(1)}, bf16[16,3072]{1,0:T(8,128)(2,1)S(1)}, u32[]{:S(2)}, u32[]{:S(2)}) collective-permute-start(bf16[16,3072]{1,0:T(8,128)(2,1)S(1)} %get-tuple-element.42), channel_id=1, source_target_pairs={{64,0},{128,64},{192,128},{0,192},{65,1},{129,65},{193,129},{1,193... | collective-permute-start | bytes 294920 | tf_op jit(solution)/shard_map/ppermute | solution.py:18
  5.6 17.9 %collective-permute-start.16 = (bf16[16,3072]{1,0:T(8,128)(2,1)S(1)}, bf16[16,3072]{1,0:T(8,128)(2,1)S(1)}, u32[]{:S(2)}, u32[]{:S(2)}) collective-permute-start(bf16[16,3072]{1,0:T(8,128)(2,1)S(1)} %get-tuple-element.42), channel_id=1, source_target_pairs={{128,0},{192,64},{0,128},{64,192},{129,1},{193,65},{1,129},{65,193... | collective-permute-start | bytes 294920 | tf_op jit(solution)/shard_map/ppermute | solution.py:18
  6.1 20.0 %collective-permute-start.17 = (bf16[16,3072]{1,0:T(8,128)(2,1)S(1)}, bf16[16,3072]{1,0:T(8,128)(2,1)S(1)}, u32[]{:S(2)}, u32[]{:S(2)}) collective-permute-start(bf16[16,3072]{1,0:T(8,128)(2,1)S(1)} %get-tuple-element.42), channel_id=1, source_target_pairs={{192,0},{0,64},{64,128},{128,192},{193,1},{1,65},{65,129},{129,193... | collective-permute-start | bytes 294920 | tf_op jit(solution)/shard_map/ppermute | solution.py:18
  6.7 21.5 %collective-permute-start.22 = (bf16[16,3072]{1,0:T(8,128)(2,1)S(1)}, bf16[16,3072]{1,0:T(8,128)(2,1)S(1)}, u32[]{:S(2)}, u32[]{:S(2)}) collective-permute-start(bf16[16,3072]{1,0:T(8,128)(2,1)S(1)} %get-tuple-element.39), channel_id=1, source_target_pairs={{16,0},{32,16},{48,32},{0,48},{17,1},{33,17},{49,33},{1,49},{18,2}... | collective-permute-start | bytes 294920 | tf_op jit(solution)/shard_map/ppermute | solution.py:18
  9.5 20.2 %collective-permute-start.23 = (bf16[16,3072]{1,0:T(8,128)(2,1)S(1)}, bf16[16,3072]{1,0:T(8,128)(2,1)S(1)}, u32[]{:S(2)}, u32[]{:S(2)}) collective-permute-start(bf16[16,3072]{1,0:T(8,128)(2,1)S(1)} %get-tuple-element.39), channel_id=1, source_target_pairs={{32,0},{48,16},{0,32},{16,48},{33,1},{49,17},{1,33},{17,49},{34,2}... | collective-permute-start | bytes 294920 | tf_op jit(solution)/shard_map/ppermute | solution.py:18
  11.4 48.9 %all-to-all-start = ((bf16[8,64,384]{2,1,0:T(8,128)(2,1)}), bf16[8,64,384]{2,1,0:T(8,128)(2,1)S(1)}, u32[]{:S(2)}, u32[]{:S(2)}) async-start(bf16[8,64,384]{2,1,0:T(8,128)(2,1)} %broadcast_in_dim.2), calls=%async_computation | async-start | bytes 786432 | tf_op jit(solution)/shard_map/all_to_all | solution.py:288
  22.8 6.9 %collective-permute-start.24 = (bf16[16,3072]{1,0:T(8,128)(2,1)S(1)}, bf16[16,3072]{1,0:T(8,128)(2,1)S(1)}, u32[]{:S(2)}, u32[]{:S(2)}) collective-permute-start(bf16[16,3072]{1,0:T(8,128)(2,1)S(1)} %get-tuple-element.39), channel_id=1, source_target_pairs={{48,0},{0,16},{16,32},{32,48},{49,1},{1,17},{17,33},{33,49},{50,2}... | collective-permute-start | bytes 294920 | tf_op jit(solution)/shard_map/ppermute | solution.py:18
  23.5 40.3 %collective-permute-start.1 = (bf16[384,3072]{1,0:T(8,128)(2,1)}, bf16[384,3072]{1,0:T(8,128)(2,1)S(1)}, u32[]{:S(2)}, u32[]{:S(2)}) collective-permute-start(bf16[384,3072]{1,0:T(8,128)(2,1)} %constant_dynamic-slice_fusion), channel_id=1, source_target_pairs={{0,8},{8,0},{1,9},{9,1},{2,10},{10,2},{3,11},{11,3},{4,12},{12,4},... | collective-permute-start | bytes 7077896 | tf_op jit(solution)/shard_map/ppermute | solution.py:22
  26.2 11.0 %collective-permute-start.18 = (bf16[64,3072]{1,0:T(8,128)(2,1)S(1)}, bf16[64,3072]{1,0:T(8,128)(2,1)S(1)}, u32[]{:S(2)}, u32[]{:S(2)}) collective-permute-start(bf16[64,3072]{1,0:T(8,128)(2,1)S(1)} %pad_maximum_fusion), channel_id=1, source_target_pairs={{16,0},{32,16},{48,32},{0,48},{17,1},{33,17},{49,33},{1,49},{18,2}... | collective-permute-start | bytes 1179656 | tf_op jit(solution)/shard_map/ppermute | solution.py:18
  28.3 12.0 %collective-permute-start.19 = (bf16[64,3072]{1,0:T(8,128)(2,1)S(1)}, bf16[64,3072]{1,0:T(8,128)(2,1)S(1)}, u32[]{:S(2)}, u32[]{:S(2)}) collective-permute-start(bf16[64,3072]{1,0:T(8,128)(2,1)S(1)} %pad_maximum_fusion), channel_id=1, source_target_pairs={{32,0},{48,16},{0,32},{16,48},{33,1},{49,17},{1,33},{17,49},{34,2}... | collective-permute-start | bytes 1179656 | tf_op jit(solution)/shard_map/ppermute | solution.py:18
  29.7 19.6 %collective-permute-start.20 = (bf16[64,3072]{1,0:T(8,128)(2,1)S(1)}, bf16[64,3072]{1,0:T(8,128)(2,1)S(1)}, u32[]{:S(2)}, u32[]{:S(2)}) collective-permute-start(bf16[64,3072]{1,0:T(8,128)(2,1)S(1)} %pad_maximum_fusion), channel_id=1, source_target_pairs={{48,0},{0,16},{16,32},{32,48},{49,1},{1,17},{17,33},{33,49},{50,2}... | collective-permute-start | bytes 1179656 | tf_op jit(solution)/shard_map/ppermute | solution.py:18
  29.7 21.9 %collective-permute-start.25 = (bf16[64,3072]{1,0:T(8,128)(2,1)S(1)}, bf16[64,3072]{1,0:T(8,128)(2,1)S(1)}, u32[]{:S(2)}, u32[]{:S(2)}) collective-permute-start(bf16[64,3072]{1,0:T(8,128)(2,1)S(1)} %pad_maximum_fusion.1), channel_id=1, source_target_pairs={{64,0},{128,64},{192,128},{0,192},{65,1},{129,65},{193,129},{1,193... | collective-permute-start | bytes 1179656 | tf_op jit(solution)/shard_map/ppermute | solution.py:18
  37.2 15.2 %collective-permute-start.26 = (bf16[64,3072]{1,0:T(8,128)(2,1)S(1)}, bf16[64,3072]{1,0:T(8,128)(2,1)S(1)}, u32[]{:S(2)}, u32[]{:S(2)}) collective-permute-start(bf16[64,3072]{1,0:T(8,128)(2,1)S(1)} %pad_maximum_fusion.1), channel_id=1, source_target_pairs={{128,0},{192,64},{0,128},{64,192},{129,1},{193,65},{1,129},{65,193... | collective-permute-start | bytes 1179656 | tf_op jit(solution)/shard_map/ppermute | solution.py:18
  40.2 12.9 %collective-permute-start.27 = (bf16[64,3072]{1,0:T(8,128)(2,1)S(1)}, bf16[64,3072]{1,0:T(8,128)(2,1)S(1)}, u32[]{:S(2)}, u32[]{:S(2)}) collective-permute-start(bf16[64,3072]{1,0:T(8,128)(2,1)S(1)} %pad_maximum_fusion.1), channel_id=1, source_target_pairs={{192,0},{0,64},{64,128},{128,192},{193,1},{1,65},{65,129},{129,193... | collective-permute-start | bytes 1179656 | tf_op jit(solution)/shard_map/ppermute | solution.py:18
  50.0 30.4 %collective-permute-start.21 = (bf16[256,3072]{1,0:T(8,128)(2,1)}, bf16[256,3072]{1,0:T(8,128)(2,1)}, u32[]{:S(2)}, u32[]{:S(2)}) collective-permute-start(bf16[256,3072]{1,0:T(8,128)(2,1)} %constant_dynamic-update-slice_fusion.a_own), channel_id=1, source_target_pairs={{0,8},{8,0},{1,9},{9,1},{2,10},{10,2},{3,11},{11,3},{4,12},{12,4},... | collective-permute-start | bytes 4718600 | tf_op jit(solution)/shard_map/ppermute | solution.py:22
  53.9 30.1 %collective-permute-start.28 = (bf16[256,3072]{1,0:T(8,128)(2,1)}, bf16[256,3072]{1,0:T(8,128)(2,1)}, u32[]{:S(2)}, u32[]{:S(2)}) collective-permute-start(bf16[256,3072]{1,0:T(8,128)(2,1)} %constant_dynamic-update-slice_fusion.7.b_own), channel_id=1, source_target_pairs={{0,8},{8,0},{1,9},{9,1},{2,10},{10,2},{3,11},{11,3},{4,12},{12,4},... | collective-permute-start | bytes 4718600 | tf_op jit(solution)/shard_map/ppermute | solution.py:22
  60.3 3.5 %collective-permute-start = (bf16[512,384]{1,0:T(8,128)(2,1)S(1)}, bf16[512,384]{1,0:T(8,128)(2,1)S(1)}, u32[]{:S(2)}, u32[]{:S(2)}) collective-permute-start(bf16[512,384]{1,0:T(8,128)(2,1)S(1)} %bitcast.5), channel_id=1, source_target_pairs={{0,8},{8,0},{1,9},{9,1},{2,10},{10,2},{3,11},{11,3},{4,12},{12,4},... | collective-permute-start | bytes 1179656 | tf_op jit(solution)/shard_map/ppermute | solution.py:22
  71.7 20.4 %collective-permute-start.2 = (bf16[1552,128]{1,0:T(8,128)(2,1)S(1)}, bf16[1552,128]{1,0:T(8,128)(2,1)S(1)}, u32[]{:S(2)}, u32[]{:S(2)}) collective-permute-start(bf16[1552,128]{1,0:T(8,128)(2,1)S(1)} %get-tuple-element.22), channel_id=1, source_target_pairs={{192,0},{0,64},{64,128},{128,192},{193,1},{1,65},{65,129},{129,193... | collective-permute-start | bytes 1191944 | tf_op jit(solution)/shard_map/ppermute | solution.py:18
  71.8 38.4 %collective-permute-start.3 = (bf16[1552,128]{1,0:T(8,128)(2,1)}, bf16[1552,128]{1,0:T(8,128)(2,1)}, u32[]{:S(2)}, u32[]{:S(2)}) collective-permute-start(bf16[1552,128]{1,0:T(8,128)(2,1)} %get-tuple-element.23), channel_id=1, source_target_pairs={{64,0},{128,64},{192,128},{0,192},{65,1},{129,65},{193,129},{1,193... | collective-permute-start | bytes 1191944 | tf_op jit(solution)/shard_map/ppermute | solution.py:18
  74.4 35.9 %collective-permute-start.4 = (bf16[1552,128]{1,0:T(8,128)(2,1)}, bf16[1552,128]{1,0:T(8,128)(2,1)}, u32[]{:S(2)}, u32[]{:S(2)}) collective-permute-start(bf16[1552,128]{1,0:T(8,128)(2,1)} %get-tuple-element.24), channel_id=1, source_target_pairs={{128,0},{192,64},{0,128},{64,192},{129,1},{193,65},{1,129},{65,193... | collective-permute-start | bytes 1191944 | tf_op jit(solution)/shard_map/ppermute | solution.py:18
  80.4 42.1 %collective-permute-start.8 = (bf16[1552,128]{1,0:T(8,128)(2,1)}, bf16[1552,128]{1,0:T(8,128)(2,1)}, u32[]{:S(2)}, u32[]{:S(2)}) collective-permute-start(bf16[1552,128]{1,0:T(8,128)(2,1)} %get-tuple-element.30), channel_id=1, source_target_pairs={{48,0},{0,16},{16,32},{32,48},{49,1},{1,17},{17,33},{33,49},{50,2}... | collective-permute-start | bytes 1191944 | tf_op jit(solution)/shard_map/ppermute | solution.py:18
  84.1 40.3 %collective-permute-start.9 = (bf16[1552,128]{1,0:T(8,128)(2,1)}, bf16[1552,128]{1,0:T(8,128)(2,1)}, u32[]{:S(2)}, u32[]{:S(2)}) collective-permute-start(bf16[1552,128]{1,0:T(8,128)(2,1)} %get-tuple-element.31), channel_id=1, source_target_pairs={{16,0},{32,16},{48,32},{0,48},{17,1},{33,17},{49,33},{1,49},{18,2}... | collective-permute-start | bytes 1191944 | tf_op jit(solution)/shard_map/ppermute | solution.py:18
  92.9 31.5 %collective-permute-start.10 = (bf16[1552,128]{1,0:T(8,128)(2,1)S(1)}, bf16[1552,128]{1,0:T(8,128)(2,1)}, u32[]{:S(2)}, u32[]{:S(2)}) collective-permute-start(bf16[1552,128]{1,0:T(8,128)(2,1)S(1)} %get-tuple-element.32), channel_id=1, source_target_pairs={{32,0},{48,16},{0,32},{16,48},{33,1},{49,17},{1,33},{17,49},{34,2}... | collective-permute-start | bytes 1191944 | tf_op jit(solution)/shard_map/ppermute | solution.py:18
  103.2 21.2 %copy-start.2 = (f32[1536,128]{1,0:T(8,128)S(1)}, f32[1536,128]{1,0:T(8,128)}, u32[]{:S(2)}) copy-start(f32[1536,128]{1,0:T(8,128)} %copy-done.1) | copy-start | bytes 2359300
  103.2 48.7 %all-to-all-start.1 = ((f32[8,64,384]{2,1,0:T(8,128)}), f32[8,64,384]{2,1,0:T(8,128)}, u32[]{:S(2)}, u32[]{:S(2)}) async-start(f32[8,64,384]{2,1,0:T(8,128)} %bitcast.4), calls=%async_computation.1 | async-start | bytes 1572864 | tf_op jit(solution)/shard_map/all_to_all | solution.py:310
  112.6 17.2 %collective-permute-start.5 = (bf16[400,128]{1,0:T(8,128)(2,1)S(1)}, bf16[400,128]{1,0:T(8,128)(2,1)S(1)}, u32[]{:S(2)}, u32[]{:S(2)}) collective-permute-start(bf16[400,128]{1,0:T(8,128)(2,1)S(1)} %get-tuple-element.26), channel_id=1, source_target_pairs={{48,0},{0,16},{16,32},{32,48},{49,1},{1,17},{17,33},{33,49},{50,2}... | collective-permute-start | bytes 307208 | tf_op jit(solution)/shard_map/ppermute | solution.py:18
  122.5 7.3 %collective-permute-start.6 = (bf16[400,128]{1,0:T(8,128)(2,1)S(1)}, bf16[400,128]{1,0:T(8,128)(2,1)S(1)}, u32[]{:S(2)}, u32[]{:S(2)}) collective-permute-start(bf16[400,128]{1,0:T(8,128)(2,1)S(1)} %get-tuple-element.27), channel_id=1, source_target_pairs={{16,0},{32,16},{48,32},{0,48},{17,1},{33,17},{49,33},{1,49},{18,2}... | collective-permute-start | bytes 307208 | tf_op jit(solution)/shard_map/ppermute | solution.py:18
  122.5 7.3 %collective-permute-start.7 = (bf16[400,128]{1,0:T(8,128)(2,1)S(1)}, bf16[400,128]{1,0:T(8,128)(2,1)S(1)}, u32[]{:S(2)}, u32[]{:S(2)}) collective-permute-start(bf16[400,128]{1,0:T(8,128)(2,1)S(1)} %get-tuple-element.28), channel_id=1, source_target_pairs={{32,0},{48,16},{0,32},{16,48},{33,1},{49,17},{1,33},{17,49},{34,2}... | collective-permute-start | bytes 307208 | tf_op jit(solution)/shard_map/ppermute | solution.py:18
  126.8 5.4 %collective-permute-start.11 = (bf16[400,128]{1,0:T(8,128)(2,1)S(1)}, bf16[400,128]{1,0:T(8,128)(2,1)S(1)}, u32[]{:S(2)}, u32[]{:S(2)}) collective-permute-start(bf16[400,128]{1,0:T(8,128)(2,1)S(1)} %get-tuple-element.34), channel_id=1, source_target_pairs={{192,0},{0,64},{64,128},{128,192},{193,1},{1,65},{65,129},{129,193... | collective-permute-start | bytes 307208 | tf_op jit(solution)/shard_map/ppermute | solution.py:18
  127.1 5.4 %collective-permute-start.12 = (bf16[400,128]{1,0:T(8,128)(2,1)S(1)}, bf16[400,128]{1,0:T(8,128)(2,1)S(1)}, u32[]{:S(2)}, u32[]{:S(2)}) collective-permute-start(bf16[400,128]{1,0:T(8,128)(2,1)S(1)} %get-tuple-element.35), channel_id=1, source_target_pairs={{64,0},{128,64},{192,128},{0,192},{65,1},{129,65},{193,129},{1,193... | collective-permute-start | bytes 307208 | tf_op jit(solution)/shard_map/ppermute | solution.py:18
  129.7 5.1 %collective-permute-start.13 = (bf16[400,128]{1,0:T(8,128)(2,1)S(1)}, bf16[400,128]{1,0:T(8,128)(2,1)S(1)}, u32[]{:S(2)}, u32[]{:S(2)}) collective-permute-start(bf16[400,128]{1,0:T(8,128)(2,1)S(1)} %get-tuple-element.36), channel_id=1, source_target_pairs={{128,0},{192,64},{0,128},{64,192},{129,1},{193,65},{1,129},{65,193... | collective-permute-start | bytes 307208 | tf_op jit(solution)/shard_map/ppermute | solution.py:18
  135.8 15.3 %collective-permute-start.14 = (bf16[16,3072]{1,0:T(8,128)(2,1)S(1)}, bf16[16,3072]{1,0:T(8,128)(2,1)S(1)}, u32[]{:S(2)}, u32[]{:S(2)}) collective-permute-start(bf16[16,3072]{1,0:T(8,128)(2,1)S(1)} %get-tuple-element.38), channel_id=1, source_target_pairs={{0,8},{8,0},{1,9},{9,1},{2,10},{10,2},{3,11},{11,3},{4,12},{12,4},... | collective-permute-start | bytes 294920 | tf_op jit(solution)/shard_map/ppermute | solution.py:22
  (6 other events, 19.2 us)

commit v2 on v0

v2 whole, which is shorter than its diff:
```python
import jax
import jax.numpy as jnp
from jax import lax
from jax.experimental import pallas as pl
from jax.experimental.pallas import tpu as pltpu
from jax.sharding import Mesh, PartitionSpec as P

BF = jnp.bfloat16
F32 = jnp.float32
SPAN = 124.5
LANES = 128
STEPS = (1, 3, 2)
ROWS = ("x", "y", "core")
VMEM = pl.BlockSpec(memory_space=pltpu.VMEM)
SMEM = pl.BlockSpec(memory_space=pltpu.SMEM)
HBM = pl.BlockSpec(memory_space=pltpu.HBM)


def index_of(x, y, core):
    return ((x % 4) * 4 + y % 4) * 2 + core


def ring(distance, second):
    pairs = []
    for x in range(4):
        for y in range(4):
            for core in range(2):
                dx, dy = (0, distance) if (core == 1) != second else (distance, 0)
                pairs.append((index_of(x + dx, y + dy, core), index_of(x, y, core)))
    return pairs


def get(value, distance, second):
    return lax.ppermute(value, ROWS, ring(distance, second))


def swap(value):
    return lax.ppermute(value, "core", [(0, 1), (1, 0)])


def encode(block):
    size = jnp.abs(block)
    top = jnp.maximum(jnp.max(size, axis=0, keepdims=True), 1e-30)
    top = (top * (1.0 + 2.0**-7)).astype(BF).astype(F32)
    level = jnp.exp2(size * (2 * SPAN / top) - SPAN)
    return jnp.where(block < 0, -level, level).astype(BF), top


def decode(code, top):
    code = code.astype(F32)
    size = (jnp.log2(jnp.abs(code)) + SPAN) * (top / (2 * SPAN))
    return jnp.where(code < 0, -size, size)


def block_at(pos, first, second, lead, core):
    dx = jnp.where(lead == 0, first, second)
    dy = jnp.where(lead == 0, second, first)
    return (((pos[0] + dx) % 4) * 4 + (pos[1] + dy) % 4) * 2 + core


def token_rows(block):
    return aligned(block * 16, 16)


def aligned(start, size):
    return pl.ds(pl.multiple_of(start, size), size)


def split_kernel(pos, weight, own, other, sems):
    copies = [
        pltpu.make_async_copy(weight.at[:, aligned(core * 3072, 3072)], out, sems.at[i])
        for i, (core, out) in enumerate(((1 - pos[2], other), (pos[2], own)))
    ]
    for copy in copies:
        copy.start()
    for copy in copies:
        copy.wait()


def split(pos, weight):
    return pl.pallas_call(
        split_kernel,
        in_specs=[SMEM, HBM],
        out_specs=[VMEM, VMEM],
        out_shape=[jax.ShapeDtypeStruct((384, 3072), BF)] * 2,
        scratch_shapes=[pltpu.SemaphoreType.DMA((2,))],
        compiler_params=pltpu.CompilerParams(vmem_limit_bytes=53 * 2**20),
        cost_estimate=pl.CostEstimate(flops=0, bytes_accessed=5 * 2**20, transcendentals=0),
        name="split",
    )(pos, weight)


def project_kernel(pos, own_in, par_in, w_own, w_par, out0, out1, out2, out3, lhs, tops, keep, sems):
    core = pos[2]
    tops[...] = jnp.zeros_like(tops)
    for first in range(4):
        for second in range(4):
            for to_core in range(2):
                to = ((first * 4 + second) * 2 + to_core) * 16
                rows = token_rows(block_at(pos, first, second, core, to_core))
                lhs[to : to + 16, :384] = own_in[rows, :]
                lhs[to : to + 16, 384:] = par_in[rows, :]

    def columns(j):
        rhs = jnp.concatenate([w_own[:, j * 512 : (j + 1) * 512], w_par[:, j * 512 : (j + 1) * 512]])
        total = jnp.dot(lhs[...], rhs, preferred_element_type=F32)
        for k in range(4):
            lanes = slice(k * LANES, (k + 1) * LANES)
            tile = j * 4 + k
            rows = slice(tile * 128, (tile + 1) * 128)
            keep[rows, :] = total[:128, lanes]
            for p, out in enumerate((out1, out2, out3)):
                d = STEPS[p]
                code, top = encode(total[d * 128 : (d + 1) * 128, lanes])
                out[rows, :] = code
                tops[p, tile : tile + 1, :] = top

    copies = []
    for j in range(6):
        columns(j)
        rows = slice(j * 512, (j + 1) * 512)
        copies.append(pltpu.make_async_copy(keep.at[rows, :], out0.at[rows, :], sems.at[j]))
        copies[j].start()
    for p, out in enumerate((out1, out2, out3)):
        out[3072:3104, :] = tops[p].astype(BF)
    for copy in copies:
        copy.wait()


def project(pos, own_in, par_in, weight, weight_par):
    piece = jax.ShapeDtypeStruct((3104, LANES), BF)
    return pl.pallas_call(
        project_kernel,
        in_specs=[SMEM, VMEM, VMEM, VMEM, VMEM],
        out_specs=[HBM] + [VMEM] * 3,
        out_shape=[jax.ShapeDtypeStruct((3072, LANES), F32), piece, piece, piece],
        scratch_shapes=[
            pltpu.VMEM((512, 768), BF),
            pltpu.VMEM((3, 32, LANES), F32),
            pltpu.VMEM((3072, LANES), F32),
            pltpu.SemaphoreType.DMA((6,)),
        ],
        compiler_params=pltpu.CompilerParams(vmem_limit_bytes=28 * 2**20),
        cost_estimate=pl.CostEstimate(flops=2 * 512 * 768 * 3072, bytes_accessed=10 * 2**20, transcendentals=2**20),
        name="project",
    )(pos, own_in, par_in, weight, weight_par)


def relay_kernel(own_in, in1, in2, in3, keep, out1, out2, out3, tops, own, sem):
    copy = pltpu.make_async_copy(own_in, own, sem)
    copy.start()
    tops[...] = jnp.zeros_like(tops)
    copy.wait()
    heads = [ref[3072:3104, :].astype(F32) for ref in (in1, in2, in3)]
    for j in range(24):
        rows = slice(j * 128, (j + 1) * 128)
        total = own[rows, :]
        for ref, head in zip((in1, in2, in3), heads):
            total += decode(ref[rows, :], head[j : j + 1, :])
        to = slice(j * 32, (j + 1) * 32)
        keep[to, :] = total[:32, :]
        for p, out in enumerate((out1, out2, out3)):
            d = STEPS[p]
            code, top = encode(total[d * 32 : (d + 1) * 32, :])
            out[to, :] = code
            tops[p, j : j + 1, :] = top
    for p, out in enumerate((out1, out2, out3)):
        out[768:800, :] = tops[p].astype(BF)


def relay(own, pieces):
    piece = jax.ShapeDtypeStruct((800, LANES), BF)
    return pl.pallas_call(
        relay_kernel,
        in_specs=[HBM] + [VMEM] * 3,
        out_specs=[VMEM] * 4,
        out_shape=[jax.ShapeDtypeStruct((768, LANES), F32), piece, piece, piece],
        scratch_shapes=[
            pltpu.VMEM((3, 32, LANES), F32),
            pltpu.VMEM((3072, LANES), F32),
            pltpu.SemaphoreType.DMA,
        ],
        compiler_params=pltpu.CompilerParams(vmem_limit_bytes=16 * 2**20),
        cost_estimate=pl.CostEstimate(flops=2**23, bytes_accessed=5 * 2**20, transcendentals=2**21),
        name="relay",
    )(own, *pieces)


def finish_kernel(pos, own, in1, in2, in3, keep, send):
    core = pos[2]
    heads = [ref[768:800, :].astype(F32) for ref in (in1, in2, in3)]
    for j in range(24):
        rows = slice(j * 32, (j + 1) * 32)
        total = own[rows, :]
        for ref, head in zip((in1, in2, in3), heads):
            total += decode(ref[rows, :], head[j : j + 1, :])
        lanes = slice(j * LANES, (j + 1) * LANES)
        low, high = total[:16, :].astype(BF), total[16:, :].astype(BF)
        keep[:, lanes] = jnp.where(core == 0, low, high)
        send[:, lanes] = jnp.where(core == 0, high, low)


def finish(pos, own, pieces):
    return pl.pallas_call(
        finish_kernel,
        in_specs=[SMEM] + [VMEM] * 4,
        out_specs=[VMEM] * 2,
        out_shape=[jax.ShapeDtypeStruct((16, 3072), BF)] * 2,
        compiler_params=pltpu.CompilerParams(vmem_limit_bytes=16 * 2**20),
        cost_estimate=pl.CostEstimate(flops=2**20, bytes_accessed=2**20, transcendentals=2**18),
        name="finish",
    )(pos, own, *pieces)


CONTRACT_LAST = (((1,), (1,)), ((), ()))


def places(pos):
    for rel in range(2):
        core = pos[2] if rel == 0 else 1 - pos[2]
        for second in range(4):
            for first in range(4):
                yield ((rel * 4 + second) * 4 + first) * 16, block_at(pos, first, second, core, core)


def grad_inputs_kernel(pos, *refs):
    pieces, (w_own, w_other, out, acc) = refs[:8], refs[8:]
    for weight, core in ((w_own, pos[2]), (w_other, 1 - pos[2])):
        cot = jnp.concatenate([ref[:, aligned(core * 3072, 3072)] for ref in pieces])
        term = lax.dot_general(cot, weight[...], CONTRACT_LAST, preferred_element_type=F32)
        acc[...] = term if weight is w_own else acc[...] + term
    for start, block in places(pos):
        out[token_rows(block), :] = acc[start : start + 16, :]


def grad_inputs_terms(pos, pieces, w_own, w_other):
    return pl.pallas_call(
        grad_inputs_kernel,
        in_specs=[SMEM] + [VMEM] * 10,
        out_specs=VMEM,
        out_shape=jax.ShapeDtypeStruct((512, 384), F32),
        scratch_shapes=[pltpu.VMEM((512, 384), F32)],
        compiler_params=pltpu.CompilerParams(vmem_limit_bytes=28 * 2**20),
        cost_estimate=pl.CostEstimate(flops=2 * 512 * 384 * 6144, bytes_accessed=12 * 2**20, transcendentals=0),
        name="grad_inputs",
    )(pos, *pieces, w_own, w_other)


def grad_weight_kernel(pos, acts, *refs):
    pieces, (out, lhs, slots, sems) = refs[:8], refs[8:]
    width = 1024
    for start, block in places(pos):
        lhs[start : start + 16, :] = acts[token_rows(block), :]
    copies = []
    for j in range(6):
        lanes = slice(j * width, (j + 1) * width)
        cot = jnp.concatenate([ref[:, lanes] for ref in pieces])
        slots[j] = lax.dot_general(
            lhs[...], cot, (((0,), (0,)), ((), ())), preferred_element_type=F32
        ).astype(BF)
        copies.append(pltpu.make_async_copy(slots.at[j], out.at[:, lanes], sems.at[j]))
        copies[j].start()
    for copy in copies:
        copy.wait()


def grad_weight_of(pos, acts, pieces):
    return pl.pallas_call(
        grad_weight_kernel,
        in_specs=[SMEM] + [VMEM] * 9,
        out_specs=HBM,
        out_shape=jax.ShapeDtypeStruct((384, 6144), BF),
        scratch_shapes=[
            pltpu.VMEM((512, 384), BF),
            pltpu.VMEM((6, 384, 1024), BF),
            pltpu.SemaphoreType.DMA((6,)),
        ],
        compiler_params=pltpu.CompilerParams(vmem_limit_bytes=28 * 2**20),
        cost_estimate=pl.CostEstimate(flops=2 * 512 * 384 * 6144, bytes_accessed=12 * 2**20, transcendentals=0),
        name="grad_weight",
    )(pos, acts, *pieces)


def body(inputs, weight, grad_out):
    core = lax.axis_index("core")
    pos = jnp.stack([lax.axis_index("x"), lax.axis_index("y"), core]).astype(jnp.int32)

    w_own, w_other = split(pos, weight)
    w_par = swap(w_other)
    grad_out, inputs, _ = lax.optimization_barrier((grad_out, inputs, w_other))

    blocks = {0: grad_out}
    for d in STEPS:
        blocks[d] = get(grad_out, d, False)

    line = jnp.concatenate([blocks[d] for d in range(4)])

    gathered = lax.all_to_all(jnp.broadcast_to(inputs[None], (8, 64, 384)), "z", 0, 0).reshape(512, 384)
    gathered_par = swap(gathered)

    pieces = {0: line}
    for d in STEPS:
        pieces[d] = get(line, d, True)

    own, *sends = project(pos, gathered, gathered_par, w_own, w_par)
    got = [get(v, 4 - d, False) for v, d in zip(sends, STEPS)]

    others = {0: swap(line)}
    late, _ = lax.optimization_barrier(({d: pieces[d] for d in STEPS}, own))
    for d in STEPS:
        pieces[d] = late[d]
        others[d] = swap(late[d])
    pieces = [pieces[d] for d in range(4)] + [others[d] for d in range(4)]
    terms = grad_inputs_terms(pos, pieces, w_own, w_other)
    grad_weight = grad_weight_of(pos, gathered, pieces)
    terms, grad_weight = lax.optimization_barrier((terms, grad_weight))
    grad_inputs = lax.all_to_all(terms.reshape(8, 64, 384), "z", 0, 0).sum(axis=0).astype(BF)

    own, *sends = relay(own, got)
    got = [get(v, 4 - d, True) for v, d in zip(sends, STEPS)]
    mine, theirs = finish(pos, own, got)
    other = swap(theirs)
    projected = jnp.where(
        core == 0, jnp.concatenate([mine, other], axis=1), jnp.concatenate([other, mine], axis=1)
    )
    return projected, grad_inputs, grad_weight


def solution(mesh):
    fine = Mesh(mesh.devices.reshape(4, 4, 2, 8), ("x", "y", "core", "z"))
    placed = (P("z", ROWS), P(ROWS, "z"), P(ROWS, "z"))
    return jax.shard_map(
        body,
        mesh=fine,
        in_specs=placed,
        out_specs=(P(ROWS, "z"), P("z", ROWS), P(ROWS, "z")),
        check_vma=False,
    )
```

time: 237 us -> 92.3 us (0.39)
  waiting for transfers between devices: 174 us -> 21.5 us
  starting transfers between devices: 0.12 us -> 36.7 us
  Pallas kernels: 0 us -> 26.3 us
  matrix products: 24.9 us -> 0 us
  blocking collectives: 21.5 us -> 0 us
  between operations: 13.8 us -> 0.82 us
  local copies, waits for them, and re-layouts: 0.01 us -> 3.94 us
    reduce_scatter x2 -> x0, waiting for transfers between devices: 112 us -> none  [the longest x1 112 us: body(): lax.psum_scatter(jnp.dot(gathered, weight, preferred_element_type=jnp.flo...]
    all_gather x1 -> x0, waiting for transfers between devices: 61 us -> none  [body(): cotangent = lax.all_gather(grad_out, 'row', axis=0, tiled=True)]
    pallas_call x0 -> x6, Pallas kernels: none -> 26.3 us  [the longest x1 8.13 us: project(): pl.pallas_call(project_kernel, in_specs=[SMEM, VMEM, VMEM, VMEM, VMEM], o...]
    dot_general x3 -> x0, matrix products: 24.9 us -> none  [the longest x1 8.73 us: body(): jnp.dot(gathered, weight, preferred_element_type=jnp.float32)]
    ppermute x0 -> x19, starting transfers between devices: none -> 23.1 us  [the longest x12 13.3 us: get(): return lax.ppermute(value, ROWS, ring(distance, second))]
    all_gather x1 -> x0, blocking collectives: 21.5 us -> none  [body(): gathered = lax.all_gather(inputs, 'col', axis=0, tiled=True)]
    all_to_all x0 -> x2, starting transfers between devices: none -> 13.6 us  [the longest x1 8.19 us: body(): lax.all_to_all(jnp.broadcast_to(inputs[None], (8, 64, 384)), 'z', 0, 0)]
    ppermute x0 -> x19, waiting for transfers between devices: none -> 11.7 us  [the longest x12 9.13 us: get(): return lax.ppermute(value, ROWS, ring(distance, second))]
  transfers between devices with their start and end apart: 3 -> 21, of which waited for: 2 -> 8; matrix products, arithmetic and copies ran while one was open for 8% -> 2% of each run, Pallas kernels for 0% -> 23%
where the time goes in v2:
time: 92.3 us; the launch traced here: 91.9 us
  starting transfers between devices  36.7 us (40%)
  Pallas kernels  26.3 us (28%)
  waiting for transfers between devices  21.5 us (23%)
  local copies, waits for them, and re-layouts  3.94 us (4%)
  other arithmetic  2.61 us (3%)
    ppermute x12, starting transfers between devices, get(): return lax.ppermute(value, ROWS, ring(distance, second))  13.3 us
    ppermute x7, starting transfers between devices, swap(): return lax.ppermute(value, 'core', [(0, 1), (1, 0)])  9.8 us
    all_to_all x1, waiting for transfers between devices, body(): lax.all_to_all(jnp.broadcast_to(inputs[None], (8, 64, 384)), 'z', 0, 0)  9.79 us
    ppermute x12, waiting for transfers between devices, get(): return lax.ppermute(value, ROWS, ring(distance, second))  9.13 us
    all_to_all x1, starting transfers between devices, body(): lax.all_to_all(jnp.broadcast_to(inputs[None], (8, 64, 384)), 'z', 0, 0)  8.19 us
    pallas_call x1, Pallas kernels, project(): pl.pallas_call(project_kernel, in_specs=[SMEM, VMEM, VMEM, VMEM, VMEM], o...  8.13 us
    all_to_all x1, starting transfers between devices, body(): lax.all_to_all(terms.reshape(8, 64, 384), 'z', 0, 0).sum(axis=0).astype(BF)  5.43 us
    pallas_call x1, Pallas kernels, split(): pl.pallas_call(split_kernel, in_specs=[SMEM, HBM], out_specs=[VMEM, VMEM]...  5.13 us
  transfers between devices with their start and end apart: 21, of which 8 were waited for; matrix products, arithmetic and copies ran while one was open for 2% of the time, Pallas kernels for 23%

profile of v2, /device:TPU:1, one launch (start us, length us, event | category | flops | bytes accessed | tf_op | source)
XLA Modules:
  0.0 91.9 jit_solution(18283342320621429865)
XLA Ops:
  0.7 5.1 %split.1 = (bf16[384,3072]{1,0:T(8,128)(2,1)}, bf16[384,3072]{1,0:T(8,128)(2,1)}) custom-call(s32[3]{0:T(128)S(1)} %pad_add_fusion.pos, bf16[384,6144]{1,0:T(8,128)(2,1)} %weight.1), custom_call_target="tpu_custom_call" | custom-call | bytes 5242880 | tf_op jit(solution)/shard_map/split/pallas_call | solution.py:81
  5.9 3.3 %collective-permute-start.1 = (bf16[384,3072]{1,0:T(8,128)(2,1)}, bf16[384,3072]{1,0:T(8,128)(2,1)}, u32[]{:S(2)}, u32[]{:S(2)}) collective-permute-start(bf16[384,3072]{1,0:T(8,128)(2,1)} %get-tuple-element.22.refs_9_), channel_id=1, source_target_pairs={{0,8},{8,0},{1,9},{9,1},{2,10},{10,2},{3,11},{11,3},{4,12},{12,4},... | collective-permute-start | bytes 7077896 | tf_op jit(solution)/shard_map/ppermute | solution.py:38
  9.2 1.0 %collective-permute-start.9 = (bf16[16,6144]{1,0:T(8,128)(2,1)S(1)}, bf16[16,6144]{1,0:T(8,128)(2,1)S(1)}, u32[]{:S(2)}, u32[]{:S(2)}) collective-permute-start(bf16[16,6144]{1,0:T(8,128)(2,1)S(1)} %copy-done.6), channel_id=1, source_target_pairs={{64,0},{24,8},{80,16},{40,24},{96,32},{56,40},{112,48},{8,56},{128... | collective-permute-start | bytes 589832 | tf_op jit(solution)/shard_map/ppermute | solution.py:34
  10.5 0.7 collective-permute-start.11
  11.2 0.8 broadcast_in_dim.2
  12.0 8.2 %all-to-all-start = ((bf16[8,64,384]{2,1,0:T(8,128)(2,1)}), bf16[8,64,384]{2,1,0:T(8,128)(2,1)S(1)}, u32[]{:S(2)}, u32[]{:S(2)}) async-start(bf16[8,64,384]{2,1,0:T(8,128)(2,1)} %broadcast_in_dim.2), calls=%async_computation | async-start | bytes 786432 | tf_op jit(solution)/shard_map/all_to_all | solution.py:298
  20.3 2.6 %collective-permute-start.12 = (bf16[64,6144]{1,0:T(8,128)(2,1)S(1)}, bf16[64,6144]{1,0:T(8,128)(2,1)S(1)}, u32[]{:S(2)}, u32[]{:S(2)}) collective-permute-start(bf16[64,6144]{1,0:T(8,128)(2,1)S(1)} %constant_dynamic-update-slice_fusion.refs_0_), channel_id=1, source_target_pairs={{16,0},{72,8},{32,16},{88,24},{48,32},{104,40},{0,48},{120,56},{80... | collective-permute-start | bytes 2359304 | tf_op jit(solution)/shard_map/ppermute | solution.py:34
  24.0 9.8 %all-to-all-done = bf16[8,64,384]{2,1,0:T(8,128)(2,1)S(1)} async-done(((bf16[8,64,384]{2,1,0:T(8,128)(2,1)}), bf16[8,64,384]{2,1,0:T(8,128)(2,1)S(1)}, u32[]{:S(2)}, u32[]{:S(2)}) %all-to-all-start) | async-done | bytes 393248 | tf_op jit(solution)/shard_map/all_to_all | solution.py:298
  33.8 2.0 %collective-permute-start = (bf16[512,384]{1,0:T(8,128)(2,1)S(1)}, bf16[512,384]{1,0:T(8,128)(2,1)S(1)}, u32[]{:S(2)}, u32[]{:S(2)}) collective-permute-start(bf16[512,384]{1,0:T(8,128)(2,1)S(1)} %bitcast.6), channel_id=1, source_target_pairs={{0,8},{8,0},{1,9},{9,1},{2,10},{10,2},{3,11},{11,3},{4,12},{12,4},... | collective-permute-start | bytes 1179656 | tf_op jit(solution)/shard_map/ppermute | solution.py:38
  35.8 1.3 %collective-permute-done.par_in = bf16[512,384]{1,0:T(8,128)(2,1)S(1)} collective-permute-done((bf16[512,384]{1,0:T(8,128)(2,1)S(1)}, bf16[512,384]{1,0:T(8,128)(2,1)S(1)}, u32[]{:S(2)}, u32[]{:S(2)}) %collective-permute-start) | collective-permute-done | bytes 393248 | tf_op jit(solution)/shard_map/ppermute | solution.py:38
  37.6 1.7 %copy-done.1 = bf16[384,3072]{1,0:T(8,128)(2,1)S(1)} copy-done((bf16[384,3072]{1,0:T(8,128)(2,1)S(1)}, bf16[384,3072]{1,0:T(8,128)(2,1)}, u32[]{:S(2)}) %copy-start.1) | copy-done | bytes 2359320
  39.2 8.1 %project.1 = (f32[3072,128]{1,0:T(8,128)S(1)}, bf16[3104,128]{1,0:T(8,128)(2,1)}, bf16[3104,128]{1,0:T(8,128)(2,1)}, bf16[3104,128]{1,0:T(8,128)(2,1)}) custom-call(s32[3]{0:T(128)S(1)} %pad_add_fusion.pos, bf16[512,384]{1,0:T(8,128)(2,1)S(1)} %bitcast.7, bf16[512,384]{1,0:T(8,128)(2,1)S(1)} %collective-permute-done.par_in, bf16[384,3072]{1,0:T(8,128)(2,1)S(1)} %copy-done.1, ...), custom_call_target="tpu_custom_call" | custom-call | flops 2415919104 | bytes 10485760 | tf_op jit(solution)/shard_map/project/pallas_call | solution.py:132
  48.2 1.6 %collective-permute-start.2 = (bf16[3104,128]{1,0:T(8,128)(2,1)}, bf16[3104,128]{1,0:T(8,128)(2,1)}, u32[]{:S(2)}, u32[]{:S(2)}) collective-permute-start(bf16[3104,128]{1,0:T(8,128)(2,1)} %get-tuple-element.26), channel_id=1, source_target_pairs={{192,0},{56,8},{208,16},{8,24},{224,32},{24,40},{240,48},{40,56},{... | collective-permute-start | bytes 2383880 | tf_op jit(solution)/shard_map/ppermute | solution.py:34
  49.8 1.1 %collective-permute-start.3 = (bf16[3104,128]{1,0:T(8,128)(2,1)}, bf16[3104,128]{1,0:T(8,128)(2,1)}, u32[]{:S(2)}, u32[]{:S(2)}) collective-permute-start(bf16[3104,128]{1,0:T(8,128)(2,1)} %get-tuple-element.27), channel_id=1, source_target_pairs={{64,0},{24,8},{80,16},{40,24},{96,32},{56,40},{112,48},{8,56},{128... | collective-permute-start | bytes 2383880 | tf_op jit(solution)/shard_map/ppermute | solution.py:34
  50.8 0.9 collective-permute-start.4
  52.1 4.0 %grad_inputs.1 = f32[512,384]{1,0:T(8,128)S(1)} custom-call(s32[3]{0:T(128)S(1)} %pad_add_fusion.pos, bf16[64,6144]{1,0:T(8,128)(2,1)S(1)} %constant_dynamic-update-slice_fusion.refs_0_, bf16[64,6144]{1,0:T(8,128)(2,1)S(1)} %collective-permute-done.12.refs_1_, bf16[64,6144]{1,0:T(8,128)(2,1)S(1)} %collective-permute-done.13.refs_2_, ...), custom_call_target="tpu_custom_call" | custom-call | flops 2415919104 | bytes 12582912 | tf_op jit(solution)/shard_map/grad_inputs/pallas_call | solution.py:237
  56.1 4.3 %grad_weight.1 = bf16[384,6144]{1,0:T(8,128)(2,1)} custom-call(s32[3]{0:T(128)S(1)} %pad_add_fusion.pos, bf16[512,384]{1,0:T(8,128)(2,1)S(1)} %bitcast.8, bf16[64,6144]{1,0:T(8,128)(2,1)S(1)} %constant_dynamic-update-slice_fusion.refs_0_, bf16[64,6144]{1,0:T(8,128)(2,1)S(1)} %collective-permute-done.12.refs_1_, ...), custom_call_target="tpu_custom_call" | custom-call | flops 2415919104 | bytes 12582912 | tf_op jit(solution)/shard_map/grad_weight/pallas_call | solution.py:268
  60.4 5.4 %all-to-all-start.1 = ((f32[8,64,384]{2,1,0:T(8,128)}), f32[8,64,384]{2,1,0:T(8,128)}, u32[]{:S(2)}, u32[]{:S(2)}) async-start(f32[8,64,384]{2,1,0:T(8,128)} %bitcast.5), calls=%async_computation.1 | async-start | bytes 1572864 | tf_op jit(solution)/shard_map/all_to_all | solution.py:317
  65.9 4.0 %collective-permute-done.4.in3 = bf16[3104,128]{1,0:T(8,128)(2,1)} collective-permute-done((bf16[3104,128]{1,0:T(8,128)(2,1)}, bf16[3104,128]{1,0:T(8,128)(2,1)}, u32[]{:S(2)}, u32[]{:S(2)}) %collective-permute-start.4) | collective-permute-done | bytes 794656 | tf_op jit(solution)/shard_map/ppermute | solution.py:34
  69.9 1.4 %copy-done.5 = f32[3072,128]{1,0:T(8,128)S(1)} copy-done((f32[3072,128]{1,0:T(8,128)S(1)}, f32[3072,128]{1,0:T(8,128)}, u32[]{:S(2)}) %copy-start.5) | copy-done | bytes 1572888
  71.3 3.8 %relay.1 = (f32[768,128]{1,0:T(8,128)S(1)}, bf16[800,128]{1,0:T(8,128)(2,1)S(1)}, bf16[800,128]{1,0:T(8,128)(2,1)S(1)}, bf16[800,128]{1,0:T(8,128)(2,1)S(1)}) custom-call(f32[3072,128]{1,0:T(8,128)S(1)} %copy-done.5, bf16[3104,128]{1,0:T(8,128)(2,1)} %collective-permute-done.2.in1, bf16[3104,128]{1,0:T(8,128)(2,1)} %collective-permute-done.3.in2, ...), custom_call_target="tpu_custom_call" | custom-call | flops 8388608 | bytes 5242880 | tf_op jit(solution)/shard_map/relay/pallas_call | solution.py:173
  75.1 1.0 %collective-permute-start.5 = (bf16[800,128]{1,0:T(8,128)(2,1)S(1)}, bf16[800,128]{1,0:T(8,128)(2,1)S(1)}, u32[]{:S(2)}, u32[]{:S(2)}) collective-permute-start(bf16[800,128]{1,0:T(8,128)(2,1)S(1)} %get-tuple-element.30), channel_id=1, source_target_pairs={{48,0},{200,8},{0,16},{216,24},{16,32},{232,40},{32,48},{248,56},{... | collective-permute-start | bytes 614408 | tf_op jit(solution)/shard_map/ppermute | solution.py:34
  76.1 1.8 %collective-permute-start.6 = (bf16[800,128]{1,0:T(8,128)(2,1)S(1)}, bf16[800,128]{1,0:T(8,128)(2,1)S(1)}, u32[]{:S(2)}, u32[]{:S(2)}) collective-permute-start(bf16[800,128]{1,0:T(8,128)(2,1)S(1)} %get-tuple-element.31), channel_id=1, source_target_pairs={{16,0},{72,8},{32,16},{88,24},{48,32},{104,40},{0,48},{120,56},{80... | collective-permute-start | bytes 614408 | tf_op jit(solution)/shard_map/ppermute | solution.py:34
  77.9 1.2 %collective-permute-start.7 = (bf16[800,128]{1,0:T(8,128)(2,1)S(1)}, bf16[800,128]{1,0:T(8,128)(2,1)S(1)}, u32[]{:S(2)}, u32[]{:S(2)}) collective-permute-start(bf16[800,128]{1,0:T(8,128)(2,1)S(1)} %get-tuple-element.32), channel_id=1, source_target_pairs={{32,0},{136,8},{48,16},{152,24},{0,32},{168,40},{16,48},{184,56},{... | collective-permute-start | bytes 614408 | tf_op jit(solution)/shard_map/ppermute | solution.py:34
  79.1 2.3 %collective-permute-done.5.in1 = bf16[800,128]{1,0:T(8,128)(2,1)S(1)} collective-permute-done((bf16[800,128]{1,0:T(8,128)(2,1)S(1)}, bf16[800,128]{1,0:T(8,128)(2,1)S(1)}, u32[]{:S(2)}, u32[]{:S(2)}) %collective-permute-start.5) | collective-permute-done | bytes 204832 | tf_op jit(solution)/shard_map/ppermute | solution.py:34
  81.4 1.4 %collective-permute-done.6.in2 = bf16[800,128]{1,0:T(8,128)(2,1)S(1)} collective-permute-done((bf16[800,128]{1,0:T(8,128)(2,1)S(1)}, bf16[800,128]{1,0:T(8,128)(2,1)S(1)}, u32[]{:S(2)}, u32[]{:S(2)}) %collective-permute-start.6) | collective-permute-done | bytes 204832 | tf_op jit(solution)/shard_map/ppermute | solution.py:34
  82.8 1.4 %collective-permute-done.7.in3 = bf16[800,128]{1,0:T(8,128)(2,1)S(1)} collective-permute-done((bf16[800,128]{1,0:T(8,128)(2,1)S(1)}, bf16[800,128]{1,0:T(8,128)(2,1)S(1)}, u32[]{:S(2)}, u32[]{:S(2)}) %collective-permute-start.7) | collective-permute-done | bytes 204832 | tf_op jit(solution)/shard_map/ppermute | solution.py:34
  84.2 0.9 %finish.1 = (bf16[16,3072]{1,0:T(8,128)(2,1)S(1)}, bf16[16,3072]{1,0:T(8,128)(2,1)S(1)}) custom-call(s32[3]{0:T(128)S(1)} %pad_add_fusion.pos, f32[768,128]{1,0:T(8,128)S(1)} %get-tuple-element.29.own, bf16[800,128]{1,0:T(8,128)(2,1)S(1)} %collective-permute-done.5.in1, bf16[800,128]{1,0:T(8,128)(2,1)S(1)} %collective-permute-done.6.in2, ...), custom_call_target="tpu_custom_call" | custom-call | flops 1048576 | bytes 1048576 | tf_op jit(solution)/shard_map/finish/pallas_call | solution.py:204
  85.1 3.3 %collective-permute-start.8 = (bf16[16,3072]{1,0:T(8,128)(2,1)S(1)}, bf16[16,3072]{1,0:T(8,128)(2,1)S(1)}, u32[]{:S(2)}, u32[]{:S(2)}) collective-permute-start(bf16[16,3072]{1,0:T(8,128)(2,1)S(1)} %get-tuple-element.34), channel_id=1, source_target_pairs={{0,8},{8,0},{1,9},{9,1},{2,10},{10,2},{3,11},{11,3},{4,12},{12,4},... | collective-permute-start | bytes 294920 | tf_op jit(solution)/shard_map/ppermute | solution.py:38
  88.4 0.9 %collective-permute-done.8 = bf16[16,3072]{1,0:T(8,128)(2,1)S(1)} collective-permute-done((bf16[16,3072]{1,0:T(8,128)(2,1)S(1)}, bf16[16,3072]{1,0:T(8,128)(2,1)S(1)}, u32[]{:S(2)}, u32[]{:S(2)}) %collective-permute-start.8) | collective-permute-done | bytes 98336 | tf_op jit(solution)/shard_map/ppermute | solution.py:38
  89.4 0.7 maximum_select_fusion
  90.1 1.8 %reduce_sum.9 = bf16[64,384]{1,0:T(8,128)(2,1)} reduce(f32[8,64,384]{2,1,0:T(8,128)} %all-to-all-done.1, f32[]{:T(128)} %constant.18.clone.1), dimensions={0}, to_apply=%region_0.0 | reduce | flops 172032 | bytes 835588 | tf_op jit(solution)/shard_map/reduce_sum | solution.py:317
  (40 shorter events, 3.1 us)
Async XLA Ops:
  0.7 8.5 %copy-start.6 = (bf16[16,6144]{1,0:T(8,128)(2,1)S(1)}, bf16[16,6144]{1,0:T(8,128)(2,1)}, u32[]{:S(2)}) copy-start(bf16[16,6144]{1,0:T(8,128)(2,1)} %param.5) | copy-start | bytes 589828
  0.7 10.5 %copy-start.7 = (bf16[64,384]{1,0:T(8,128)(2,1)S(1)}, bf16[64,384]{1,0:T(8,128)(2,1)}, u32[]{:S(2)}) copy-start(bf16[64,384]{1,0:T(8,128)(2,1)} %param.3) | copy-start | bytes 147460
  5.9 31.7 %collective-permute-start.1 = (bf16[384,3072]{1,0:T(8,128)(2,1)}, bf16[384,3072]{1,0:T(8,128)(2,1)}, u32[]{:S(2)}, u32[]{:S(2)}) collective-permute-start(bf16[384,3072]{1,0:T(8,128)(2,1)} %get-tuple-element.22.refs_9_), channel_id=1, source_target_pairs={{0,8},{8,0},{1,9},{9,1},{2,10},{10,2},{3,11},{11,3},{4,12},{12,4},... | collective-permute-start | bytes 7077896 | tf_op jit(solution)/shard_map/ppermute | solution.py:38
  9.2 11.0 %collective-permute-start.9 = (bf16[16,6144]{1,0:T(8,128)(2,1)S(1)}, bf16[16,6144]{1,0:T(8,128)(2,1)S(1)}, u32[]{:S(2)}, u32[]{:S(2)}) collective-permute-start(bf16[16,6144]{1,0:T(8,128)(2,1)S(1)} %copy-done.6), channel_id=1, source_target_pairs={{64,0},{24,8},{80,16},{40,24},{96,32},{56,40},{112,48},{8,56},{128... | collective-permute-start | bytes 589832 | tf_op jit(solution)/shard_map/ppermute | solution.py:34
  10.2 10.1 %collective-permute-start.10 = (bf16[16,6144]{1,0:T(8,128)(2,1)S(1)}, bf16[16,6144]{1,0:T(8,128)(2,1)S(1)}, u32[]{:S(2)}, u32[]{:S(2)}) collective-permute-start(bf16[16,6144]{1,0:T(8,128)(2,1)S(1)} %copy-done.6), channel_id=1, source_target_pairs={{128,0},{40,8},{144,16},{56,24},{160,32},{8,40},{176,48},{24,56},{... | collective-permute-start | bytes 589832 | tf_op jit(solution)/shard_map/ppermute | solution.py:34
  10.5 9.8 %collective-permute-start.11 = (bf16[16,6144]{1,0:T(8,128)(2,1)S(1)}, bf16[16,6144]{1,0:T(8,128)(2,1)S(1)}, u32[]{:S(2)}, u32[]{:S(2)}) collective-permute-start(bf16[16,6144]{1,0:T(8,128)(2,1)S(1)} %copy-done.6), channel_id=1, source_target_pairs={{192,0},{56,8},{208,16},{8,24},{224,32},{24,40},{240,48},{40,56},{... | collective-permute-start | bytes 589832 | tf_op jit(solution)/shard_map/ppermute | solution.py:34
  12.0 21.8 %all-to-all-start = ((bf16[8,64,384]{2,1,0:T(8,128)(2,1)}), bf16[8,64,384]{2,1,0:T(8,128)(2,1)S(1)}, u32[]{:S(2)}, u32[]{:S(2)}) async-start(bf16[8,64,384]{2,1,0:T(8,128)(2,1)} %broadcast_in_dim.2), calls=%async_computation | async-start | bytes 786432 | tf_op jit(solution)/shard_map/all_to_all | solution.py:298
  20.3 27.1 %collective-permute-start.12 = (bf16[64,6144]{1,0:T(8,128)(2,1)S(1)}, bf16[64,6144]{1,0:T(8,128)(2,1)S(1)}, u32[]{:S(2)}, u32[]{:S(2)}) collective-permute-start(bf16[64,6144]{1,0:T(8,128)(2,1)S(1)} %constant_dynamic-update-slice_fusion.refs_0_), channel_id=1, source_target_pairs={{16,0},{72,8},{32,16},{88,24},{48,32},{104,40},{0,48},{120,56},{80... | collective-permute-start | bytes 2359304 | tf_op jit(solution)/shard_map/ppermute | solution.py:34
  22.9 24.5 %collective-permute-start.13 = (bf16[64,6144]{1,0:T(8,128)(2,1)S(1)}, bf16[64,6144]{1,0:T(8,128)(2,1)S(1)}, u32[]{:S(2)}, u32[]{:S(2)}) collective-permute-start(bf16[64,6144]{1,0:T(8,128)(2,1)S(1)} %constant_dynamic-update-slice_fusion.refs_0_), channel_id=1, source_target_pairs={{32,0},{136,8},{48,16},{152,24},{0,32},{168,40},{16,48},{184,56},{... | collective-permute-start | bytes 2359304 | tf_op jit(solution)/shard_map/ppermute | solution.py:34
  23.4 24.0 %collective-permute-start.14 = (bf16[64,6144]{1,0:T(8,128)(2,1)S(1)}, bf16[64,6144]{1,0:T(8,128)(2,1)S(1)}, u32[]{:S(2)}, u32[]{:S(2)}) collective-permute-start(bf16[64,6144]{1,0:T(8,128)(2,1)S(1)} %constant_dynamic-update-slice_fusion.refs_0_), channel_id=1, source_target_pairs={{48,0},{200,8},{0,16},{216,24},{16,32},{232,40},{32,48},{248,56},{... | collective-permute-start | bytes 2359304 | tf_op jit(solution)/shard_map/ppermute | solution.py:34
  33.8 3.4 %collective-permute-start = (bf16[512,384]{1,0:T(8,128)(2,1)S(1)}, bf16[512,384]{1,0:T(8,128)(2,1)S(1)}, u32[]{:S(2)}, u32[]{:S(2)}) collective-permute-start(bf16[512,384]{1,0:T(8,128)(2,1)S(1)} %bitcast.6), channel_id=1, source_target_pairs={{0,8},{8,0},{1,9},{9,1},{2,10},{10,2},{3,11},{11,3},{4,12},{12,4},... | collective-permute-start | bytes 1179656 | tf_op jit(solution)/shard_map/ppermute | solution.py:38
  37.2 12.6 %collective-permute-start.15 = (bf16[64,6144]{1,0:T(8,128)(2,1)S(1)}, bf16[64,6144]{1,0:T(8,128)(2,1)S(1)}, u32[]{:S(2)}, u32[]{:S(2)}) collective-permute-start(bf16[64,6144]{1,0:T(8,128)(2,1)S(1)} %constant_dynamic-update-slice_fusion.refs_0_), channel_id=1, source_target_pairs={{0,8},{8,0},{1,9},{9,1},{2,10},{10,2},{3,11},{11,3},{4,12},{12,4},... | collective-permute-start | bytes 2359304 | tf_op jit(solution)/shard_map/ppermute | solution.py:38
  37.6 1.7 %copy-start.1 = (bf16[384,3072]{1,0:T(8,128)(2,1)S(1)}, bf16[384,3072]{1,0:T(8,128)(2,1)}, u32[]{:S(2)}) copy-start(bf16[384,3072]{1,0:T(8,128)(2,1)} %get-tuple-element.24.w_own.refs_8_) | copy-start | bytes 7077892
  39.2 12.8 %copy-start.2 = (bf16[384,3072]{1,0:T(8,128)(2,1)S(1)}, bf16[384,3072]{1,0:T(8,128)(2,1)}, u32[]{:S(2)}) copy-start(bf16[384,3072]{1,0:T(8,128)(2,1)} %get-tuple-element.24.w_own.refs_8_) | copy-start | bytes 7077892
  39.2 12.8 %copy-start.3 = (bf16[384,3072]{1,0:T(8,128)(2,1)S(1)}, bf16[384,3072]{1,0:T(8,128)(2,1)}, u32[]{:S(2)}) copy-start(bf16[384,3072]{1,0:T(8,128)(2,1)} %get-tuple-element.22.refs_9_) | copy-start | bytes 7077892
  47.4 8.7 %copy-start.4 = (f32[3072,128]{1,0:T(8,128)}, f32[3072,128]{1,0:T(8,128)S(1)}, u32[]{:S(2)}) copy-start(f32[3072,128]{1,0:T(8,128)S(1)} %get-tuple-element.25.own_in) | copy-start | bytes 4718596
  47.4 3.4 %collective-permute-start.16 = (bf16[64,6144]{1,0:T(8,128)(2,1)S(1)}, bf16[64,6144]{1,0:T(8,128)(2,1)S(1)}, u32[]{:S(2)}, u32[]{:S(2)}) collective-permute-start(bf16[64,6144]{1,0:T(8,128)(2,1)S(1)} %collective-permute-done.12.refs_1_), channel_id=1, source_target_pairs={{0,8},{8,0},{1,9},{9,1},{2,10},{10,2},{3,11},{11,3},{4,12},{12,4},... | collective-permute-start | bytes 2359304 | tf_op jit(solution)/shard_map/ppermute | solution.py:38
  47.6 4.1 %collective-permute-start.17 = (bf16[64,6144]{1,0:T(8,128)(2,1)S(1)}, bf16[64,6144]{1,0:T(8,128)(2,1)S(1)}, u32[]{:S(2)}, u32[]{:S(2)}) collective-permute-start(bf16[64,6144]{1,0:T(8,128)(2,1)S(1)} %collective-permute-done.13.refs_2_), channel_id=1, source_target_pairs={{0,8},{8,0},{1,9},{9,1},{2,10},{10,2},{3,11},{11,3},{4,12},{12,4},... | collective-permute-start | bytes 2359304 | tf_op jit(solution)/shard_map/ppermute | solution.py:38
  48.0 4.0 %collective-permute-start.18 = (bf16[64,6144]{1,0:T(8,128)(2,1)S(1)}, bf16[64,6144]{1,0:T(8,128)(2,1)S(1)}, u32[]{:S(2)}, u32[]{:S(2)}) collective-permute-start(bf16[64,6144]{1,0:T(8,128)(2,1)S(1)} %collective-permute-done.14.refs_3_), channel_id=1, source_target_pairs={{0,8},{8,0},{1,9},{9,1},{2,10},{10,2},{3,11},{11,3},{4,12},{12,4},... | collective-permute-start | bytes 2359304 | tf_op jit(solution)/shard_map/ppermute | solution.py:38
  48.2 17.7 %collective-permute-start.2 = (bf16[3104,128]{1,0:T(8,128)(2,1)}, bf16[3104,128]{1,0:T(8,128)(2,1)}, u32[]{:S(2)}, u32[]{:S(2)}) collective-permute-start(bf16[3104,128]{1,0:T(8,128)(2,1)} %get-tuple-element.26), channel_id=1, source_target_pairs={{192,0},{56,8},{208,16},{8,24},{224,32},{24,40},{240,48},{40,56},{... | collective-permute-start | bytes 2383880 | tf_op jit(solution)/shard_map/ppermute | solution.py:34
  49.8 16.1 %collective-permute-start.3 = (bf16[3104,128]{1,0:T(8,128)(2,1)}, bf16[3104,128]{1,0:T(8,128)(2,1)}, u32[]{:S(2)}, u32[]{:S(2)}) collective-permute-start(bf16[3104,128]{1,0:T(8,128)(2,1)} %get-tuple-element.27), channel_id=1, source_target_pairs={{64,0},{24,8},{80,16},{40,24},{96,32},{56,40},{112,48},{8,56},{128... | collective-permute-start | bytes 2383880 | tf_op jit(solution)/shard_map/ppermute | solution.py:34
  50.8 19.1 %collective-permute-start.4 = (bf16[3104,128]{1,0:T(8,128)(2,1)}, bf16[3104,128]{1,0:T(8,128)(2,1)}, u32[]{:S(2)}, u32[]{:S(2)}) collective-permute-start(bf16[3104,128]{1,0:T(8,128)(2,1)} %get-tuple-element.28), channel_id=1, source_target_pairs={{128,0},{40,8},{144,16},{56,24},{160,32},{8,40},{176,48},{24,56},{... | collective-permute-start | bytes 2383880 | tf_op jit(solution)/shard_map/ppermute | solution.py:34
  56.1 4.3 %copy-start = (f32[512,384]{1,0:T(8,128)}, f32[512,384]{1,0:T(8,128)S(1)}, u32[]{:S(2)}) copy-start(f32[512,384]{1,0:T(8,128)S(1)} %grad_inputs.1) | copy-start | bytes 2359300
  60.4 29.7 %all-to-all-start.1 = ((f32[8,64,384]{2,1,0:T(8,128)}), f32[8,64,384]{2,1,0:T(8,128)}, u32[]{:S(2)}, u32[]{:S(2)}) async-start(f32[8,64,384]{2,1,0:T(8,128)} %bitcast.5), calls=%async_computation.1 | async-start | bytes 1572864 | tf_op jit(solution)/shard_map/all_to_all | solution.py:317
  69.9 1.4 %copy-start.5 = (f32[3072,128]{1,0:T(8,128)S(1)}, f32[3072,128]{1,0:T(8,128)}, u32[]{:S(2)}) copy-start(f32[3072,128]{1,0:T(8,128)} %copy-done.4) | copy-start | bytes 4718596
  75.1 6.3 %collective-permute-start.5 = (bf16[800,128]{1,0:T(8,128)(2,1)S(1)}, bf16[800,128]{1,0:T(8,128)(2,1)S(1)}, u32[]{:S(2)}, u32[]{:S(2)}) collective-permute-start(bf16[800,128]{1,0:T(8,128)(2,1)S(1)} %get-tuple-element.30), channel_id=1, source_target_pairs={{48,0},{200,8},{0,16},{216,24},{16,32},{232,40},{32,48},{248,56},{... | collective-permute-start | bytes 614408 | tf_op jit(solution)/shard_map/ppermute | solution.py:34
  76.1 6.7 %collective-permute-start.6 = (bf16[800,128]{1,0:T(8,128)(2,1)S(1)}, bf16[800,128]{1,0:T(8,128)(2,1)S(1)}, u32[]{:S(2)}, u32[]{:S(2)}) collective-permute-start(bf16[800,128]{1,0:T(8,128)(2,1)S(1)} %get-tuple-element.31), channel_id=1, source_target_pairs={{16,0},{72,8},{32,16},{88,24},{48,32},{104,40},{0,48},{120,56},{80... | collective-permute-start | bytes 614408 | tf_op jit(solution)/shard_map/ppermute | solution.py:34
  77.9 6.3 %collective-permute-start.7 = (bf16[800,128]{1,0:T(8,128)(2,1)S(1)}, bf16[800,128]{1,0:T(8,128)(2,1)S(1)}, u32[]{:S(2)}, u32[]{:S(2)}) collective-permute-start(bf16[800,128]{1,0:T(8,128)(2,1)S(1)} %get-tuple-element.32), channel_id=1, source_target_pairs={{32,0},{136,8},{48,16},{152,24},{0,32},{168,40},{16,48},{184,56},{... | collective-permute-start | bytes 614408 | tf_op jit(solution)/shard_map/ppermute | solution.py:34
  85.1 4.3 %collective-permute-start.8 = (bf16[16,3072]{1,0:T(8,128)(2,1)S(1)}, bf16[16,3072]{1,0:T(8,128)(2,1)S(1)}, u32[]{:S(2)}, u32[]{:S(2)}) collective-permute-start(bf16[16,3072]{1,0:T(8,128)(2,1)S(1)} %get-tuple-element.34), channel_id=1, source_target_pairs={{0,8},{8,0},{1,9},{9,1},{2,10},{10,2},{3,11},{11,3},{4,12},{12,4},... | collective-permute-start | bytes 294920 | tf_op jit(solution)/shard_map/ppermute | solution.py:38

commit v3 on v2

v3 whole, which is shorter than its diff:
```python
import jax
import jax.numpy as jnp
from jax import lax
from jax.experimental import pallas as pl
from jax.experimental.pallas import tpu as pltpu
from jax.sharding import Mesh, PartitionSpec as P

BF = jnp.bfloat16
F32 = jnp.float32
SPAN = 124.5
LANES = 128
STEPS = (1, 3, 2)
ROWS = ("x", "y", "core")
VMEM = pl.BlockSpec(memory_space=pltpu.VMEM)
SMEM = pl.BlockSpec(memory_space=pltpu.SMEM)
HBM = pl.BlockSpec(memory_space=pltpu.HBM)


def index_of(x, y, core):
    return ((x % 4) * 4 + y % 4) * 2 + core


def ring(distance, second):
    pairs = []
    for x in range(4):
        for y in range(4):
            for core in range(2):
                dx, dy = (0, distance) if (core == 1) != second else (distance, 0)
                pairs.append((index_of(x + dx, y + dy, core), index_of(x, y, core)))
    return pairs


def get(value, distance, second):
    return lax.ppermute(value, ROWS, ring(distance, second))


def swap(value):
    return lax.ppermute(value, "core", [(0, 1), (1, 0)])


def encode(block):
    size = jnp.abs(block)
    top = jnp.maximum(jnp.max(size, axis=0, keepdims=True), 1e-30)
    top = (top * (1.0 + 2.0**-7)).astype(BF).astype(F32)
    level = jnp.exp2(size * (2 * SPAN / top) - SPAN)
    return jnp.where(block < 0, -level, level).astype(BF), top


def decode(code, top):
    code = code.astype(F32)
    size = (jnp.log2(jnp.abs(code)) + SPAN) * (top / (2 * SPAN))
    return jnp.where(code < 0, -size, size)


def block_at(pos, first, second, lead, core):
    dx = jnp.where(lead == 0, first, second)
    dy = jnp.where(lead == 0, second, first)
    return (((pos[0] + dx) % 4) * 4 + (pos[1] + dy) % 4) * 2 + core


def token_rows(block):
    return aligned(block * 16, 16)


def aligned(start, size):
    return pl.ds(pl.multiple_of(start, size), size)


def project_kernel(
    pos, own_in, par_in, weight, w_par, out0, out1, out2, out3, lhs, rhs, tops, keep, codes, in_sems, out_sems, end_sems
):
    core = pos[2]
    reads, writes = [], []
    for j in range(12):
        lanes = slice(j * 512, (j + 1) * 512)
        reads.append(
            (
                pltpu.make_async_copy(weight.at[:, lanes], rhs.at[:384, lanes], in_sems.at[0, j]),
                pltpu.make_async_copy(w_par.at[:, lanes], rhs.at[384:, lanes], in_sems.at[1, j]),
            )
        )
        for read in reads[j]:
            read.start()
    tops[...] = jnp.zeros_like(tops)
    for first in range(4):
        for second in range(4):
            to = (first * 4 + second) * 16
            rows = token_rows(block_at(pos, first, second, core, core))
            lhs[to : to + 16, :384] = own_in[rows, :]
            lhs[to : to + 16, 384:] = par_in[rows, :]

    for j in range(12):
        for read in reads[j]:
            read.wait()
        total = jnp.dot(lhs[...], rhs[:, j * 512 : (j + 1) * 512], preferred_element_type=F32)
        for k in range(4):
            lanes = slice(k * LANES, (k + 1) * LANES)
            tile = j * 4 + k
            rows = slice(tile * 64, (tile + 1) * 64)
            keep[rows, :] = total[:64, lanes]
            for p in range(3):
                d = STEPS[p]
                code, top = encode(total[d * 64 : (d + 1) * 64, lanes])
                codes[p, rows, :] = code
                tops[p, tile : tile + 1, :] = top
        rows = slice(j * 256, (j + 1) * 256)
        writes.append(pltpu.make_async_copy(keep.at[rows, :], out0.at[rows, :], out_sems.at[0, j]))
        for p, out in enumerate((out1, out2, out3)):
            writes.append(pltpu.make_async_copy(codes.at[p, rows, :], out.at[rows, :], out_sems.at[p + 1, j]))
        for write in writes[-4:]:
            write.start()

    for p, out in enumerate((out1, out2, out3)):
        codes[p, 3072:3120, :] = tops[p].astype(BF)
        writes.append(pltpu.make_async_copy(codes.at[p, 3072:3120, :], out.at[3072:3120, :], end_sems.at[p]))
        writes[-1].start()
    for write in writes:
        write.wait()


def project(pos, own_in, par_in, weight, weight_par):
    piece = jax.ShapeDtypeStruct((3120, LANES), BF)
    return pl.pallas_call(
        project_kernel,
        in_specs=[SMEM, VMEM, VMEM, HBM, HBM],
        out_specs=[HBM] * 4,
        out_shape=[jax.ShapeDtypeStruct((3072, LANES), F32), piece, piece, piece],
        scratch_shapes=[
            pltpu.VMEM((256, 768), BF),
            pltpu.VMEM((768, 6144), BF),
            pltpu.VMEM((3, 48, LANES), F32),
            pltpu.VMEM((3072, LANES), F32),
            pltpu.VMEM((3, 3120, LANES), BF),
            pltpu.SemaphoreType.DMA((2, 12)),
            pltpu.SemaphoreType.DMA((4, 12)),
            pltpu.SemaphoreType.DMA((3,)),
        ],
        compiler_params=pltpu.CompilerParams(vmem_limit_bytes=56 * 2**20),
        cost_estimate=pl.CostEstimate(flops=2 * 512 * 768 * 3072, bytes_accessed=10 * 2**20, transcendentals=2**20),
        name="project",
    )(pos, own_in, par_in, weight, weight_par)


def relay_kernel(own_in, in1, in2, in3, keep, out1, out2, out3, tops, own, sem):
    copy = pltpu.make_async_copy(own_in, own, sem)
    copy.start()
    tops[...] = jnp.zeros_like(tops)
    copy.wait()
    heads = [ref[3072:3120, :].astype(F32) for ref in (in1, in2, in3)]
    for j in range(48):
        rows = slice(j * 64, (j + 1) * 64)
        total = own[rows, :]
        for ref, head in zip((in1, in2, in3), heads):
            total += decode(ref[rows, :], head[j : j + 1, :])
        to = slice(j * 16, (j + 1) * 16)
        keep[to, :] = total[:16, :]
        for p, out in enumerate((out1, out2, out3)):
            d = STEPS[p]
            code, top = encode(total[d * 16 : (d + 1) * 16, :])
            out[to, :] = code
            tops[p, j : j + 1, :] = top
    for p, out in enumerate((out1, out2, out3)):
        out[768:816, :] = tops[p].astype(BF)


def relay(own, pieces):
    piece = jax.ShapeDtypeStruct((816, LANES), BF)
    return pl.pallas_call(
        relay_kernel,
        in_specs=[HBM] + [VMEM] * 3,
        out_specs=[VMEM] * 4,
        out_shape=[jax.ShapeDtypeStruct((768, LANES), F32), piece, piece, piece],
        scratch_shapes=[
            pltpu.VMEM((3, 48, LANES), F32),
            pltpu.VMEM((3072, LANES), F32),
            pltpu.SemaphoreType.DMA,
        ],
        compiler_params=pltpu.CompilerParams(vmem_limit_bytes=16 * 2**20),
        cost_estimate=pl.CostEstimate(flops=2**23, bytes_accessed=5 * 2**20, transcendentals=2**21),
        name="relay",
    )(own, *pieces)


def finish_kernel(own, in1, in2, in3, out):
    heads = [ref[768:816, :].astype(F32) for ref in (in1, in2, in3)]
    for j in range(48):
        rows = slice(j * 16, (j + 1) * 16)
        total = own[rows, :]
        for ref, head in zip((in1, in2, in3), heads):
            total += decode(ref[rows, :], head[j : j + 1, :])
        out[:, j * LANES : (j + 1) * LANES] = total.astype(BF)


def finish(own, pieces):
    return pl.pallas_call(
        finish_kernel,
        in_specs=[VMEM] * 4,
        out_specs=VMEM,
        out_shape=jax.ShapeDtypeStruct((16, 6144), BF),
        compiler_params=pltpu.CompilerParams(vmem_limit_bytes=16 * 2**20),
        cost_estimate=pl.CostEstimate(flops=2**33, bytes_accessed=2**20, transcendentals=2**18),
        name="finish",
    )(own, *pieces)


CONTRACT_LAST = (((1,), (1,)), ((), ()))


def places(pos):
    for rel in range(2):
        core = pos[2] if rel == 0 else 1 - pos[2]
        for second in range(4):
            for first in range(4):
                yield ((rel * 4 + second) * 4 + first) * 16, block_at(pos, first, second, core, core)


def grad_inputs_kernel(pos, *refs):
    pieces, (weight, out, acc) = refs[:8], refs[8:]
    for half in range(2):
        lanes = slice(half * 3072, (half + 1) * 3072)
        cot = jnp.concatenate([ref[:, lanes] for ref in pieces])
        term = lax.dot_general(cot, weight[:, lanes], CONTRACT_LAST, preferred_element_type=F32)
        acc[...] = term if half == 0 else acc[...] + term
    for start, block in places(pos):
        out[token_rows(block), :] = acc[start : start + 16, :]


def grad_inputs_terms(pos, pieces, weight):
    return pl.pallas_call(
        grad_inputs_kernel,
        in_specs=[SMEM] + [VMEM] * 9,
        out_specs=VMEM,
        out_shape=jax.ShapeDtypeStruct((512, 384), F32),
        scratch_shapes=[pltpu.VMEM((512, 384), F32)],
        compiler_params=pltpu.CompilerParams(vmem_limit_bytes=28 * 2**20),
        cost_estimate=pl.CostEstimate(flops=2 * 512 * 384 * 6144, bytes_accessed=12 * 2**20, transcendentals=0),
        name="grad_inputs",
    )(pos, *pieces, weight)


def grad_weight_kernel(pos, acts, *refs):
    pieces, (out, lhs, slots, sems) = refs[:8], refs[8:]
    width = 1024
    for start, block in places(pos):
        lhs[start : start + 16, :] = acts[token_rows(block), :]
    copies = []
    for j in range(6):
        lanes = slice(j * width, (j + 1) * width)
        cot = jnp.concatenate([ref[:, lanes] for ref in pieces])
        slots[j] = lax.dot_general(
            lhs[...], cot, (((0,), (0,)), ((), ())), preferred_element_type=F32
        ).astype(BF)
        copies.append(pltpu.make_async_copy(slots.at[j], out.at[:, lanes], sems.at[j]))
        copies[j].start()
    for copy in copies:
        copy.wait()


def grad_weight_of(pos, acts, pieces):
    return pl.pallas_call(
        grad_weight_kernel,
        in_specs=[SMEM] + [VMEM] * 9,
        out_specs=HBM,
        out_shape=jax.ShapeDtypeStruct((384, 6144), BF),
        scratch_shapes=[
            pltpu.VMEM((512, 384), BF),
            pltpu.VMEM((6, 384, 1024), BF),
            pltpu.SemaphoreType.DMA((6,)),
        ],
        compiler_params=pltpu.CompilerParams(vmem_limit_bytes=28 * 2**20),
        cost_estimate=pl.CostEstimate(flops=2 * 512 * 384 * 6144, bytes_accessed=12 * 2**20, transcendentals=0),
        name="grad_weight",
    )(pos, acts, *pieces)


def body(inputs, weight, grad_out):
    core = lax.axis_index("core")
    pos = jnp.stack([lax.axis_index("x"), lax.axis_index("y"), core]).astype(jnp.int32)

    w_par = swap(weight)

    blocks = {0: grad_out}
    for d in STEPS:
        blocks[d] = get(grad_out, d, False)

    line = jnp.concatenate([blocks[d] for d in range(4)])

    gathered = lax.all_to_all(jnp.broadcast_to(inputs[None], (8, 64, 384)), "z", 0, 0).reshape(512, 384)
    gathered_par = swap(gathered)

    pieces = {0: line}
    for d in STEPS:
        pieces[d] = get(line, d, True)

    own, *sends = project(pos, gathered, gathered_par, weight, w_par)
    got = [get(v, 4 - d, False) for v, d in zip(sends, STEPS)]

    others = {0: swap(line)}
    late, _ = lax.optimization_barrier(({d: pieces[d] for d in STEPS}, own))
    for d in STEPS:
        pieces[d] = late[d]
        others[d] = swap(late[d])
    pieces = [pieces[d] for d in range(4)] + [others[d] for d in range(4)]
    terms = grad_inputs_terms(pos, pieces, weight)
    grad_weight = grad_weight_of(pos, gathered, pieces)
    terms, grad_weight = lax.optimization_barrier((terms, grad_weight))
    grad_inputs = lax.all_to_all(terms.reshape(8, 64, 384), "z", 0, 0).sum(axis=0).astype(BF)

    own, grad_weight = lax.optimization_barrier((own, grad_weight))
    own, *sends = relay(own, got)
    got = [get(v, 4 - d, True) for v, d in zip(sends, STEPS)]
    return finish(own, got), grad_inputs, grad_weight


def solution(mesh):
    fine = Mesh(mesh.devices.reshape(4, 4, 2, 8), ("x", "y", "core", "z"))
    placed = (P("z", ROWS), P(ROWS, "z"), P(ROWS, "z"))
    return jax.shard_map(
        body,
        mesh=fine,
        in_specs=placed,
        out_specs=(P(ROWS, "z"), P("z", ROWS), P(ROWS, "z")),
        check_vma=False,
    )
```

time: 92.3 us -> 89.3 us (0.967)
  Pallas kernels: 26.3 us -> 22.6 us
  local copies, waits for them, and re-layouts: 3.94 us -> 6.07 us
  starting transfers between devices: 36.7 us -> 34.7 us
  waiting for transfers between devices: 21.5 us -> 23.5 us
  other arithmetic: 2.61 us -> 1.26 us
    all_to_all x1, waiting for transfers between devices: 0.01 us -> 7.19 us  [body(): lax.all_to_all(terms.reshape(8, 64, 384), 'z', 0, 0).sum(axis=0).astype(BF)]
    pallas_call x4 -> x3, Pallas kernels: 18.2 us -> 14.6 us  [the longest x1 9.48 us: project(): pl.pallas_call(project_kernel, in_specs=[SMEM, VMEM, VMEM, HBM, HBM], out...]
    ppermute x7 -> x6, starting transfers between devices: 9.8 us -> 6.48 us  [swap(): return lax.ppermute(value, 'core', [(0, 1), (1, 0)])]
    ppermute x12, waiting for transfers between devices: 9.13 us -> 6.21 us  [get(): return lax.ppermute(value, ROWS, ring(distance, second))]
    ppermute x7 -> x6, waiting for transfers between devices: 2.62 us -> 1.2 us  [swap(): return lax.ppermute(value, 'core', [(0, 1), (1, 0)])]
    all_to_all x1, starting transfers between devices: 5.43 us -> 6.77 us  [body(): lax.all_to_all(terms.reshape(8, 64, 384), 'z', 0, 0).sum(axis=0).astype(BF)]
    unnamed x19 -> x17, local copies, waits for them, and re-layouts: 3.14 us -> 4.47 us
    reduce_sum x1, other arithmetic: 1.81 us -> 0.66 us  [body(): lax.all_to_all(terms.reshape(8, 64, 384), 'z', 0, 0).sum(axis=0).astype(BF)]
  transfers between devices with their start and end apart: 21 -> 20, of which waited for: 8 -> 8; matrix products, arithmetic and copies ran while one was open for 2% -> 4% of each run, Pallas kernels for 23% -> 25%
where the time goes in v3:
time: 89.3 us; the launch traced here: 88.9 us
  starting transfers between devices  34.7 us (39%)
  waiting for transfers between devices  23.5 us (26%)
  Pallas kernels  22.6 us (25%)
  local copies, waits for them, and re-layouts  6.07 us (7%)
  other arithmetic  1.26 us (1%)
    ppermute x12, starting transfers between devices, get(): return lax.ppermute(value, ROWS, ring(distance, second))  13.3 us
    pallas_call x1, Pallas kernels, project(): pl.pallas_call(project_kernel, in_specs=[SMEM, VMEM, VMEM, HBM, HBM], out...  9.48 us
    all_to_all x1, waiting for transfers between devices, body(): lax.all_to_all(jnp.broadcast_to(inputs[None], (8, 64, 384)), 'z', 0, 0)  8.87 us
    all_to_all x1, starting transfers between devices, body(): lax.all_to_all(jnp.broadcast_to(inputs[None], (8, 64, 384)), 'z', 0, 0)  8.19 us
    all_to_all x1, waiting for transfers between devices, body(): lax.all_to_all(terms.reshape(8, 64, 384), 'z', 0, 0).sum(axis=0).astype(BF)  7.19 us
    all_to_all x1, starting transfers between devices, body(): lax.all_to_all(terms.reshape(8, 64, 384), 'z', 0, 0).sum(axis=0).astype(BF)  6.77 us
    ppermute x6, starting transfers between devices, swap(): return lax.ppermute(value, 'core', [(0, 1), (1, 0)])  6.48 us
    ppermute x12, waiting for transfers between devices, get(): return lax.ppermute(value, ROWS, ring(distance, second))  6.21 us
  transfers between devices with their start and end apart: 20, of which 8 were waited for; matrix products, arithmetic and copies ran while one was open for 4% of the time, Pallas kernels for 25%

profile of v3, /device:TPU:1, one launch (start us, length us, event | category | flops | bytes accessed | tf_op | source)
XLA Modules:
  0.0 88.9 jit_solution(16775115646067965172)
XLA Ops:
  0.6 3.3 %collective-permute-start.1 = (bf16[384,6144]{1,0:T(8,128)(2,1)}, bf16[384,6144]{1,0:T(8,128)(2,1)}, u32[]{:S(2)}, u32[]{:S(2)}) collective-permute-start(bf16[384,6144]{1,0:T(8,128)(2,1)} %refs_8_.1), channel_id=1, source_target_pairs={{0,8},{8,0},{1,9},{9,1},{2,10},{10,2},{3,11},{11,3},{4,12},{12,4},... | collective-permute-start | bytes 14155784 | tf_op jit(solution)/shard_map/ppermute | solution.py:38
  4.0 1.0 %collective-permute-start.2 = (bf16[16,6144]{1,0:T(8,128)(2,1)}, bf16[16,6144]{1,0:T(8,128)(2,1)S(1)}, u32[]{:S(2)}, u32[]{:S(2)}) collective-permute-start(bf16[16,6144]{1,0:T(8,128)(2,1)} %param.5), channel_id=1, source_target_pairs={{64,0},{24,8},{80,16},{40,24},{96,32},{56,40},{112,48},{8,56},{128... | collective-permute-start | bytes 589832 | tf_op jit(solution)/shard_map/ppermute | solution.py:34
  5.3 0.7 collective-permute-start.4
  6.0 1.6 %broadcast_in_dim.2 = bf16[8,64,384]{2,1,0:T(8,128)(2,1)} broadcast(bf16[64,384]{1,0:T(8,128)(2,1)} %param.3), dimensions={1,2} | broadcast | bytes 442368 | tf_op jit(solution)/shard_map/broadcast_in_dim | solution.py:288
  7.6 8.2 %all-to-all-start = ((bf16[8,64,384]{2,1,0:T(8,128)(2,1)}), bf16[8,64,384]{2,1,0:T(8,128)(2,1)S(1)}, u32[]{:S(2)}, u32[]{:S(2)}) async-start(bf16[8,64,384]{2,1,0:T(8,128)(2,1)} %broadcast_in_dim.2), calls=%async_computation | async-start | bytes 786432 | tf_op jit(solution)/shard_map/all_to_all | solution.py:288
  15.8 0.9 %constant_dynamic-update-slice_fusion.3 = bf16[64,6144]{1,0:T(8,128)(2,1)S(1)} fusion(bf16[16,6144]{1,0:T(8,128)(2,1)} %param.5), kind=kLoop, calls=%fused_computation.3 | loop fusion | bytes 393216
  16.8 2.6 %collective-permute-start.5 = (bf16[64,6144]{1,0:T(8,128)(2,1)S(1)}, bf16[64,6144]{1,0:T(8,128)(2,1)S(1)}, u32[]{:S(2)}, u32[]{:S(2)}) collective-permute-start(bf16[64,6144]{1,0:T(8,128)(2,1)S(1)} %constant_dynamic-update-slice_fusion.refs_0_), channel_id=1, source_target_pairs={{16,0},{72,8},{32,16},{88,24},{48,32},{104,40},{0,48},{120,56},{80... | collective-permute-start | bytes 2359304 | tf_op jit(solution)/shard_map/ppermute | solution.py:34
  19.9 0.6 collective-permute-start.7
  20.5 8.9 %all-to-all-done = bf16[8,64,384]{2,1,0:T(8,128)(2,1)S(1)} async-done(((bf16[8,64,384]{2,1,0:T(8,128)(2,1)}), bf16[8,64,384]{2,1,0:T(8,128)(2,1)S(1)}, u32[]{:S(2)}, u32[]{:S(2)}) %all-to-all-start) | async-done | bytes 393248 | tf_op jit(solution)/shard_map/all_to_all | solution.py:288
  29.4 2.0 %collective-permute-start = (bf16[512,384]{1,0:T(8,128)(2,1)S(1)}, bf16[512,384]{1,0:T(8,128)(2,1)}, u32[]{:S(2)}, u32[]{:S(2)}) collective-permute-start(bf16[512,384]{1,0:T(8,128)(2,1)S(1)} %bitcast.7), channel_id=1, source_target_pairs={{0,8},{8,0},{1,9},{9,1},{2,10},{10,2},{3,11},{11,3},{4,12},{12,4},... | collective-permute-start | bytes 1179656 | tf_op jit(solution)/shard_map/ppermute | solution.py:38
  32.0 0.9 collective-permute-done.par_in
  33.3 9.5 %project.1 = (f32[3072,128]{1,0:T(8,128)}, bf16[3120,128]{1,0:T(8,128)(2,1)}, bf16[3120,128]{1,0:T(8,128)(2,1)}, bf16[3120,128]{1,0:T(8,128)(2,1)}) custom-call(s32[3]{0:T(128)} %pad_add_fusion.pos, bf16[512,384]{1,0:T(8,128)(2,1)} %bitcast.8, bf16[512,384]{1,0:T(8,128)(2,1)} %collective-permute-done.par_in, bf16[384,6144]{1,0:T(8,128)(2,1)} %refs_8_.1, ...), custom_call_target="tpu_custom_call" | custom-call | flops 2415919104 | bytes 10485760 | tf_op jit(solution)/shard_map/project/pallas_call | solution.py:123
  43.5 1.6 %collective-permute-start.12 = (bf16[3120,128]{1,0:T(8,128)(2,1)}, bf16[3120,128]{1,0:T(8,128)(2,1)}, u32[]{:S(2)}, u32[]{:S(2)}) collective-permute-start(bf16[3120,128]{1,0:T(8,128)(2,1)} %get-tuple-element.24), channel_id=1, source_target_pairs={{192,0},{56,8},{208,16},{8,24},{224,32},{24,40},{240,48},{40,56},{... | collective-permute-start | bytes 2396168 | tf_op jit(solution)/shard_map/ppermute | solution.py:34
  45.1 1.1 %collective-permute-start.13 = (bf16[3120,128]{1,0:T(8,128)(2,1)}, bf16[3120,128]{1,0:T(8,128)(2,1)}, u32[]{:S(2)}, u32[]{:S(2)}) collective-permute-start(bf16[3120,128]{1,0:T(8,128)(2,1)} %get-tuple-element.25), channel_id=1, source_target_pairs={{64,0},{24,8},{80,16},{40,24},{96,32},{56,40},{112,48},{8,56},{128... | collective-permute-start | bytes 2396168 | tf_op jit(solution)/shard_map/ppermute | solution.py:34
  46.2 0.9 collective-permute-start.14
  47.4 1.2 %copy-done.1 = bf16[8,64,384]{2,1,0:T(8,128)(2,1)S(1)} copy-done((bf16[8,64,384]{2,1,0:T(8,128)(2,1)S(1)}, bf16[8,64,384]{2,1,0:T(8,128)(2,1)}, u32[]{:S(2)}) %copy-start.1) | copy-done | bytes 393240
  48.6 4.3 %grad_weight.1 = bf16[384,6144]{1,0:T(8,128)(2,1)} custom-call(s32[3]{0:T(128)S(1)} %copy-done.3, bf16[512,384]{1,0:T(8,128)(2,1)S(1)} %bitcast.9, bf16[64,6144]{1,0:T(8,128)(2,1)S(1)} %constant_dynamic-update-slice_fusion.refs_0_, bf16[64,6144]{1,0:T(8,128)(2,1)S(1)} %collective-permute-done.5.refs_1_, bf16[64,6144]{1,0:T(8,128)(2,1)S(1)} %collective-permute-done.6.refs_2_, ...), custom_call_target="tpu_custom_call" | custom-call | flops 2415919104 | bytes 12582912 | tf_op jit(solution)/shard_map/grad_weight/pallas_call | solution.py:260
  53.0 4.0 %grad_inputs.1 = f32[512,384]{1,0:T(8,128)S(1)} custom-call(s32[3]{0:T(128)S(1)} %copy-done.3, bf16[64,6144]{1,0:T(8,128)(2,1)S(1)} %constant_dynamic-update-slice_fusion.refs_0_, bf16[64,6144]{1,0:T(8,128)(2,1)S(1)} %collective-permute-done.5.refs_1_, bf16[64,6144]{1,0:T(8,128)(2,1)S(1)} %collective-permute-done.6.refs_2_, ...), custom_call_target="tpu_custom_call" | custom-call | flops 2415919104 | bytes 12582912 | tf_op jit(solution)/shard_map/grad_inputs/pallas_call | solution.py:229
  57.0 0.9 copy-done.2
  57.9 6.8 %all-to-all-start.1 = ((f32[8,64,384]{2,1,0:T(8,128)}), f32[8,64,384]{2,1,0:T(8,128)S(1)}, u32[]{:S(2)}, u32[]{:S(2)}) async-start(f32[8,64,384]{2,1,0:T(8,128)} %bitcast.10), calls=%async_computation.1 | async-start | bytes 1572864 | tf_op jit(solution)/shard_map/all_to_all | solution.py:307
  64.6 0.7 collective-permute-done.14.in3
  65.4 1.4 %copy-done.4 = f32[3072,128]{1,0:T(8,128)S(1)} copy-done((f32[3072,128]{1,0:T(8,128)S(1)}, f32[3072,128]{1,0:T(8,128)}, u32[]{:S(2)}) %copy-start.4) | copy-done | bytes 1572888
  66.8 3.7 %relay.1 = (f32[768,128]{1,0:T(8,128)S(1)}, bf16[816,128]{1,0:T(8,128)(2,1)S(1)}, bf16[816,128]{1,0:T(8,128)(2,1)S(1)}, bf16[816,128]{1,0:T(8,128)(2,1)S(1)}) custom-call(f32[3072,128]{1,0:T(8,128)S(1)} %copy-done.4, bf16[3120,128]{1,0:T(8,128)(2,1)} %collective-permute-done.12.in1, bf16[3120,128]{1,0:T(8,128)(2,1)} %collective-permute-done.13.in2, ...), custom_call_target="tpu_custom_call" | custom-call | flops 8388608 | bytes 5242880 | tf_op jit(solution)/shard_map/relay/pallas_call | solution.py:168
  70.5 1.0 %collective-permute-start.15 = (bf16[816,128]{1,0:T(8,128)(2,1)S(1)}, bf16[816,128]{1,0:T(8,128)(2,1)S(1)}, u32[]{:S(2)}, u32[]{:S(2)}) collective-permute-start(bf16[816,128]{1,0:T(8,128)(2,1)S(1)} %get-tuple-element.28), channel_id=1, source_target_pairs={{48,0},{200,8},{0,16},{216,24},{16,32},{232,40},{32,48},{248,56},{... | collective-permute-start | bytes 626696 | tf_op jit(solution)/shard_map/ppermute | solution.py:34
  71.5 1.8 %collective-permute-start.16 = (bf16[816,128]{1,0:T(8,128)(2,1)S(1)}, bf16[816,128]{1,0:T(8,128)(2,1)S(1)}, u32[]{:S(2)}, u32[]{:S(2)}) collective-permute-start(bf16[816,128]{1,0:T(8,128)(2,1)S(1)} %get-tuple-element.29), channel_id=1, source_target_pairs={{16,0},{72,8},{32,16},{88,24},{48,32},{104,40},{0,48},{120,56},{80... | collective-permute-start | bytes 626696 | tf_op jit(solution)/shard_map/ppermute | solution.py:34
  73.2 1.2 %collective-permute-start.17 = (bf16[816,128]{1,0:T(8,128)(2,1)S(1)}, bf16[816,128]{1,0:T(8,128)(2,1)S(1)}, u32[]{:S(2)}, u32[]{:S(2)}) collective-permute-start(bf16[816,128]{1,0:T(8,128)(2,1)S(1)} %get-tuple-element.30), channel_id=1, source_target_pairs={{32,0},{136,8},{48,16},{152,24},{0,32},{168,40},{16,48},{184,56},{... | collective-permute-start | bytes 626696 | tf_op jit(solution)/shard_map/ppermute | solution.py:34
  74.5 2.2 %collective-permute-done.15.in1 = bf16[816,128]{1,0:T(8,128)(2,1)S(1)} collective-permute-done((bf16[816,128]{1,0:T(8,128)(2,1)S(1)}, bf16[816,128]{1,0:T(8,128)(2,1)S(1)}, u32[]{:S(2)}, u32[]{:S(2)}) %collective-permute-start.15) | collective-permute-done | bytes 208928 | tf_op jit(solution)/shard_map/ppermute | solution.py:34
  76.7 1.5 %collective-permute-done.16.in2 = bf16[816,128]{1,0:T(8,128)(2,1)S(1)} collective-permute-done((bf16[816,128]{1,0:T(8,128)(2,1)S(1)}, bf16[816,128]{1,0:T(8,128)(2,1)S(1)}, u32[]{:S(2)}, u32[]{:S(2)}) %collective-permute-start.16) | collective-permute-done | bytes 208928 | tf_op jit(solution)/shard_map/ppermute | solution.py:34
  78.2 1.7 %collective-permute-done.17.in3 = bf16[816,128]{1,0:T(8,128)(2,1)S(1)} collective-permute-done((bf16[816,128]{1,0:T(8,128)(2,1)S(1)}, bf16[816,128]{1,0:T(8,128)(2,1)S(1)}, u32[]{:S(2)}, u32[]{:S(2)}) %collective-permute-start.17) | collective-permute-done | bytes 208928 | tf_op jit(solution)/shard_map/ppermute | solution.py:34
  79.9 1.1 %finish.1 = bf16[16,6144]{1,0:T(8,128)(2,1)} custom-call(f32[768,128]{1,0:T(8,128)S(1)} %get-tuple-element.27.own, bf16[816,128]{1,0:T(8,128)(2,1)S(1)} %collective-permute-done.15.in1, bf16[816,128]{1,0:T(8,128)(2,1)S(1)} %collective-permute-done.16.in2, bf16[816,128]{1,0:T(8,128)(2,1)S(1)} %collective-permute-done.17.in3), custom_call_target="tpu_custom_call" | custom-call | flops 8589934592 | bytes 1048576 | tf_op jit(solution)/shard_map/finish/pallas_call | solution.py:195
  81.0 7.2 %all-to-all-done.1 = f32[8,64,384]{2,1,0:T(8,128)S(1)} async-done(((f32[8,64,384]{2,1,0:T(8,128)}), f32[8,64,384]{2,1,0:T(8,128)S(1)}, u32[]{:S(2)}, u32[]{:S(2)}) %all-to-all-start.1) | async-done | bytes 786464 | tf_op jit(solution)/shard_map/all_to_all | solution.py:307
  88.2 0.7 reduce_sum.9
  (35 shorter events, 3.0 us)
Async XLA Ops:
  0.6 32.6 %collective-permute-start.1 = (bf16[384,6144]{1,0:T(8,128)(2,1)}, bf16[384,6144]{1,0:T(8,128)(2,1)}, u32[]{:S(2)}, u32[]{:S(2)}) collective-permute-start(bf16[384,6144]{1,0:T(8,128)(2,1)} %refs_8_.1), channel_id=1, source_target_pairs={{0,8},{8,0},{1,9},{9,1},{2,10},{10,2},{3,11},{11,3},{4,12},{12,4},... | collective-permute-start | bytes 14155784 | tf_op jit(solution)/shard_map/ppermute | solution.py:38
  4.0 12.8 %collective-permute-start.2 = (bf16[16,6144]{1,0:T(8,128)(2,1)}, bf16[16,6144]{1,0:T(8,128)(2,1)S(1)}, u32[]{:S(2)}, u32[]{:S(2)}) collective-permute-start(bf16[16,6144]{1,0:T(8,128)(2,1)} %param.5), channel_id=1, source_target_pairs={{64,0},{24,8},{80,16},{40,24},{96,32},{56,40},{112,48},{8,56},{128... | collective-permute-start | bytes 589832 | tf_op jit(solution)/shard_map/ppermute | solution.py:34
  5.0 11.8 %collective-permute-start.3 = (bf16[16,6144]{1,0:T(8,128)(2,1)}, bf16[16,6144]{1,0:T(8,128)(2,1)S(1)}, u32[]{:S(2)}, u32[]{:S(2)}) collective-permute-start(bf16[16,6144]{1,0:T(8,128)(2,1)} %param.5), channel_id=1, source_target_pairs={{128,0},{40,8},{144,16},{56,24},{160,32},{8,40},{176,48},{24,56},{... | collective-permute-start | bytes 589832 | tf_op jit(solution)/shard_map/ppermute | solution.py:34
  5.3 11.5 %collective-permute-start.4 = (bf16[16,6144]{1,0:T(8,128)(2,1)}, bf16[16,6144]{1,0:T(8,128)(2,1)S(1)}, u32[]{:S(2)}, u32[]{:S(2)}) collective-permute-start(bf16[16,6144]{1,0:T(8,128)(2,1)} %param.5), channel_id=1, source_target_pairs={{192,0},{56,8},{208,16},{8,24},{224,32},{24,40},{240,48},{40,56},{... | collective-permute-start | bytes 589832 | tf_op jit(solution)/shard_map/ppermute | solution.py:34
  7.6 21.8 %all-to-all-start = ((bf16[8,64,384]{2,1,0:T(8,128)(2,1)}), bf16[8,64,384]{2,1,0:T(8,128)(2,1)S(1)}, u32[]{:S(2)}, u32[]{:S(2)}) async-start(bf16[8,64,384]{2,1,0:T(8,128)(2,1)} %broadcast_in_dim.2), calls=%async_computation | async-start | bytes 786432 | tf_op jit(solution)/shard_map/all_to_all | solution.py:288
  16.8 26.0 %collective-permute-start.5 = (bf16[64,6144]{1,0:T(8,128)(2,1)S(1)}, bf16[64,6144]{1,0:T(8,128)(2,1)S(1)}, u32[]{:S(2)}, u32[]{:S(2)}) collective-permute-start(bf16[64,6144]{1,0:T(8,128)(2,1)S(1)} %constant_dynamic-update-slice_fusion.refs_0_), channel_id=1, source_target_pairs={{16,0},{72,8},{32,16},{88,24},{48,32},{104,40},{0,48},{120,56},{80... | collective-permute-start | bytes 2359304 | tf_op jit(solution)/shard_map/ppermute | solution.py:34
  19.4 23.4 %collective-permute-start.6 = (bf16[64,6144]{1,0:T(8,128)(2,1)S(1)}, bf16[64,6144]{1,0:T(8,128)(2,1)S(1)}, u32[]{:S(2)}, u32[]{:S(2)}) collective-permute-start(bf16[64,6144]{1,0:T(8,128)(2,1)S(1)} %constant_dynamic-update-slice_fusion.refs_0_), channel_id=1, source_target_pairs={{32,0},{136,8},{48,16},{152,24},{0,32},{168,40},{16,48},{184,56},{... | collective-permute-start | bytes 2359304 | tf_op jit(solution)/shard_map/ppermute | solution.py:34
  19.9 22.9 %collective-permute-start.7 = (bf16[64,6144]{1,0:T(8,128)(2,1)S(1)}, bf16[64,6144]{1,0:T(8,128)(2,1)S(1)}, u32[]{:S(2)}, u32[]{:S(2)}) collective-permute-start(bf16[64,6144]{1,0:T(8,128)(2,1)S(1)} %constant_dynamic-update-slice_fusion.refs_0_), channel_id=1, source_target_pairs={{48,0},{200,8},{0,16},{216,24},{16,32},{232,40},{32,48},{248,56},{... | collective-permute-start | bytes 2359304 | tf_op jit(solution)/shard_map/ppermute | solution.py:34
  29.4 3.9 %copy-start = (bf16[8,64,384]{2,1,0:T(8,128)(2,1)}, bf16[8,64,384]{2,1,0:T(8,128)(2,1)S(1)}, u32[]{:S(2)}) copy-start(bf16[8,64,384]{2,1,0:T(8,128)(2,1)S(1)} %all-to-all-done) | copy-start | bytes 1179652
  29.4 3.5 %collective-permute-start = (bf16[512,384]{1,0:T(8,128)(2,1)S(1)}, bf16[512,384]{1,0:T(8,128)(2,1)}, u32[]{:S(2)}, u32[]{:S(2)}) collective-permute-start(bf16[512,384]{1,0:T(8,128)(2,1)S(1)} %bitcast.7), channel_id=1, source_target_pairs={{0,8},{8,0},{1,9},{9,1},{2,10},{10,2},{3,11},{11,3},{4,12},{12,4},... | collective-permute-start | bytes 1179656 | tf_op jit(solution)/shard_map/ppermute | solution.py:38
  32.0 15.4 %copy-start.3 = (s32[3]{0:T(128)S(1)}, s32[3]{0:T(128)}, u32[]{:S(2)}) copy-start(s32[3]{0:T(128)} %pad_add_fusion.pos) | copy-start | bytes 40
  32.9 12.2 %collective-permute-start.8 = (bf16[64,6144]{1,0:T(8,128)(2,1)S(1)}, bf16[64,6144]{1,0:T(8,128)(2,1)S(1)}, u32[]{:S(2)}, u32[]{:S(2)}) collective-permute-start(bf16[64,6144]{1,0:T(8,128)(2,1)S(1)} %constant_dynamic-update-slice_fusion.refs_0_), channel_id=1, source_target_pairs={{0,8},{8,0},{1,9},{9,1},{2,10},{10,2},{3,11},{11,3},{4,12},{12,4},... | collective-permute-start | bytes 2359304 | tf_op jit(solution)/shard_map/ppermute | solution.py:38
  42.8 3.4 %collective-permute-start.10 = (bf16[64,6144]{1,0:T(8,128)(2,1)S(1)}, bf16[64,6144]{1,0:T(8,128)(2,1)S(1)}, u32[]{:S(2)}, u32[]{:S(2)}) collective-permute-start(bf16[64,6144]{1,0:T(8,128)(2,1)S(1)} %collective-permute-done.6.refs_2_), channel_id=1, source_target_pairs={{0,8},{8,0},{1,9},{9,1},{2,10},{10,2},{3,11},{11,3},{4,12},{12,4},... | collective-permute-start | bytes 2359304 | tf_op jit(solution)/shard_map/ppermute | solution.py:38
  43.0 4.1 %collective-permute-start.11 = (bf16[64,6144]{1,0:T(8,128)(2,1)S(1)}, bf16[64,6144]{1,0:T(8,128)(2,1)S(1)}, u32[]{:S(2)}, u32[]{:S(2)}) collective-permute-start(bf16[64,6144]{1,0:T(8,128)(2,1)S(1)} %collective-permute-done.7.refs_3_), channel_id=1, source_target_pairs={{0,8},{8,0},{1,9},{9,1},{2,10},{10,2},{3,11},{11,3},{4,12},{12,4},... | collective-permute-start | bytes 2359304 | tf_op jit(solution)/shard_map/ppermute | solution.py:38
  43.4 4.0 %collective-permute-start.9 = (bf16[64,6144]{1,0:T(8,128)(2,1)S(1)}, bf16[64,6144]{1,0:T(8,128)(2,1)S(1)}, u32[]{:S(2)}, u32[]{:S(2)}) collective-permute-start(bf16[64,6144]{1,0:T(8,128)(2,1)S(1)} %collective-permute-done.5.refs_1_), channel_id=1, source_target_pairs={{0,8},{8,0},{1,9},{9,1},{2,10},{10,2},{3,11},{11,3},{4,12},{12,4},... | collective-permute-start | bytes 2359304 | tf_op jit(solution)/shard_map/ppermute | solution.py:38
  43.5 21.1 %collective-permute-start.12 = (bf16[3120,128]{1,0:T(8,128)(2,1)}, bf16[3120,128]{1,0:T(8,128)(2,1)}, u32[]{:S(2)}, u32[]{:S(2)}) collective-permute-start(bf16[3120,128]{1,0:T(8,128)(2,1)} %get-tuple-element.24), channel_id=1, source_target_pairs={{192,0},{56,8},{208,16},{8,24},{224,32},{24,40},{240,48},{40,56},{... | collective-permute-start | bytes 2396168 | tf_op jit(solution)/shard_map/ppermute | solution.py:34
  45.1 19.5 %collective-permute-start.13 = (bf16[3120,128]{1,0:T(8,128)(2,1)}, bf16[3120,128]{1,0:T(8,128)(2,1)}, u32[]{:S(2)}, u32[]{:S(2)}) collective-permute-start(bf16[3120,128]{1,0:T(8,128)(2,1)} %get-tuple-element.25), channel_id=1, source_target_pairs={{64,0},{24,8},{80,16},{40,24},{96,32},{56,40},{112,48},{8,56},{128... | collective-permute-start | bytes 2396168 | tf_op jit(solution)/shard_map/ppermute | solution.py:34
  46.2 6.7 %slice-start = ((s8[4718592]{0:T(1024)(128)(4,1)}), s8[4194304]{0:T(1024)(128)(4,1)S(1)}, s32[]{:S(2)}) async-start(s8[4718592]{0:T(1024)(128)(4,1)} %bitcast.5), calls=%async_computation.2 | async-start | bytes 8388608
  46.2 6.7 %slice-start.1 = ((s8[4718592]{0:T(1024)(128)(4,1)}), s8[524288]{0:T(1024)(128)(4,1)S(1)}, s32[]{:S(2)}) async-start(s8[4718592]{0:T(1024)(128)(4,1)} %bitcast.5), calls=%async_computation.3 | async-start | bytes 1048576
  46.2 19.2 %collective-permute-start.14 = (bf16[3120,128]{1,0:T(8,128)(2,1)}, bf16[3120,128]{1,0:T(8,128)(2,1)}, u32[]{:S(2)}, u32[]{:S(2)}) collective-permute-start(bf16[3120,128]{1,0:T(8,128)(2,1)} %get-tuple-element.26), channel_id=1, source_target_pairs={{128,0},{40,8},{144,16},{56,24},{160,32},{8,40},{176,48},{24,56},{... | collective-permute-start | bytes 2396168 | tf_op jit(solution)/shard_map/ppermute | solution.py:34
  47.4 1.2 %copy-start.1 = (bf16[8,64,384]{2,1,0:T(8,128)(2,1)S(1)}, bf16[8,64,384]{2,1,0:T(8,128)(2,1)}, u32[]{:S(2)}) copy-start(bf16[8,64,384]{2,1,0:T(8,128)(2,1)} %copy-done) | copy-start | bytes 1179652
  57.0 0.9 copy-start.2
  57.9 30.3 %all-to-all-start.1 = ((f32[8,64,384]{2,1,0:T(8,128)}), f32[8,64,384]{2,1,0:T(8,128)S(1)}, u32[]{:S(2)}, u32[]{:S(2)}) async-start(f32[8,64,384]{2,1,0:T(8,128)} %bitcast.10), calls=%async_computation.1 | async-start | bytes 1572864 | tf_op jit(solution)/shard_map/all_to_all | solution.py:307
  65.4 1.4 %copy-start.4 = (f32[3072,128]{1,0:T(8,128)S(1)}, f32[3072,128]{1,0:T(8,128)}, u32[]{:S(2)}) copy-start(f32[3072,128]{1,0:T(8,128)} %get-tuple-element.23.own_in) | copy-start | bytes 4718596
  70.5 6.2 %collective-permute-start.15 = (bf16[816,128]{1,0:T(8,128)(2,1)S(1)}, bf16[816,128]{1,0:T(8,128)(2,1)S(1)}, u32[]{:S(2)}, u32[]{:S(2)}) collective-permute-start(bf16[816,128]{1,0:T(8,128)(2,1)S(1)} %get-tuple-element.28), channel_id=1, source_target_pairs={{48,0},{200,8},{0,16},{216,24},{16,32},{232,40},{32,48},{248,56},{... | collective-permute-start | bytes 626696 | tf_op jit(solution)/shard_map/ppermute | solution.py:34
  71.5 6.7 %collective-permute-start.16 = (bf16[816,128]{1,0:T(8,128)(2,1)S(1)}, bf16[816,128]{1,0:T(8,128)(2,1)S(1)}, u32[]{:S(2)}, u32[]{:S(2)}) collective-permute-start(bf16[816,128]{1,0:T(8,128)(2,1)S(1)} %get-tuple-element.29), channel_id=1, source_target_pairs={{16,0},{72,8},{32,16},{88,24},{48,32},{104,40},{0,48},{120,56},{80... | collective-permute-start | bytes 626696 | tf_op jit(solution)/shard_map/ppermute | solution.py:34
  73.2 6.7 %collective-permute-start.17 = (bf16[816,128]{1,0:T(8,128)(2,1)S(1)}, bf16[816,128]{1,0:T(8,128)(2,1)S(1)}, u32[]{:S(2)}, u32[]{:S(2)}) collective-permute-start(bf16[816,128]{1,0:T(8,128)(2,1)S(1)} %get-tuple-element.30), channel_id=1, source_target_pairs={{32,0},{136,8},{48,16},{152,24},{0,32},{168,40},{16,48},{184,56},{... | collective-permute-start | bytes 626696 | tf_op jit(solution)/shard_map/ppermute | solution.py:34

commit v4 on v3

--- a/solution.py
+++ b/solution.py
@@ -198,7 +198,7 @@
         out_specs=VMEM,
         out_shape=jax.ShapeDtypeStruct((16, 6144), BF),
         compiler_params=pltpu.CompilerParams(vmem_limit_bytes=16 * 2**20),
-        cost_estimate=pl.CostEstimate(flops=2**33, bytes_accessed=2**20, transcendentals=2**18),
+        cost_estimate=pl.CostEstimate(flops=2**32, bytes_accessed=2**20, transcendentals=2**18),
         name="finish",
     )(own, *pieces)
 
@@ -302,12 +302,11 @@
         others[d] = swap(late[d])
     pieces = [pieces[d] for d in range(4)] + [others[d] for d in range(4)]
     terms = grad_inputs_terms(pos, pieces, weight)
+    grad_inputs = lax.all_to_all(terms.reshape(8, 64, 384), "z", 0, 0).sum(axis=0).astype(BF)
+
+    own, *sends = relay(own, got)
+    pieces, own = lax.optimization_barrier((pieces, own))
     grad_weight = grad_weight_of(pos, gathered, pieces)
-    terms, grad_weight = lax.optimization_barrier((terms, grad_weight))
-    grad_inputs = lax.all_to_all(terms.reshape(8, 64, 384), "z", 0, 0).sum(axis=0).astype(BF)
-
-    own, grad_weight = lax.optimization_barrier((own, grad_weight))
-    own, *sends = relay(own, got)
     got = [get(v, 4 - d, True) for v, d in zip(sends, STEPS)]
     return finish(own, got), grad_inputs, grad_weight
 

time: 89.3 us -> 86.8 us (0.972)
  waiting for transfers between devices: 23.5 us -> 15.5 us
  local copies, waits for them, and re-layouts: 6.07 us -> 8.28 us
  Pallas kernels: 22.6 us -> 24 us
  other arithmetic: 1.26 us -> 2.4 us
    all_to_all x1, waiting for transfers between devices: 7.19 us -> 0.01 us  [body(): lax.all_to_all(terms.reshape(8, 64, 384), 'z', 0, 0).sum(axis=0).astype(BF)]
    unnamed x17 -> x29, local copies, waits for them, and re-layouts: 4.47 us -> 6.68 us
    reduce_sum x1, other arithmetic: 0.66 us -> 1.81 us  [body(): lax.all_to_all(terms.reshape(8, 64, 384), 'z', 0, 0).sum(axis=0).astype(BF)]
  transfers between devices with their start and end apart: 20 -> 20, of which waited for: 8 -> 4; matrix products, arithmetic and copies ran while one was open for 4% -> 4% of each run, Pallas kernels for 25% -> 28%
where the time goes in v4:
time: 86.8 us; the launch traced here: 85.7 us
  starting transfers between devices  34.6 us (40%)
  Pallas kernels  24 us (28%)
  waiting for transfers between devices  15.5 us (18%)
  local copies, waits for them, and re-layouts  8.28 us (10%)
  other arithmetic  2.4 us (3%)
    ppermute x12, starting transfers between devices, get(): return lax.ppermute(value, ROWS, ring(distance, second))  13.3 us
    pallas_call x1, Pallas kernels, project(): pl.pallas_call(project_kernel, in_specs=[SMEM, VMEM, VMEM, HBM, HBM], out...  9.45 us
    all_to_all x1, waiting for transfers between devices, body(): lax.all_to_all(jnp.broadcast_to(inputs[None], (8, 64, 384)), 'z', 0, 0)  8.87 us
    all_to_all x1, starting transfers between devices, body(): lax.all_to_all(jnp.broadcast_to(inputs[None], (8, 64, 384)), 'z', 0, 0)  8.19 us
    all_to_all x1, starting transfers between devices, body(): lax.all_to_all(terms.reshape(8, 64, 384), 'z', 0, 0).sum(axis=0).astype(BF)  6.69 us
    unnamed x29, local copies, waits for them, and re-layouts  6.68 us
    ppermute x6, starting transfers between devices, swap(): return lax.ppermute(value, 'core', [(0, 1), (1, 0)])  6.48 us
    ppermute x12, waiting for transfers between devices, get(): return lax.ppermute(value, ROWS, ring(distance, second))  5.43 us
  transfers between devices with their start and end apart: 20, of which 4 were waited for; matrix products, arithmetic and copies ran while one was open for 4% of the time, Pallas kernels for 28%

profile of v4, /device:TPU:1, one launch (start us, length us, event | category | flops | bytes accessed | tf_op | source)
XLA Modules:
  0.0 85.7 jit_solution(9512800020153340896)
XLA Ops:
  0.6 3.3 %collective-permute-start.7 = (bf16[384,6144]{1,0:T(8,128)(2,1)}, bf16[384,6144]{1,0:T(8,128)(2,1)}, u32[]{:S(2)}, u32[]{:S(2)}) collective-permute-start(bf16[384,6144]{1,0:T(8,128)(2,1)} %refs_8_.1), channel_id=1, source_target_pairs={{0,8},{8,0},{1,9},{9,1},{2,10},{10,2},{3,11},{11,3},{4,12},{12,4},... | collective-permute-start | bytes 14155784 | tf_op jit(solution)/shard_map/ppermute | solution.py:38
  4.0 1.0 %collective-permute-start = (bf16[16,6144]{1,0:T(8,128)(2,1)}, bf16[16,6144]{1,0:T(8,128)(2,1)S(1)}, u32[]{:S(2)}, u32[]{:S(2)}) collective-permute-start(bf16[16,6144]{1,0:T(8,128)(2,1)} %param.5), channel_id=1, source_target_pairs={{64,0},{24,8},{80,16},{40,24},{96,32},{56,40},{112,48},{8,56},{128... | collective-permute-start | bytes 589832 | tf_op jit(solution)/shard_map/ppermute | solution.py:34
  5.3 0.7 collective-permute-start.2
  6.0 1.6 %broadcast_in_dim.2 = bf16[8,64,384]{2,1,0:T(8,128)(2,1)} broadcast(bf16[64,384]{1,0:T(8,128)(2,1)} %param.3), dimensions={1,2} | broadcast | bytes 442368 | tf_op jit(solution)/shard_map/broadcast_in_dim | solution.py:288
  7.6 8.2 %all-to-all-start = ((bf16[8,64,384]{2,1,0:T(8,128)(2,1)}), bf16[8,64,384]{2,1,0:T(8,128)(2,1)S(1)}, u32[]{:S(2)}, u32[]{:S(2)}) async-start(bf16[8,64,384]{2,1,0:T(8,128)(2,1)} %broadcast_in_dim.2), calls=%async_computation | async-start | bytes 786432 | tf_op jit(solution)/shard_map/all_to_all | solution.py:288
  15.8 0.9 %constant_dynamic-update-slice_fusion.3 = bf16[64,6144]{1,0:T(8,128)(2,1)S(1)} fusion(bf16[16,6144]{1,0:T(8,128)(2,1)} %param.5), kind=kLoop, calls=%fused_computation.3 | loop fusion | bytes 393216
  16.8 2.6 %collective-permute-start.3 = (bf16[64,6144]{1,0:T(8,128)(2,1)S(1)}, bf16[64,6144]{1,0:T(8,128)(2,1)S(1)}, u32[]{:S(2)}, u32[]{:S(2)}) collective-permute-start(bf16[64,6144]{1,0:T(8,128)(2,1)S(1)} %constant_dynamic-update-slice_fusion.refs_0_), channel_id=1, source_target_pairs={{16,0},{72,8},{32,16},{88,24},{48,32},{104,40},{0,48},{120,56},{80... | collective-permute-start | bytes 2359304 | tf_op jit(solution)/shard_map/ppermute | solution.py:34
  19.4 0.5 collective-permute-start.4
  19.9 0.6 collective-permute-start.5
  20.5 8.9 %all-to-all-done = bf16[8,64,384]{2,1,0:T(8,128)(2,1)S(1)} async-done(((bf16[8,64,384]{2,1,0:T(8,128)(2,1)}), bf16[8,64,384]{2,1,0:T(8,128)(2,1)S(1)}, u32[]{:S(2)}, u32[]{:S(2)}) %all-to-all-start) | async-done | bytes 393248 | tf_op jit(solution)/shard_map/all_to_all | solution.py:288
  29.4 2.0 %collective-permute-start.6 = (bf16[512,384]{1,0:T(8,128)(2,1)S(1)}, bf16[512,384]{1,0:T(8,128)(2,1)}, u32[]{:S(2)}, u32[]{:S(2)}) collective-permute-start(bf16[512,384]{1,0:T(8,128)(2,1)S(1)} %bitcast.7), channel_id=1, source_target_pairs={{0,8},{8,0},{1,9},{9,1},{2,10},{10,2},{3,11},{11,3},{4,12},{12,4},... | collective-permute-start | bytes 1179656 | tf_op jit(solution)/shard_map/ppermute | solution.py:38
  31.4 0.6 pad_add_fusion.pos
  32.0 0.9 %collective-permute-done.6.par_in = bf16[512,384]{1,0:T(8,128)(2,1)} collective-permute-done((bf16[512,384]{1,0:T(8,128)(2,1)S(1)}, bf16[512,384]{1,0:T(8,128)(2,1)}, u32[]{:S(2)}, u32[]{:S(2)}) %collective-permute-start.6) | collective-permute-done | bytes 393248 | tf_op jit(solution)/shard_map/ppermute | solution.py:38
  33.3 9.5 %project.1 = (f32[3072,128]{1,0:T(8,128)}, bf16[3120,128]{1,0:T(8,128)(2,1)}, bf16[3120,128]{1,0:T(8,128)(2,1)}, bf16[3120,128]{1,0:T(8,128)(2,1)}) custom-call(s32[3]{0:T(128)} %pad_add_fusion.pos, bf16[512,384]{1,0:T(8,128)(2,1)} %bitcast.8, bf16[512,384]{1,0:T(8,128)(2,1)} %collective-permute-done.6.par_in, bf16[384,6144]{1,0:T(8,128)(2,1)} %refs_8_.1, ...), custom_call_target="tpu_custom_call" | custom-call | flops 2415919104 | bytes 10485760 | tf_op jit(solution)/shard_map/project/pallas_call | solution.py:123
  43.5 1.6 %collective-permute-start.12 = (bf16[3120,128]{1,0:T(8,128)(2,1)}, bf16[3120,128]{1,0:T(8,128)(2,1)}, u32[]{:S(2)}, u32[]{:S(2)}) collective-permute-start(bf16[3120,128]{1,0:T(8,128)(2,1)} %get-tuple-element.27), channel_id=1, source_target_pairs={{192,0},{56,8},{208,16},{8,24},{224,32},{24,40},{240,48},{40,56},{... | collective-permute-start | bytes 2396168 | tf_op jit(solution)/shard_map/ppermute | solution.py:34
  45.1 1.1 %collective-permute-start.13 = (bf16[3120,128]{1,0:T(8,128)(2,1)}, bf16[3120,128]{1,0:T(8,128)(2,1)}, u32[]{:S(2)}, u32[]{:S(2)}) collective-permute-start(bf16[3120,128]{1,0:T(8,128)(2,1)} %get-tuple-element.28), channel_id=1, source_target_pairs={{64,0},{24,8},{80,16},{40,24},{96,32},{56,40},{112,48},{8,56},{128... | collective-permute-start | bytes 2396168 | tf_op jit(solution)/shard_map/ppermute | solution.py:34
  46.2 0.9 %collective-permute-start.14 = (bf16[3120,128]{1,0:T(8,128)(2,1)}, bf16[3120,128]{1,0:T(8,128)(2,1)}, u32[]{:S(2)}, u32[]{:S(2)}) collective-permute-start(bf16[3120,128]{1,0:T(8,128)(2,1)} %get-tuple-element.29), channel_id=1, source_target_pairs={{128,0},{40,8},{144,16},{56,24},{160,32},{8,40},{176,48},{24,56},{... | collective-permute-start | bytes 2396168 | tf_op jit(solution)/shard_map/ppermute | solution.py:34
  47.4 4.9 %grad_inputs.1 = f32[512,384]{1,0:T(8,128)S(1)} custom-call(s32[3]{0:T(128)S(1)} %copy-done.9, bf16[64,6144]{1,0:T(8,128)(2,1)S(1)} %constant_dynamic-update-slice_fusion.refs_0_, bf16[64,6144]{1,0:T(8,128)(2,1)S(1)} %collective-permute-done.3.refs_1_, bf16[64,6144]{1,0:T(8,128)(2,1)S(1)} %collective-permute-done.4.refs_2_, ...), custom_call_target="tpu_custom_call" | custom-call | flops 2415919104 | bytes 12582912 | tf_op jit(solution)/shard_map/grad_inputs/pallas_call | solution.py:229
  52.4 0.9 %copy-done.8 = f32[512,384]{1,0:T(8,128)} copy-done((f32[512,384]{1,0:T(8,128)}, f32[512,384]{1,0:T(8,128)S(1)}, u32[]{:S(2)}) %copy-start.8) | copy-done | bytes 786456
  53.2 6.7 %all-to-all-start.1 = ((f32[8,64,384]{2,1,0:T(8,128)}), f32[8,64,384]{2,1,0:T(8,128)}, u32[]{:S(2)}, u32[]{:S(2)}) async-start(f32[8,64,384]{2,1,0:T(8,128)} %bitcast.10), calls=%async_computation.1 | async-start | bytes 1572864 | tf_op jit(solution)/shard_map/all_to_all | solution.py:305
  59.9 5.4 %collective-permute-done.14.in3 = bf16[3120,128]{1,0:T(8,128)(2,1)} collective-permute-done((bf16[3120,128]{1,0:T(8,128)(2,1)}, bf16[3120,128]{1,0:T(8,128)(2,1)}, u32[]{:S(2)}, u32[]{:S(2)}) %collective-permute-start.14) | collective-permute-done | bytes 798752 | tf_op jit(solution)/shard_map/ppermute | solution.py:34
  65.3 1.4 %copy-done.10 = f32[3072,128]{1,0:T(8,128)S(1)} copy-done((f32[3072,128]{1,0:T(8,128)S(1)}, f32[3072,128]{1,0:T(8,128)}, u32[]{:S(2)}) %copy-start.10) | copy-done | bytes 1572888
  66.8 3.7 %relay.1 = (f32[768,128]{1,0:T(8,128)S(1)}, bf16[816,128]{1,0:T(8,128)(2,1)S(1)}, bf16[816,128]{1,0:T(8,128)(2,1)S(1)}, bf16[816,128]{1,0:T(8,128)(2,1)S(1)}) custom-call(f32[3072,128]{1,0:T(8,128)S(1)} %copy-done.10, bf16[3120,128]{1,0:T(8,128)(2,1)} %collective-permute-done.12.in1, bf16[3120,128]{1,0:T(8,128)(2,1)} %collective-permute-done.13.in2, ...), custom_call_target="tpu_custom_call" | custom-call | flops 8388608 | bytes 5242880 | tf_op jit(solution)/shard_map/relay/pallas_call | solution.py:168
  70.5 1.0 %collective-permute-start.15 = (bf16[816,128]{1,0:T(8,128)(2,1)S(1)}, bf16[816,128]{1,0:T(8,128)(2,1)S(1)}, u32[]{:S(2)}, u32[]{:S(2)}) collective-permute-start(bf16[816,128]{1,0:T(8,128)(2,1)S(1)} %get-tuple-element.32), channel_id=1, source_target_pairs={{48,0},{200,8},{0,16},{216,24},{16,32},{232,40},{32,48},{248,56},{... | collective-permute-start | bytes 626696 | tf_op jit(solution)/shard_map/ppermute | solution.py:34
  71.5 1.8 %collective-permute-start.16 = (bf16[816,128]{1,0:T(8,128)(2,1)S(1)}, bf16[816,128]{1,0:T(8,128)(2,1)S(1)}, u32[]{:S(2)}, u32[]{:S(2)}) collective-permute-start(bf16[816,128]{1,0:T(8,128)(2,1)S(1)} %get-tuple-element.33), channel_id=1, source_target_pairs={{16,0},{72,8},{32,16},{88,24},{48,32},{104,40},{0,48},{120,56},{80... | collective-permute-start | bytes 626696 | tf_op jit(solution)/shard_map/ppermute | solution.py:34
  73.2 1.2 %collective-permute-start.17 = (bf16[816,128]{1,0:T(8,128)(2,1)S(1)}, bf16[816,128]{1,0:T(8,128)(2,1)S(1)}, u32[]{:S(2)}, u32[]{:S(2)}) collective-permute-start(bf16[816,128]{1,0:T(8,128)(2,1)S(1)} %get-tuple-element.34), channel_id=1, source_target_pairs={{32,0},{136,8},{48,16},{152,24},{0,32},{168,40},{16,48},{184,56},{... | collective-permute-start | bytes 626696 | tf_op jit(solution)/shard_map/ppermute | solution.py:34
  74.5 1.1 %copy-done.3 = bf16[64,6144]{1,0:T(8,128)(2,1)S(1)} copy-done((bf16[64,6144]{1,0:T(8,128)(2,1)S(1)}, bf16[64,6144]{1,0:T(8,128)(2,1)}, u32[]{:S(2)}) %copy-start.3) | copy-done | bytes 786456
  75.6 1.1 %copy-done.5 = bf16[64,6144]{1,0:T(8,128)(2,1)S(1)} copy-done((bf16[64,6144]{1,0:T(8,128)(2,1)S(1)}, bf16[64,6144]{1,0:T(8,128)(2,1)}, u32[]{:S(2)}) %copy-start.5) | copy-done | bytes 786456
  76.7 1.1 %copy-done.7 = bf16[64,6144]{1,0:T(8,128)(2,1)S(1)} copy-done((bf16[64,6144]{1,0:T(8,128)(2,1)S(1)}, bf16[64,6144]{1,0:T(8,128)(2,1)}, u32[]{:S(2)}) %copy-start.7) | copy-done | bytes 786456
  77.9 4.9 %grad_weight.1 = bf16[384,6144]{1,0:T(8,128)(2,1)} custom-call(s32[3]{0:T(128)S(1)} %copy-done.9, bf16[512,384]{1,0:T(8,128)(2,1)S(1)} %bitcast.9, bf16[64,6144]{1,0:T(8,128)(2,1)S(1)} %constant_dynamic-update-slice_fusion.refs_0_, bf16[64,6144]{1,0:T(8,128)(2,1)S(1)} %collective-permute-done.3.refs_1_, bf16[64,6144]{1,0:T(8,128)(2,1)S(1)} %collective-permute-done.4.refs_2_, ...), custom_call_target="tpu_custom_call" | custom-call | flops 2415919104 | bytes 12582912 | tf_op jit(solution)/shard_map/grad_weight/pallas_call | solution.py:260
  82.8 1.1 %finish.1 = bf16[16,6144]{1,0:T(8,128)(2,1)} custom-call(f32[768,128]{1,0:T(8,128)S(1)} %get-tuple-element.31.own, bf16[816,128]{1,0:T(8,128)(2,1)S(1)} %collective-permute-done.15.in1, bf16[816,128]{1,0:T(8,128)(2,1)S(1)} %collective-permute-done.16.in2, bf16[816,128]{1,0:T(8,128)(2,1)S(1)} %collective-permute-done.17.in3), custom_call_target="tpu_custom_call" | custom-call | flops 4294967296 | bytes 1048576 | tf_op jit(solution)/shard_map/finish/pallas_call | solution.py:195
  83.9 1.8 %reduce_sum.9 = bf16[64,384]{1,0:T(8,128)(2,1)} reduce(f32[8,64,384]{2,1,0:T(8,128)} %all-to-all-done.1, f32[]{:T(128)} %constant.16.clone.1), dimensions={0}, to_apply=%region_0.0 | reduce | flops 172032 | bytes 835588 | tf_op jit(solution)/shard_map/reduce_sum | solution.py:305
  (47 shorter events, 1.9 us)
Async XLA Ops:
  0.6 32.6 %collective-permute-start.7 = (bf16[384,6144]{1,0:T(8,128)(2,1)}, bf16[384,6144]{1,0:T(8,128)(2,1)}, u32[]{:S(2)}, u32[]{:S(2)}) collective-permute-start(bf16[384,6144]{1,0:T(8,128)(2,1)} %refs_8_.1), channel_id=1, source_target_pairs={{0,8},{8,0},{1,9},{9,1},{2,10},{10,2},{3,11},{11,3},{4,12},{12,4},... | collective-permute-start | bytes 14155784 | tf_op jit(solution)/shard_map/ppermute | solution.py:38
  4.0 12.8 %collective-permute-start = (bf16[16,6144]{1,0:T(8,128)(2,1)}, bf16[16,6144]{1,0:T(8,128)(2,1)S(1)}, u32[]{:S(2)}, u32[]{:S(2)}) collective-permute-start(bf16[16,6144]{1,0:T(8,128)(2,1)} %param.5), channel_id=1, source_target_pairs={{64,0},{24,8},{80,16},{40,24},{96,32},{56,40},{112,48},{8,56},{128... | collective-permute-start | bytes 589832 | tf_op jit(solution)/shard_map/ppermute | solution.py:34
  5.0 11.8 %collective-permute-start.1 = (bf16[16,6144]{1,0:T(8,128)(2,1)}, bf16[16,6144]{1,0:T(8,128)(2,1)S(1)}, u32[]{:S(2)}, u32[]{:S(2)}) collective-permute-start(bf16[16,6144]{1,0:T(8,128)(2,1)} %param.5), channel_id=1, source_target_pairs={{128,0},{40,8},{144,16},{56,24},{160,32},{8,40},{176,48},{24,56},{... | collective-permute-start | bytes 589832 | tf_op jit(solution)/shard_map/ppermute | solution.py:34
  5.3 11.5 %collective-permute-start.2 = (bf16[16,6144]{1,0:T(8,128)(2,1)}, bf16[16,6144]{1,0:T(8,128)(2,1)S(1)}, u32[]{:S(2)}, u32[]{:S(2)}) collective-permute-start(bf16[16,6144]{1,0:T(8,128)(2,1)} %param.5), channel_id=1, source_target_pairs={{192,0},{56,8},{208,16},{8,24},{224,32},{24,40},{240,48},{40,56},{... | collective-permute-start | bytes 589832 | tf_op jit(solution)/shard_map/ppermute | solution.py:34
  7.6 21.8 %all-to-all-start = ((bf16[8,64,384]{2,1,0:T(8,128)(2,1)}), bf16[8,64,384]{2,1,0:T(8,128)(2,1)S(1)}, u32[]{:S(2)}, u32[]{:S(2)}) async-start(bf16[8,64,384]{2,1,0:T(8,128)(2,1)} %broadcast_in_dim.2), calls=%async_computation | async-start | bytes 786432 | tf_op jit(solution)/shard_map/all_to_all | solution.py:288
  16.8 25.9 %collective-permute-start.3 = (bf16[64,6144]{1,0:T(8,128)(2,1)S(1)}, bf16[64,6144]{1,0:T(8,128)(2,1)S(1)}, u32[]{:S(2)}, u32[]{:S(2)}) collective-permute-start(bf16[64,6144]{1,0:T(8,128)(2,1)S(1)} %constant_dynamic-update-slice_fusion.refs_0_), channel_id=1, source_target_pairs={{16,0},{72,8},{32,16},{88,24},{48,32},{104,40},{0,48},{120,56},{80... | collective-permute-start | bytes 2359304 | tf_op jit(solution)/shard_map/ppermute | solution.py:34
  19.4 23.4 %collective-permute-start.4 = (bf16[64,6144]{1,0:T(8,128)(2,1)S(1)}, bf16[64,6144]{1,0:T(8,128)(2,1)S(1)}, u32[]{:S(2)}, u32[]{:S(2)}) collective-permute-start(bf16[64,6144]{1,0:T(8,128)(2,1)S(1)} %constant_dynamic-update-slice_fusion.refs_0_), channel_id=1, source_target_pairs={{32,0},{136,8},{48,16},{152,24},{0,32},{168,40},{16,48},{184,56},{... | collective-permute-start | bytes 2359304 | tf_op jit(solution)/shard_map/ppermute | solution.py:34
  19.9 22.9 %collective-permute-start.5 = (bf16[64,6144]{1,0:T(8,128)(2,1)S(1)}, bf16[64,6144]{1,0:T(8,128)(2,1)S(1)}, u32[]{:S(2)}, u32[]{:S(2)}) collective-permute-start(bf16[64,6144]{1,0:T(8,128)(2,1)S(1)} %constant_dynamic-update-slice_fusion.refs_0_), channel_id=1, source_target_pairs={{48,0},{200,8},{0,16},{216,24},{16,32},{232,40},{32,48},{248,56},{... | collective-permute-start | bytes 2359304 | tf_op jit(solution)/shard_map/ppermute | solution.py:34
  29.4 3.9 %copy-start = (bf16[8,64,384]{2,1,0:T(8,128)(2,1)}, bf16[8,64,384]{2,1,0:T(8,128)(2,1)S(1)}, u32[]{:S(2)}) copy-start(bf16[8,64,384]{2,1,0:T(8,128)(2,1)S(1)} %all-to-all-done) | copy-start | bytes 1179652
  29.4 3.5 %collective-permute-start.6 = (bf16[512,384]{1,0:T(8,128)(2,1)S(1)}, bf16[512,384]{1,0:T(8,128)(2,1)}, u32[]{:S(2)}, u32[]{:S(2)}) collective-permute-start(bf16[512,384]{1,0:T(8,128)(2,1)S(1)} %bitcast.7), channel_id=1, source_target_pairs={{0,8},{8,0},{1,9},{9,1},{2,10},{10,2},{3,11},{11,3},{4,12},{12,4},... | collective-permute-start | bytes 1179656 | tf_op jit(solution)/shard_map/ppermute | solution.py:38
  31.4 16.0 %slice-start = ((s8[4718592]{0:T(1024)(128)(4,1)}), s8[4194304]{0:T(1024)(128)(4,1)S(1)}, s32[]{:S(2)}) async-start(s8[4718592]{0:T(1024)(128)(4,1)} %bitcast.5), calls=%async_computation.2 | async-start | bytes 8388608
  32.0 15.4 %slice-start.1 = ((s8[4718592]{0:T(1024)(128)(4,1)}), s8[524288]{0:T(1024)(128)(4,1)S(1)}, s32[]{:S(2)}) async-start(s8[4718592]{0:T(1024)(128)(4,1)} %bitcast.5), calls=%async_computation.3 | async-start | bytes 1048576
  32.0 15.4 %copy-start.9 = (s32[3]{0:T(128)S(1)}, s32[3]{0:T(128)}, u32[]{:S(2)}) copy-start(s32[3]{0:T(128)} %pad_add_fusion.pos) | copy-start | bytes 40
  32.9 12.2 %collective-permute-start.8 = (bf16[64,6144]{1,0:T(8,128)(2,1)S(1)}, bf16[64,6144]{1,0:T(8,128)(2,1)}, u32[]{:S(2)}, u32[]{:S(2)}) collective-permute-start(bf16[64,6144]{1,0:T(8,128)(2,1)S(1)} %constant_dynamic-update-slice_fusion.refs_0_), channel_id=1, source_target_pairs={{0,8},{8,0},{1,9},{9,1},{2,10},{10,2},{3,11},{11,3},{4,12},{12,4},... | collective-permute-start | bytes 2359304 | tf_op jit(solution)/shard_map/ppermute | solution.py:38
  42.8 3.4 %collective-permute-start.9 = (bf16[64,6144]{1,0:T(8,128)(2,1)S(1)}, bf16[64,6144]{1,0:T(8,128)(2,1)S(1)}, u32[]{:S(2)}, u32[]{:S(2)}) collective-permute-start(bf16[64,6144]{1,0:T(8,128)(2,1)S(1)} %collective-permute-done.3.refs_1_), channel_id=1, source_target_pairs={{0,8},{8,0},{1,9},{9,1},{2,10},{10,2},{3,11},{11,3},{4,12},{12,4},... | collective-permute-start | bytes 2359304 | tf_op jit(solution)/shard_map/ppermute | solution.py:38
  43.0 4.1 %collective-permute-start.10 = (bf16[64,6144]{1,0:T(8,128)(2,1)S(1)}, bf16[64,6144]{1,0:T(8,128)(2,1)S(1)}, u32[]{:S(2)}, u32[]{:S(2)}) collective-permute-start(bf16[64,6144]{1,0:T(8,128)(2,1)S(1)} %collective-permute-done.4.refs_2_), channel_id=1, source_target_pairs={{0,8},{8,0},{1,9},{9,1},{2,10},{10,2},{3,11},{11,3},{4,12},{12,4},... | collective-permute-start | bytes 2359304 | tf_op jit(solution)/shard_map/ppermute | solution.py:38
  43.4 4.0 %collective-permute-start.11 = (bf16[64,6144]{1,0:T(8,128)(2,1)S(1)}, bf16[64,6144]{1,0:T(8,128)(2,1)S(1)}, u32[]{:S(2)}, u32[]{:S(2)}) collective-permute-start(bf16[64,6144]{1,0:T(8,128)(2,1)S(1)} %collective-permute-done.5.refs_3_), channel_id=1, source_target_pairs={{0,8},{8,0},{1,9},{9,1},{2,10},{10,2},{3,11},{11,3},{4,12},{12,4},... | collective-permute-start | bytes 2359304 | tf_op jit(solution)/shard_map/ppermute | solution.py:38
  43.5 16.4 %collective-permute-start.12 = (bf16[3120,128]{1,0:T(8,128)(2,1)}, bf16[3120,128]{1,0:T(8,128)(2,1)}, u32[]{:S(2)}, u32[]{:S(2)}) collective-permute-start(bf16[3120,128]{1,0:T(8,128)(2,1)} %get-tuple-element.27), channel_id=1, source_target_pairs={{192,0},{56,8},{208,16},{8,24},{224,32},{24,40},{240,48},{40,56},{... | collective-permute-start | bytes 2396168 | tf_op jit(solution)/shard_map/ppermute | solution.py:34
  45.1 14.8 %collective-permute-start.13 = (bf16[3120,128]{1,0:T(8,128)(2,1)}, bf16[3120,128]{1,0:T(8,128)(2,1)}, u32[]{:S(2)}, u32[]{:S(2)}) collective-permute-start(bf16[3120,128]{1,0:T(8,128)(2,1)} %get-tuple-element.28), channel_id=1, source_target_pairs={{64,0},{24,8},{80,16},{40,24},{96,32},{56,40},{112,48},{8,56},{128... | collective-permute-start | bytes 2396168 | tf_op jit(solution)/shard_map/ppermute | solution.py:34
  46.2 6.1 %copy-start.2 = (bf16[64,6144]{1,0:T(8,128)(2,1)}, bf16[64,6144]{1,0:T(8,128)(2,1)S(1)}, u32[]{:S(2)}) copy-start(bf16[64,6144]{1,0:T(8,128)(2,1)S(1)} %collective-permute-done.9.refs_5_) | copy-start | bytes 2359300
  46.2 19.2 %collective-permute-start.14 = (bf16[3120,128]{1,0:T(8,128)(2,1)}, bf16[3120,128]{1,0:T(8,128)(2,1)}, u32[]{:S(2)}, u32[]{:S(2)}) collective-permute-start(bf16[3120,128]{1,0:T(8,128)(2,1)} %get-tuple-element.29), channel_id=1, source_target_pairs={{128,0},{40,8},{144,16},{56,24},{160,32},{8,40},{176,48},{24,56},{... | collective-permute-start | bytes 2396168 | tf_op jit(solution)/shard_map/ppermute | solution.py:34
  47.1 5.3 %copy-start.4 = (bf16[64,6144]{1,0:T(8,128)(2,1)}, bf16[64,6144]{1,0:T(8,128)(2,1)S(1)}, u32[]{:S(2)}) copy-start(bf16[64,6144]{1,0:T(8,128)(2,1)S(1)} %collective-permute-done.10.refs_6_) | copy-start | bytes 2359300
  47.4 4.9 %copy-start.6 = (bf16[64,6144]{1,0:T(8,128)(2,1)}, bf16[64,6144]{1,0:T(8,128)(2,1)S(1)}, u32[]{:S(2)}) copy-start(bf16[64,6144]{1,0:T(8,128)(2,1)S(1)} %collective-permute-done.11.refs_7_) | copy-start | bytes 2359300
  53.2 21.2 %copy-start.1 = (bf16[8,64,384]{2,1,0:T(8,128)(2,1)S(1)}, bf16[8,64,384]{2,1,0:T(8,128)(2,1)}, u32[]{:S(2)}) copy-start(bf16[8,64,384]{2,1,0:T(8,128)(2,1)} %copy-done) | copy-start | bytes 1179652
  53.2 30.6 %all-to-all-start.1 = ((f32[8,64,384]{2,1,0:T(8,128)}), f32[8,64,384]{2,1,0:T(8,128)}, u32[]{:S(2)}, u32[]{:S(2)}) async-start(f32[8,64,384]{2,1,0:T(8,128)} %bitcast.10), calls=%async_computation.1 | async-start | bytes 1572864 | tf_op jit(solution)/shard_map/all_to_all | solution.py:305
  65.3 1.4 %copy-start.10 = (f32[3072,128]{1,0:T(8,128)S(1)}, f32[3072,128]{1,0:T(8,128)}, u32[]{:S(2)}) copy-start(f32[3072,128]{1,0:T(8,128)} %get-tuple-element.23.own_in) | copy-start | bytes 4718596
  70.5 12.3 %collective-permute-start.15 = (bf16[816,128]{1,0:T(8,128)(2,1)S(1)}, bf16[816,128]{1,0:T(8,128)(2,1)S(1)}, u32[]{:S(2)}, u32[]{:S(2)}) collective-permute-start(bf16[816,128]{1,0:T(8,128)(2,1)S(1)} %get-tuple-element.32), channel_id=1, source_target_pairs={{48,0},{200,8},{0,16},{216,24},{16,32},{232,40},{32,48},{248,56},{... | collective-permute-start | bytes 626696 | tf_op jit(solution)/shard_map/ppermute | solution.py:34
  71.5 11.3 %collective-permute-start.16 = (bf16[816,128]{1,0:T(8,128)(2,1)S(1)}, bf16[816,128]{1,0:T(8,128)(2,1)S(1)}, u32[]{:S(2)}, u32[]{:S(2)}) collective-permute-start(bf16[816,128]{1,0:T(8,128)(2,1)S(1)} %get-tuple-element.33), channel_id=1, source_target_pairs={{16,0},{72,8},{32,16},{88,24},{48,32},{104,40},{0,48},{120,56},{80... | collective-permute-start | bytes 626696 | tf_op jit(solution)/shard_map/ppermute | solution.py:34
  73.2 9.6 %collective-permute-start.17 = (bf16[816,128]{1,0:T(8,128)(2,1)S(1)}, bf16[816,128]{1,0:T(8,128)(2,1)S(1)}, u32[]{:S(2)}, u32[]{:S(2)}) collective-permute-start(bf16[816,128]{1,0:T(8,128)(2,1)S(1)} %get-tuple-element.34), channel_id=1, source_target_pairs={{32,0},{136,8},{48,16},{152,24},{0,32},{168,40},{16,48},{184,56},{... | collective-permute-start | bytes 626696 | tf_op jit(solution)/shard_map/ppermute | solution.py:34
  74.5 1.1 %copy-start.3 = (bf16[64,6144]{1,0:T(8,128)(2,1)S(1)}, bf16[64,6144]{1,0:T(8,128)(2,1)}, u32[]{:S(2)}) copy-start(bf16[64,6144]{1,0:T(8,128)(2,1)} %copy-done.2) | copy-start | bytes 2359300
  75.6 1.1 %copy-start.5 = (bf16[64,6144]{1,0:T(8,128)(2,1)S(1)}, bf16[64,6144]{1,0:T(8,128)(2,1)}, u32[]{:S(2)}) copy-start(bf16[64,6144]{1,0:T(8,128)(2,1)} %copy-done.4) | copy-start | bytes 2359300
  76.7 1.1 %copy-start.7 = (bf16[64,6144]{1,0:T(8,128)(2,1)S(1)}, bf16[64,6144]{1,0:T(8,128)(2,1)}, u32[]{:S(2)}) copy-start(bf16[64,6144]{1,0:T(8,128)(2,1)} %copy-done.6) | copy-start | bytes 2359300
  (1 other events, 0.9 us)

commit v5 on v4

--- a/solution.py
+++ b/solution.py
@@ -267,7 +267,7 @@
             pltpu.VMEM((6, 384, 1024), BF),
             pltpu.SemaphoreType.DMA((6,)),
         ],
-        compiler_params=pltpu.CompilerParams(vmem_limit_bytes=28 * 2**20),
+        compiler_params=pltpu.CompilerParams(vmem_limit_bytes=58 * 2**20),
         cost_estimate=pl.CostEstimate(flops=2 * 512 * 384 * 6144, bytes_accessed=12 * 2**20, transcendentals=0),
         name="grad_weight",
     )(pos, acts, *pieces)

time: 86.8 us -> 84.5 us (0.974)
  local copies, waits for them, and re-layouts: 8.28 us -> 4.89 us
  Pallas kernels: 24 us -> 25.8 us
  waiting for transfers between devices: 15.5 us -> 16.7 us
  other arithmetic: 2.4 us -> 1.26 us
    unnamed x29, local copies, waits for them, and re-layouts: 6.68 us -> 3.29 us
    pallas_call x1, Pallas kernels: 4.9 us -> 6.68 us  [grad_weight_of(): pl.pallas_call(grad_weight_kernel, in_specs=[SMEM] + [VMEM] * 9, out_spec...]
    reduce_sum x1, other arithmetic: 1.81 us -> 0.66 us  [body(): lax.all_to_all(terms.reshape(8, 64, 384), 'z', 0, 0).sum(axis=0).astype(BF)]
    all_to_all x1, waiting for transfers between devices: 0.01 us -> 1.15 us  [body(): lax.all_to_all(terms.reshape(8, 64, 384), 'z', 0, 0).sum(axis=0).astype(BF)]
  transfers between devices with their start and end apart: 20 -> 20, of which waited for: 4 -> 5; matrix products, arithmetic and copies ran while one was open for 4% -> 4% of each run, Pallas kernels for 28% -> 31%
where the time goes in v5:
time: 84.5 us; the launch traced here: 84.1 us
  starting transfers between devices  34.5 us (41%)
  Pallas kernels  25.8 us (31%)
  waiting for transfers between devices  16.7 us (20%)
  local copies, waits for them, and re-layouts  4.89 us (6%)
  other arithmetic  1.26 us (1%)
  between operations  0.91 us (1%)
    ppermute x12, starting transfers between devices, get(): return lax.ppermute(value, ROWS, ring(distance, second))  13.3 us
    pallas_call x1, Pallas kernels, project(): pl.pallas_call(project_kernel, in_specs=[SMEM, VMEM, VMEM, HBM, HBM], out...  9.45 us
    all_to_all x1, waiting for transfers between devices, body(): lax.all_to_all(jnp.broadcast_to(inputs[None], (8, 64, 384)), 'z', 0, 0)  8.86 us
    all_to_all x1, starting transfers between devices, body(): lax.all_to_all(jnp.broadcast_to(inputs[None], (8, 64, 384)), 'z', 0, 0)  8.19 us
    pallas_call x1, Pallas kernels, grad_weight_of(): pl.pallas_call(grad_weight_kernel, in_specs=[SMEM] + [VMEM] * 9, out_spec...  6.68 us
    all_to_all x1, starting transfers between devices, body(): lax.all_to_all(terms.reshape(8, 64, 384), 'z', 0, 0).sum(axis=0).astype(BF)  6.55 us
    ppermute x6, starting transfers between devices, swap(): return lax.ppermute(value, 'core', [(0, 1), (1, 0)])  6.48 us
    ppermute x12, waiting for transfers between devices, get(): return lax.ppermute(value, ROWS, ring(distance, second))  5.54 us
  transfers between devices with their start and end apart: 20, of which 5 were waited for; matrix products, arithmetic and copies ran while one was open for 4% of the time, Pallas kernels for 31%

profile of v5, /device:TPU:1, one launch (start us, length us, event | category | flops | bytes accessed | tf_op | source)
XLA Modules:
  0.0 84.1 jit_solution(14375297947112555634)
XLA Ops:
  0.6 3.3 %collective-permute-start.7 = (bf16[384,6144]{1,0:T(8,128)(2,1)}, bf16[384,6144]{1,0:T(8,128)(2,1)}, u32[]{:S(2)}, u32[]{:S(2)}) collective-permute-start(bf16[384,6144]{1,0:T(8,128)(2,1)} %refs_8_.1), channel_id=1, source_target_pairs={{0,8},{8,0},{1,9},{9,1},{2,10},{10,2},{3,11},{11,3},{4,12},{12,4},... | collective-permute-start | bytes 14155784 | tf_op jit(solution)/shard_map/ppermute | solution.py:38
  4.0 1.0 %collective-permute-start = (bf16[16,6144]{1,0:T(8,128)(2,1)}, bf16[16,6144]{1,0:T(8,128)(2,1)S(1)}, u32[]{:S(2)}, u32[]{:S(2)}) collective-permute-start(bf16[16,6144]{1,0:T(8,128)(2,1)} %param.5), channel_id=1, source_target_pairs={{64,0},{24,8},{80,16},{40,24},{96,32},{56,40},{112,48},{8,56},{128... | collective-permute-start | bytes 589832 | tf_op jit(solution)/shard_map/ppermute | solution.py:34
  5.3 0.7 collective-permute-start.2
  6.0 1.6 %broadcast_in_dim.2 = bf16[8,64,384]{2,1,0:T(8,128)(2,1)} broadcast(bf16[64,384]{1,0:T(8,128)(2,1)} %param.3), dimensions={1,2} | broadcast | bytes 442368 | tf_op jit(solution)/shard_map/broadcast_in_dim | solution.py:288
  7.6 8.2 %all-to-all-start = ((bf16[8,64,384]{2,1,0:T(8,128)(2,1)}), bf16[8,64,384]{2,1,0:T(8,128)(2,1)S(1)}, u32[]{:S(2)}, u32[]{:S(2)}) async-start(bf16[8,64,384]{2,1,0:T(8,128)(2,1)} %broadcast_in_dim.2), calls=%async_computation | async-start | bytes 786432 | tf_op jit(solution)/shard_map/all_to_all | solution.py:288
  15.8 0.9 %constant_dynamic-update-slice_fusion.3 = bf16[64,6144]{1,0:T(8,128)(2,1)S(1)} fusion(bf16[16,6144]{1,0:T(8,128)(2,1)} %param.5), kind=kLoop, calls=%fused_computation.3 | loop fusion | bytes 393216
  16.8 2.6 %collective-permute-start.3 = (bf16[64,6144]{1,0:T(8,128)(2,1)S(1)}, bf16[64,6144]{1,0:T(8,128)(2,1)S(1)}, u32[]{:S(2)}, u32[]{:S(2)}) collective-permute-start(bf16[64,6144]{1,0:T(8,128)(2,1)S(1)} %constant_dynamic-update-slice_fusion.refs_0_), channel_id=1, source_target_pairs={{16,0},{72,8},{32,16},{88,24},{48,32},{104,40},{0,48},{120,56},{80... | collective-permute-start | bytes 2359304 | tf_op jit(solution)/shard_map/ppermute | solution.py:34
  19.4 0.5 collective-permute-start.4
  19.9 0.6 collective-permute-start.5
  20.5 8.9 %all-to-all-done = bf16[8,64,384]{2,1,0:T(8,128)(2,1)S(1)} async-done(((bf16[8,64,384]{2,1,0:T(8,128)(2,1)}), bf16[8,64,384]{2,1,0:T(8,128)(2,1)S(1)}, u32[]{:S(2)}, u32[]{:S(2)}) %all-to-all-start) | async-done | bytes 393248 | tf_op jit(solution)/shard_map/all_to_all | solution.py:288
  29.4 2.0 %collective-permute-start.6 = (bf16[512,384]{1,0:T(8,128)(2,1)S(1)}, bf16[512,384]{1,0:T(8,128)(2,1)}, u32[]{:S(2)}, u32[]{:S(2)}) collective-permute-start(bf16[512,384]{1,0:T(8,128)(2,1)S(1)} %bitcast.8), channel_id=1, source_target_pairs={{0,8},{8,0},{1,9},{9,1},{2,10},{10,2},{3,11},{11,3},{4,12},{12,4},... | collective-permute-start | bytes 1179656 | tf_op jit(solution)/shard_map/ppermute | solution.py:38
  31.4 0.6 pad_add_fusion.pos
  32.0 0.9 %collective-permute-done.6.par_in = bf16[512,384]{1,0:T(8,128)(2,1)} collective-permute-done((bf16[512,384]{1,0:T(8,128)(2,1)S(1)}, bf16[512,384]{1,0:T(8,128)(2,1)}, u32[]{:S(2)}, u32[]{:S(2)}) %collective-permute-start.6) | collective-permute-done | bytes 393248 | tf_op jit(solution)/shard_map/ppermute | solution.py:38
  32.9 0.4 collective-permute-start.8
  33.3 9.4 %project.1 = (f32[3072,128]{1,0:T(8,128)}, bf16[3120,128]{1,0:T(8,128)(2,1)}, bf16[3120,128]{1,0:T(8,128)(2,1)}, bf16[3120,128]{1,0:T(8,128)(2,1)}) custom-call(s32[3]{0:T(128)} %pad_add_fusion.pos, bf16[512,384]{1,0:T(8,128)(2,1)} %bitcast.9, bf16[512,384]{1,0:T(8,128)(2,1)} %collective-permute-done.6.par_in, bf16[384,6144]{1,0:T(8,128)(2,1)} %refs_8_.1, ...), custom_call_target="tpu_custom_call" | custom-call | flops 2415919104 | bytes 10485760 | tf_op jit(solution)/shard_map/project/pallas_call | solution.py:123
  43.0 0.4 collective-permute-start.10
  43.5 1.6 %collective-permute-start.12 = (bf16[3120,128]{1,0:T(8,128)(2,1)}, bf16[3120,128]{1,0:T(8,128)(2,1)}, u32[]{:S(2)}, u32[]{:S(2)}) collective-permute-start(bf16[3120,128]{1,0:T(8,128)(2,1)} %get-tuple-element.27), channel_id=1, source_target_pairs={{192,0},{56,8},{208,16},{8,24},{224,32},{24,40},{240,48},{40,56},{... | collective-permute-start | bytes 2396168 | tf_op jit(solution)/shard_map/ppermute | solution.py:34
  45.1 1.1 %collective-permute-start.13 = (bf16[3120,128]{1,0:T(8,128)(2,1)}, bf16[3120,128]{1,0:T(8,128)(2,1)}, u32[]{:S(2)}, u32[]{:S(2)}) collective-permute-start(bf16[3120,128]{1,0:T(8,128)(2,1)} %get-tuple-element.28), channel_id=1, source_target_pairs={{64,0},{24,8},{80,16},{40,24},{96,32},{56,40},{112,48},{8,56},{128... | collective-permute-start | bytes 2396168 | tf_op jit(solution)/shard_map/ppermute | solution.py:34
  46.2 0.9 %collective-permute-start.14 = (bf16[3120,128]{1,0:T(8,128)(2,1)}, bf16[3120,128]{1,0:T(8,128)(2,1)}, u32[]{:S(2)}, u32[]{:S(2)}) collective-permute-start(bf16[3120,128]{1,0:T(8,128)(2,1)} %get-tuple-element.29), channel_id=1, source_target_pairs={{128,0},{40,8},{144,16},{56,24},{160,32},{8,40},{176,48},{24,56},{... | collective-permute-start | bytes 2396168 | tf_op jit(solution)/shard_map/ppermute | solution.py:34
  47.4 4.9 %grad_inputs.1 = f32[512,384]{1,0:T(8,128)S(1)} custom-call(s32[3]{0:T(128)S(1)} %copy-done.8, bf16[64,6144]{1,0:T(8,128)(2,1)S(1)} %constant_dynamic-update-slice_fusion.refs_0_, bf16[64,6144]{1,0:T(8,128)(2,1)S(1)} %collective-permute-done.3.refs_1_, bf16[64,6144]{1,0:T(8,128)(2,1)S(1)} %collective-permute-done.4.refs_2_, ...), custom_call_target="tpu_custom_call" | custom-call | flops 2415919104 | bytes 12582912 | tf_op jit(solution)/shard_map/grad_inputs/pallas_call | solution.py:229
  52.4 0.9 %copy-done.7 = f32[512,384]{1,0:T(8,128)} copy-done((f32[512,384]{1,0:T(8,128)}, f32[512,384]{1,0:T(8,128)S(1)}, u32[]{:S(2)}) %copy-start.7) | copy-done | bytes 786456
  53.3 6.5 %all-to-all-start.1 = ((f32[8,64,384]{2,1,0:T(8,128)}), f32[8,64,384]{2,1,0:T(8,128)S(1)}, u32[]{:S(2)}, u32[]{:S(2)}) async-start(f32[8,64,384]{2,1,0:T(8,128)} %bitcast.7), calls=%async_computation.1 | async-start | bytes 1572864 | tf_op jit(solution)/shard_map/all_to_all | solution.py:305
  59.9 5.5 %collective-permute-done.14.in3 = bf16[3120,128]{1,0:T(8,128)(2,1)} collective-permute-done((bf16[3120,128]{1,0:T(8,128)(2,1)}, bf16[3120,128]{1,0:T(8,128)(2,1)}, u32[]{:S(2)}, u32[]{:S(2)}) %collective-permute-start.14) | collective-permute-done | bytes 798752 | tf_op jit(solution)/shard_map/ppermute | solution.py:34
  65.4 1.4 %copy-done.9 = f32[3072,128]{1,0:T(8,128)S(1)} copy-done((f32[3072,128]{1,0:T(8,128)S(1)}, f32[3072,128]{1,0:T(8,128)}, u32[]{:S(2)}) %copy-start.9) | copy-done | bytes 1572888
  66.8 3.7 %relay.1 = (f32[768,128]{1,0:T(8,128)S(1)}, bf16[816,128]{1,0:T(8,128)(2,1)S(1)}, bf16[816,128]{1,0:T(8,128)(2,1)S(1)}, bf16[816,128]{1,0:T(8,128)(2,1)S(1)}) custom-call(f32[3072,128]{1,0:T(8,128)S(1)} %copy-done.9, bf16[3120,128]{1,0:T(8,128)(2,1)} %collective-permute-done.12.in1, bf16[3120,128]{1,0:T(8,128)(2,1)} %collective-permute-done.13.in2, ...), custom_call_target="tpu_custom_call" | custom-call | flops 8388608 | bytes 5242880 | tf_op jit(solution)/shard_map/relay/pallas_call | solution.py:168
  70.5 1.0 %collective-permute-start.15 = (bf16[816,128]{1,0:T(8,128)(2,1)S(1)}, bf16[816,128]{1,0:T(8,128)(2,1)S(1)}, u32[]{:S(2)}, u32[]{:S(2)}) collective-permute-start(bf16[816,128]{1,0:T(8,128)(2,1)S(1)} %get-tuple-element.32), channel_id=1, source_target_pairs={{48,0},{200,8},{0,16},{216,24},{16,32},{232,40},{32,48},{248,56},{... | collective-permute-start | bytes 626696 | tf_op jit(solution)/shard_map/ppermute | solution.py:34
  71.5 1.8 %collective-permute-start.16 = (bf16[816,128]{1,0:T(8,128)(2,1)S(1)}, bf16[816,128]{1,0:T(8,128)(2,1)S(1)}, u32[]{:S(2)}, u32[]{:S(2)}) collective-permute-start(bf16[816,128]{1,0:T(8,128)(2,1)S(1)} %get-tuple-element.33), channel_id=1, source_target_pairs={{16,0},{72,8},{32,16},{88,24},{48,32},{104,40},{0,48},{120,56},{80... | collective-permute-start | bytes 626696 | tf_op jit(solution)/shard_map/ppermute | solution.py:34
  73.2 1.2 %collective-permute-start.17 = (bf16[816,128]{1,0:T(8,128)(2,1)S(1)}, bf16[816,128]{1,0:T(8,128)(2,1)S(1)}, u32[]{:S(2)}, u32[]{:S(2)}) collective-permute-start(bf16[816,128]{1,0:T(8,128)(2,1)S(1)} %get-tuple-element.34), channel_id=1, source_target_pairs={{32,0},{136,8},{48,16},{152,24},{0,32},{168,40},{16,48},{184,56},{... | collective-permute-start | bytes 626696 | tf_op jit(solution)/shard_map/ppermute | solution.py:34
  74.5 6.7 %grad_weight.1 = bf16[384,6144]{1,0:T(8,128)(2,1)} custom-call(s32[3]{0:T(128)} %pad_add_fusion.pos, bf16[512,384]{1,0:T(8,128)(2,1)} %bitcast.10, bf16[64,6144]{1,0:T(8,128)(2,1)} %copy-done, bf16[64,6144]{1,0:T(8,128)(2,1)} %copy-done.1, bf16[64,6144]{1,0:T(8,128)(2,1)} %copy-done.2, bf16[64,6144]{1,0:T(8,128)(2,1)} %copy-done.3, ...), custom_call_target="tpu_custom_call" | custom-call | flops 2415919104 | bytes 12582912 | tf_op jit(solution)/shard_map/grad_weight/pallas_call | solution.py:260
  81.2 1.1 %finish.1 = bf16[16,6144]{1,0:T(8,128)(2,1)} custom-call(f32[768,128]{1,0:T(8,128)S(1)} %get-tuple-element.31.own, bf16[816,128]{1,0:T(8,128)(2,1)S(1)} %collective-permute-done.15.in1, bf16[816,128]{1,0:T(8,128)(2,1)S(1)} %collective-permute-done.16.in2, bf16[816,128]{1,0:T(8,128)(2,1)S(1)} %collective-permute-done.17.in3), custom_call_target="tpu_custom_call" | custom-call | flops 4294967296 | bytes 1048576 | tf_op jit(solution)/shard_map/finish/pallas_call | solution.py:195
  82.3 1.1 %all-to-all-done.1 = f32[8,64,384]{2,1,0:T(8,128)S(1)} async-done(((f32[8,64,384]{2,1,0:T(8,128)}), f32[8,64,384]{2,1,0:T(8,128)S(1)}, u32[]{:S(2)}, u32[]{:S(2)}) %all-to-all-start.1) | async-done | bytes 786464 | tf_op jit(solution)/shard_map/all_to_all | solution.py:305
  83.4 0.7 reduce_sum.9
  (47 shorter events, 1.2 us)
Async XLA Ops:
  0.6 32.6 %collective-permute-start.7 = (bf16[384,6144]{1,0:T(8,128)(2,1)}, bf16[384,6144]{1,0:T(8,128)(2,1)}, u32[]{:S(2)}, u32[]{:S(2)}) collective-permute-start(bf16[384,6144]{1,0:T(8,128)(2,1)} %refs_8_.1), channel_id=1, source_target_pairs={{0,8},{8,0},{1,9},{9,1},{2,10},{10,2},{3,11},{11,3},{4,12},{12,4},... | collective-permute-start | bytes 14155784 | tf_op jit(solution)/shard_map/ppermute | solution.py:38
  4.0 12.8 %collective-permute-start = (bf16[16,6144]{1,0:T(8,128)(2,1)}, bf16[16,6144]{1,0:T(8,128)(2,1)S(1)}, u32[]{:S(2)}, u32[]{:S(2)}) collective-permute-start(bf16[16,6144]{1,0:T(8,128)(2,1)} %param.5), channel_id=1, source_target_pairs={{64,0},{24,8},{80,16},{40,24},{96,32},{56,40},{112,48},{8,56},{128... | collective-permute-start | bytes 589832 | tf_op jit(solution)/shard_map/ppermute | solution.py:34
  5.0 11.8 %collective-permute-start.1 = (bf16[16,6144]{1,0:T(8,128)(2,1)}, bf16[16,6144]{1,0:T(8,128)(2,1)S(1)}, u32[]{:S(2)}, u32[]{:S(2)}) collective-permute-start(bf16[16,6144]{1,0:T(8,128)(2,1)} %param.5), channel_id=1, source_target_pairs={{128,0},{40,8},{144,16},{56,24},{160,32},{8,40},{176,48},{24,56},{... | collective-permute-start | bytes 589832 | tf_op jit(solution)/shard_map/ppermute | solution.py:34
  5.3 11.5 %collective-permute-start.2 = (bf16[16,6144]{1,0:T(8,128)(2,1)}, bf16[16,6144]{1,0:T(8,128)(2,1)S(1)}, u32[]{:S(2)}, u32[]{:S(2)}) collective-permute-start(bf16[16,6144]{1,0:T(8,128)(2,1)} %param.5), channel_id=1, source_target_pairs={{192,0},{56,8},{208,16},{8,24},{224,32},{24,40},{240,48},{40,56},{... | collective-permute-start | bytes 589832 | tf_op jit(solution)/shard_map/ppermute | solution.py:34
  7.6 21.8 %all-to-all-start = ((bf16[8,64,384]{2,1,0:T(8,128)(2,1)}), bf16[8,64,384]{2,1,0:T(8,128)(2,1)S(1)}, u32[]{:S(2)}, u32[]{:S(2)}) async-start(bf16[8,64,384]{2,1,0:T(8,128)(2,1)} %broadcast_in_dim.2), calls=%async_computation | async-start | bytes 786432 | tf_op jit(solution)/shard_map/all_to_all | solution.py:288
  16.8 30.6 %copy-start = (bf16[64,6144]{1,0:T(8,128)(2,1)}, bf16[64,6144]{1,0:T(8,128)(2,1)S(1)}, u32[]{:S(2)}) copy-start(bf16[64,6144]{1,0:T(8,128)(2,1)S(1)} %constant_dynamic-update-slice_fusion.refs_0_) | copy-start | bytes 2359300
  16.8 25.9 %collective-permute-start.3 = (bf16[64,6144]{1,0:T(8,128)(2,1)S(1)}, bf16[64,6144]{1,0:T(8,128)(2,1)S(1)}, u32[]{:S(2)}, u32[]{:S(2)}) collective-permute-start(bf16[64,6144]{1,0:T(8,128)(2,1)S(1)} %constant_dynamic-update-slice_fusion.refs_0_), channel_id=1, source_target_pairs={{16,0},{72,8},{32,16},{88,24},{48,32},{104,40},{0,48},{120,56},{80... | collective-permute-start | bytes 2359304 | tf_op jit(solution)/shard_map/ppermute | solution.py:34
  19.4 23.4 %collective-permute-start.4 = (bf16[64,6144]{1,0:T(8,128)(2,1)S(1)}, bf16[64,6144]{1,0:T(8,128)(2,1)S(1)}, u32[]{:S(2)}, u32[]{:S(2)}) collective-permute-start(bf16[64,6144]{1,0:T(8,128)(2,1)S(1)} %constant_dynamic-update-slice_fusion.refs_0_), channel_id=1, source_target_pairs={{32,0},{136,8},{48,16},{152,24},{0,32},{168,40},{16,48},{184,56},{... | collective-permute-start | bytes 2359304 | tf_op jit(solution)/shard_map/ppermute | solution.py:34
  19.9 22.9 %collective-permute-start.5 = (bf16[64,6144]{1,0:T(8,128)(2,1)S(1)}, bf16[64,6144]{1,0:T(8,128)(2,1)S(1)}, u32[]{:S(2)}, u32[]{:S(2)}) collective-permute-start(bf16[64,6144]{1,0:T(8,128)(2,1)S(1)} %constant_dynamic-update-slice_fusion.refs_0_), channel_id=1, source_target_pairs={{48,0},{200,8},{0,16},{216,24},{16,32},{232,40},{32,48},{248,56},{... | collective-permute-start | bytes 2359304 | tf_op jit(solution)/shard_map/ppermute | solution.py:34
  29.4 3.9 %copy-start.10 = (bf16[8,64,384]{2,1,0:T(8,128)(2,1)}, bf16[8,64,384]{2,1,0:T(8,128)(2,1)S(1)}, u32[]{:S(2)}) copy-start(bf16[8,64,384]{2,1,0:T(8,128)(2,1)S(1)} %all-to-all-done) | copy-start | bytes 1179652
  29.4 3.5 %collective-permute-start.6 = (bf16[512,384]{1,0:T(8,128)(2,1)S(1)}, bf16[512,384]{1,0:T(8,128)(2,1)}, u32[]{:S(2)}, u32[]{:S(2)}) collective-permute-start(bf16[512,384]{1,0:T(8,128)(2,1)S(1)} %bitcast.8), channel_id=1, source_target_pairs={{0,8},{8,0},{1,9},{9,1},{2,10},{10,2},{3,11},{11,3},{4,12},{12,4},... | collective-permute-start | bytes 1179656 | tf_op jit(solution)/shard_map/ppermute | solution.py:38
  31.4 16.0 %slice-start = ((s8[4718592]{0:T(1024)(128)(4,1)}), s8[4194304]{0:T(1024)(128)(4,1)S(1)}, s32[]{:S(2)}) async-start(s8[4718592]{0:T(1024)(128)(4,1)} %bitcast.5), calls=%async_computation.2 | async-start | bytes 8388608
  32.0 15.4 %slice-start.1 = ((s8[4718592]{0:T(1024)(128)(4,1)}), s8[524288]{0:T(1024)(128)(4,1)S(1)}, s32[]{:S(2)}) async-start(s8[4718592]{0:T(1024)(128)(4,1)} %bitcast.5), calls=%async_computation.3 | async-start | bytes 1048576
  32.0 15.4 %copy-start.8 = (s32[3]{0:T(128)S(1)}, s32[3]{0:T(128)}, u32[]{:S(2)}) copy-start(s32[3]{0:T(128)} %pad_add_fusion.pos) | copy-start | bytes 40
  32.9 12.2 %collective-permute-start.8 = (bf16[64,6144]{1,0:T(8,128)(2,1)S(1)}, bf16[64,6144]{1,0:T(8,128)(2,1)}, u32[]{:S(2)}, u32[]{:S(2)}) collective-permute-start(bf16[64,6144]{1,0:T(8,128)(2,1)S(1)} %constant_dynamic-update-slice_fusion.refs_0_), channel_id=1, source_target_pairs={{0,8},{8,0},{1,9},{9,1},{2,10},{10,2},{3,11},{11,3},{4,12},{12,4},... | collective-permute-start | bytes 2359304 | tf_op jit(solution)/shard_map/ppermute | solution.py:38
  42.7 9.6 %copy-start.1 = (bf16[64,6144]{1,0:T(8,128)(2,1)}, bf16[64,6144]{1,0:T(8,128)(2,1)S(1)}, u32[]{:S(2)}) copy-start(bf16[64,6144]{1,0:T(8,128)(2,1)S(1)} %collective-permute-done.3.refs_1_) | copy-start | bytes 2359300
  42.8 9.6 %copy-start.2 = (bf16[64,6144]{1,0:T(8,128)(2,1)}, bf16[64,6144]{1,0:T(8,128)(2,1)S(1)}, u32[]{:S(2)}) copy-start(bf16[64,6144]{1,0:T(8,128)(2,1)S(1)} %collective-permute-done.4.refs_2_) | copy-start | bytes 2359300
  42.8 9.6 %copy-start.3 = (bf16[64,6144]{1,0:T(8,128)(2,1)}, bf16[64,6144]{1,0:T(8,128)(2,1)S(1)}, u32[]{:S(2)}) copy-start(bf16[64,6144]{1,0:T(8,128)(2,1)S(1)} %collective-permute-done.5.refs_3_) | copy-start | bytes 2359300
  42.8 3.4 %collective-permute-start.9 = (bf16[64,6144]{1,0:T(8,128)(2,1)S(1)}, bf16[64,6144]{1,0:T(8,128)(2,1)S(1)}, u32[]{:S(2)}, u32[]{:S(2)}) collective-permute-start(bf16[64,6144]{1,0:T(8,128)(2,1)S(1)} %collective-permute-done.3.refs_1_), channel_id=1, source_target_pairs={{0,8},{8,0},{1,9},{9,1},{2,10},{10,2},{3,11},{11,3},{4,12},{12,4},... | collective-permute-start | bytes 2359304 | tf_op jit(solution)/shard_map/ppermute | solution.py:38
  43.0 4.1 %collective-permute-start.10 = (bf16[64,6144]{1,0:T(8,128)(2,1)S(1)}, bf16[64,6144]{1,0:T(8,128)(2,1)S(1)}, u32[]{:S(2)}, u32[]{:S(2)}) collective-permute-start(bf16[64,6144]{1,0:T(8,128)(2,1)S(1)} %collective-permute-done.4.refs_2_), channel_id=1, source_target_pairs={{0,8},{8,0},{1,9},{9,1},{2,10},{10,2},{3,11},{11,3},{4,12},{12,4},... | collective-permute-start | bytes 2359304 | tf_op jit(solution)/shard_map/ppermute | solution.py:38
  43.4 4.0 %collective-permute-start.11 = (bf16[64,6144]{1,0:T(8,128)(2,1)S(1)}, bf16[64,6144]{1,0:T(8,128)(2,1)S(1)}, u32[]{:S(2)}, u32[]{:S(2)}) collective-permute-start(bf16[64,6144]{1,0:T(8,128)(2,1)S(1)} %collective-permute-done.5.refs_3_), channel_id=1, source_target_pairs={{0,8},{8,0},{1,9},{9,1},{2,10},{10,2},{3,11},{11,3},{4,12},{12,4},... | collective-permute-start | bytes 2359304 | tf_op jit(solution)/shard_map/ppermute | solution.py:38
  43.5 16.3 %collective-permute-start.12 = (bf16[3120,128]{1,0:T(8,128)(2,1)}, bf16[3120,128]{1,0:T(8,128)(2,1)}, u32[]{:S(2)}, u32[]{:S(2)}) collective-permute-start(bf16[3120,128]{1,0:T(8,128)(2,1)} %get-tuple-element.27), channel_id=1, source_target_pairs={{192,0},{56,8},{208,16},{8,24},{224,32},{24,40},{240,48},{40,56},{... | collective-permute-start | bytes 2396168 | tf_op jit(solution)/shard_map/ppermute | solution.py:34
  45.1 14.7 %collective-permute-start.13 = (bf16[3120,128]{1,0:T(8,128)(2,1)}, bf16[3120,128]{1,0:T(8,128)(2,1)}, u32[]{:S(2)}, u32[]{:S(2)}) collective-permute-start(bf16[3120,128]{1,0:T(8,128)(2,1)} %get-tuple-element.28), channel_id=1, source_target_pairs={{64,0},{24,8},{80,16},{40,24},{96,32},{56,40},{112,48},{8,56},{128... | collective-permute-start | bytes 2396168 | tf_op jit(solution)/shard_map/ppermute | solution.py:34
  46.2 6.2 %copy-start.4 = (bf16[64,6144]{1,0:T(8,128)(2,1)}, bf16[64,6144]{1,0:T(8,128)(2,1)S(1)}, u32[]{:S(2)}) copy-start(bf16[64,6144]{1,0:T(8,128)(2,1)S(1)} %collective-permute-done.9.refs_5_) | copy-start | bytes 2359300
  46.2 19.2 %collective-permute-start.14 = (bf16[3120,128]{1,0:T(8,128)(2,1)}, bf16[3120,128]{1,0:T(8,128)(2,1)}, u32[]{:S(2)}, u32[]{:S(2)}) collective-permute-start(bf16[3120,128]{1,0:T(8,128)(2,1)} %get-tuple-element.29), channel_id=1, source_target_pairs={{128,0},{40,8},{144,16},{56,24},{160,32},{8,40},{176,48},{24,56},{... | collective-permute-start | bytes 2396168 | tf_op jit(solution)/shard_map/ppermute | solution.py:34
  47.1 5.3 %copy-start.5 = (bf16[64,6144]{1,0:T(8,128)(2,1)}, bf16[64,6144]{1,0:T(8,128)(2,1)S(1)}, u32[]{:S(2)}) copy-start(bf16[64,6144]{1,0:T(8,128)(2,1)S(1)} %collective-permute-done.10.refs_6_) | copy-start | bytes 2359300
  47.4 5.0 %copy-start.6 = (bf16[64,6144]{1,0:T(8,128)(2,1)}, bf16[64,6144]{1,0:T(8,128)(2,1)S(1)}, u32[]{:S(2)}) copy-start(bf16[64,6144]{1,0:T(8,128)(2,1)S(1)} %collective-permute-done.11.refs_7_) | copy-start | bytes 2359300
  53.3 30.1 %all-to-all-start.1 = ((f32[8,64,384]{2,1,0:T(8,128)}), f32[8,64,384]{2,1,0:T(8,128)S(1)}, u32[]{:S(2)}, u32[]{:S(2)}) async-start(f32[8,64,384]{2,1,0:T(8,128)} %bitcast.7), calls=%async_computation.1 | async-start | bytes 1572864 | tf_op jit(solution)/shard_map/all_to_all | solution.py:305
  65.4 1.4 %copy-start.9 = (f32[3072,128]{1,0:T(8,128)S(1)}, f32[3072,128]{1,0:T(8,128)}, u32[]{:S(2)}) copy-start(f32[3072,128]{1,0:T(8,128)} %get-tuple-element.23.own_in) | copy-start | bytes 4718596
  70.5 10.7 %collective-permute-start.15 = (bf16[816,128]{1,0:T(8,128)(2,1)S(1)}, bf16[816,128]{1,0:T(8,128)(2,1)S(1)}, u32[]{:S(2)}, u32[]{:S(2)}) collective-permute-start(bf16[816,128]{1,0:T(8,128)(2,1)S(1)} %get-tuple-element.32), channel_id=1, source_target_pairs={{48,0},{200,8},{0,16},{216,24},{16,32},{232,40},{32,48},{248,56},{... | collective-permute-start | bytes 626696 | tf_op jit(solution)/shard_map/ppermute | solution.py:34
  71.5 9.7 %collective-permute-start.16 = (bf16[816,128]{1,0:T(8,128)(2,1)S(1)}, bf16[816,128]{1,0:T(8,128)(2,1)S(1)}, u32[]{:S(2)}, u32[]{:S(2)}) collective-permute-start(bf16[816,128]{1,0:T(8,128)(2,1)S(1)} %get-tuple-element.33), channel_id=1, source_target_pairs={{16,0},{72,8},{32,16},{88,24},{48,32},{104,40},{0,48},{120,56},{80... | collective-permute-start | bytes 626696 | tf_op jit(solution)/shard_map/ppermute | solution.py:34
  73.2 8.0 %collective-permute-start.17 = (bf16[816,128]{1,0:T(8,128)(2,1)S(1)}, bf16[816,128]{1,0:T(8,128)(2,1)S(1)}, u32[]{:S(2)}, u32[]{:S(2)}) collective-permute-start(bf16[816,128]{1,0:T(8,128)(2,1)S(1)} %get-tuple-element.34), channel_id=1, source_target_pairs={{32,0},{136,8},{48,16},{152,24},{0,32},{168,40},{16,48},{184,56},{... | collective-permute-start | bytes 626696 | tf_op jit(solution)/shard_map/ppermute | solution.py:34
  (1 other events, 0.9 us)
